TPU v7x, 32 devices: a whole 2x2x4 slice. The times are simulated.
32 devices in a mesh: stn: 16 (over z, y, core), chan: 2 (over x).
Axes of the slice: x: 2, y: 2, z: 4, core: 2. Of those that a mesh axis runs over, the one named last changes fastest.
Arguments:
- volts: bfloat16 [48, 2, 16, 32768], P('chan', None, None, 'stn'), may hold values from -6 to 6
- antenna_tile_weights: bfloat16 [48, 2, 32768], P('chan', None, 'stn'), may hold values from -1 to 1
- station_weights: bfloat16 [48, 2, 2048], P('chan', None, 'stn'), may hold values from -1 to 1
- tile_station: int32 [2048], P('stn'), may hold values from 0 to 127, as said below
- station_group: int32 [128], replicated, may hold values from 0 to 3
- station_pos: float32 [128, 2], replicated, may hold values from -3 to 3
- beam_dir: float32 [64, 2], replicated, may hold values from -1 to 1
- beam_order: int32 [64], replicated, may hold values from 0 to 63, each once
Outputs:
- tied_beams: bfloat16 [64, 48, 32], P(('stn', 'chan'))
Inputs may be any that keep to these rules, and one draw needn't show every extreme that they name: `tile_station`: the tiles of aligned block j of 128 tiles belong to stations j * 8 to j * 8 + 7, each of them exactly 16 tiles.
All inputs are finite; a program needn't handle non-finite values.
Results may differ from a plain program's by a relative error of at most 0.011.
Values may be sent and summed in bfloat16 or wider, within the bound.
No kernel may reach another device: no remote copies, remote signals or barrier semaphores. Data moves between devices by JAX's collectives and lax.ppermute only.
A program may use at most 128 MiB of HBM per device.

v0:
```python
import math

import jax
import jax.numpy as jnp
from jax import lax
from jax.sharding import PartitionSpec as P

TILE_ANTENNAS = 16
TPS = 16
GROUPS = 4


def tied_weights(directions, positions, groups, beam_ids, freq, scale):
    delay = directions[:, 0:1] * positions[None, :, 0] + directions[:, 1:2] * positions[None, :, 1]
    phase = (2.0 * math.pi * freq)[None, None, :] * delay[:, :, None]
    member = (groups[None, :] == beam_ids[:, None] % GROUPS).astype(jnp.float32)
    return (
        jnp.stack([jnp.cos(phase), jnp.sin(phase)], axis=-1) * (member * scale)[:, :, None, None]
    ).astype(jnp.bfloat16)


def shards(
    volts,
    antenna_tile_weights,
    station_weights,
    tile_station,
    station_group,
    station_pos,
    beam_dir,
    beam_order,
):
    channel_list, _, sample_values, antennas = volts.shape
    tile_list = station_weights.shape[2]
    stations = tile_list // TPS
    total_stations = stations * lax.axis_size("stn")
    total_chans = channel_list * lax.axis_size("chan")
    rows_stn = beam_order.shape[0] // lax.axis_size("stn")
    first_station = lax.axis_index("stn") * stations
    first_chan = lax.axis_index("chan") * channel_list
    volt_re = volts[:, 0].astype(jnp.float32)
    volt_im = volts[:, 1].astype(jnp.float32)
    weight_re = antenna_tile_weights[:, 0, None, :].astype(jnp.float32)
    weight_im = antenna_tile_weights[:, 1, None, :].astype(jnp.float32)
    product_real = weight_re * volt_re - weight_im * volt_im
    product_imaginary = weight_re * volt_im + weight_im * volt_re
    tile_beam_real = (
        product_real.reshape(channel_list, sample_values, tile_list, TILE_ANTENNAS)
        .sum(-1)
        .astype(jnp.bfloat16)
        .astype(jnp.float32)
    )
    tile_beam_imaginary = (
        product_imaginary.reshape(channel_list, sample_values, tile_list, TILE_ANTENNAS)
        .sum(-1)
        .astype(jnp.bfloat16)
        .astype(jnp.float32)
    )
    swt_re = station_weights[:, 0, None, :].astype(jnp.float32)
    swt_im = station_weights[:, 1, None, :].astype(jnp.float32)
    term_re = swt_re * tile_beam_real - swt_im * tile_beam_imaginary
    term_im = swt_re * tile_beam_imaginary + swt_im * tile_beam_real
    local_ids = tile_station - first_station
    member_table = (local_ids[:, None] == jnp.arange(stations)[None, :]).astype(jnp.float32)
    stn_re = jnp.einsum(
        "ctk,ks->sct", term_re, member_table, precision=lax.Precision.HIGHEST
    ).astype(jnp.bfloat16)
    stn_im = jnp.einsum(
        "ctk,ks->sct", term_im, member_table, precision=lax.Precision.HIGHEST
    ).astype(jnp.bfloat16)
    first_rows = jnp.concatenate([stn_re, stn_im], axis=2)
    second_rows = jnp.concatenate([stn_im, -stn_re], axis=2)
    stacked = jnp.stack([first_rows, second_rows], axis=2)
    freq = 1.0 + (first_chan + jnp.arange(channel_list)).astype(jnp.float32) / total_chans
    scale = 1.0 / math.sqrt(total_stations)
    own_ids = lax.dynamic_slice_in_dim(beam_order, lax.axis_index("stn") * rows_stn, rows_stn, 0)
    own_dirs = beam_dir[own_ids]
    weights = tied_weights(own_dirs, station_pos, station_group, own_ids, freq, scale)
    tied = jnp.einsum(
        "bscp,scpx->bcx",
        weights,
        lax.all_gather(stacked, "stn", axis=0, tiled=True),
        preferred_element_type=jnp.float32,
    )
    rounded = tied.astype(jnp.bfloat16)
    return lax.all_to_all(rounded, "chan", split_axis=0, concat_axis=1, tiled=True)


def solution(mesh):
    in_specs = (
        P("chan", None, None, "stn"),
        P("chan", None, "stn"),
        P("chan", None, "stn"),
        P("stn"),
        P(),
        P(),
        P(),
        P(),
    )
    out_specs = P(("stn", "chan"), None, None)
    return jax.shard_map(shards, mesh=mesh, in_specs=in_specs, out_specs=out_specs, check_vma=False)
```

profile of v0, /device:TPU:0, one launch (start us, length us, event | category | flops | bytes accessed | tf_op | source)
XLA Modules:
  0.0 103.0 jit_solution(11931107036758437747)
XLA Ops:
  0.0 4.5 %slice_convert_fusion.1 = (f32[24,1,16,2048]{3,2,1,0:T(8,128)}, f32[24,1,16,2048]{3,2,1,0:T(8,128)S(1)}) fusion(bf16[24,2,16,2048]{3,2,1,0:T(8,128)(2,1)} %param.8), kind=kLoop, calls=%fused_computation.4 | loop fusion | flops 1572864 | bytes 9437184 | tf_op jit(solution)/shard_map/convert_element_type | solution.py:40
  4.5 14.7 %reshape.151 = f32[24,16,128,16]{3,2,1,0:T(8,128)} reshape(f32[24,1,16,2048]{3,2,1,0:T(8,128)} %get-tuple-element.11) | data formatting | bytes 6291456 | tf_op jit(solution)/shard_map/convert_element_type | solution.py:40
  19.2 0.0 copy-start
  19.2 13.1 %reshape.153 = f32[24,16,128,16]{3,2,1,0:T(8,128)} reshape(f32[24,1,16,2048]{3,2,1,0:T(8,128)S(1)} %get-tuple-element.12) | data formatting | bytes 6291456 | tf_op jit(solution)/shard_map/convert_element_type | solution.py:41
  32.2 0.0 copy-done
  32.2 0.0 copy-start.1
  32.2 0.0 copy-start.6
  32.2 1.0 convert_reduce_fusion.1
  33.2 0.5 reshape.150
  33.8 0.5 reshape.152
  34.3 0.0 copy-done.1
  34.4 0.0 copy-done.6
  34.4 19.8 %subtract_reduce_fusion = (bf16[24,16,128]{2,1,0:T(8,128)(2,1)S(1)}, bf16[24,16,128]{2,1,0:T(8,128)(2,1)S(1)}) fusion(f32[24,16,128,16]{3,2,1,0:T(8,128)} %reshape.153, f32[24,16,128,16]{3,2,1,0:T(8,128)} %reshape.151, f32[24,128,16]{2,1,0:T(8,128)S(1)} %reshape.152, f32[24,128,16]{2,1,0:T(8,128)S(1)} %reshape.150), kind=kLoop, calls=%fused_computation.2 | loop fusion | flops 6193152 | bytes 6881280 | tf_op jit(solution)/shard_map/reduce_sum | solution.py:48
  54.2 0.1 fusion.3
  54.3 0.6 fusion.16
  54.9 0.6 convolution_convert_fusion
  55.5 0.0 copy-start.4
  55.5 0.0 copy-start.2
  55.6 0.0 copy-start.3
  55.6 0.0 copy-start.5
  55.6 32.2 %all_gather.3 = bf16[128,24,2,32]{1,0,3,2:T(8,128)(2,1)S(1)} all-gather(bf16[8,24,2,32]{1,0,3,2:T(8,128)(2,1)S(1)} %pad_maximum_fusion), channel_id=1, replica_groups=mesh['stn'=16,'chan'=2] {'stn'}, dimensions={0}, use_global_device_ids=true | all-gather | bytes 417792 | tf_op jit(solution)/shard_map/all_gather | solution.py:81
  87.8 4.6 %copy.19 = bf16[128,24,2,32]{3,0,2,1:T(8,128)(2,1)} copy(bf16[128,24,2,32]{1,0,3,2:T(8,128)(2,1)S(1)} %all_gather.3) | data formatting | bytes 786432 | tf_op jit(solution)/shard_map/all_gather | solution.py:81
  92.4 0.0 copy-done.4
  92.4 0.1 and_select_fusion
  92.5 0.0 copy-done.2
  92.5 0.1 copy.18
  92.6 0.6 gather_fusion
  93.2 0.2 slice_reduce_fusion.1
  93.4 0.0 copy-done.3
  93.4 0.1 multiply_add_fusion
  93.5 0.4 multiply_cosine_fusion
  93.9 0.0 copy-done.5
  93.9 0.1 compare_select_fusion.3
  94.0 1.7 %fusion.1 = bf16[4,24,32]{2,0,1:T(4,128)(2,1)S(1)} fusion(bf16[128,24,2,32]{3,0,2,1:T(8,128)(2,1)} %copy.19, f32[4,128,24,1]{1,0,3,2:T(4,128)S(1)} %get-tuple-element.20, f32[4,128,24,1]{1,0,3,2:T(4,128)S(1)} %get-tuple-element.19, f32[4,128]{1,0:T(4,128)S(1)} %compare_select_fusion.3), kind=kOutput, calls=%fused_computation.9 | convolution fusion | flops 1649664 | bytes 499712 | tf_op jit(solution)/shard_map/bscp,scpx->bcx/dot_general | solution.py:78
  95.7 0.1 reshape.170
  95.8 6.4 %all_to_all.18 = bf16[2,2,768]{2,1,0:T(2,128)(2,1)S(1)} all-to-all(bf16[2,2,768]{2,1,0:T(2,128)(2,1)S(1)} %reshape.170), channel_id=1, replica_groups=mesh['stn'=16,'chan'=2] {'chan'}, dimensions={0} | all-to-all | bytes 12288 | tf_op jit(solution)/shard_map/all_to_all | solution.py:85
  102.2 0.1 reshape.171
  102.3 0.7 copy.22
  (9 shorter events, 0.1 us)
Async XLA Ops:
  19.2 13.1 %copy-start = (bf16[24,2,2048]{2,1,0:T(2,128)(2,1)S(1)}, bf16[24,2,2048]{2,1,0:T(2,128)(2,1)}, u32[]{:S(2)}) copy-start(bf16[24,2,2048]{2,1,0:T(2,128)(2,1)} %param.9) | copy-start | bytes 589828
  32.2 2.1 %copy-start.1 = (bf16[24,2,128]{2,1,0:T(2,128)(2,1)S(1)}, bf16[24,2,128]{2,1,0:T(2,128)(2,1)}, u32[]{:S(2)}) copy-start(bf16[24,2,128]{2,1,0:T(2,128)(2,1)} %param.10) | copy-start | bytes 36868
  32.2 2.1 %copy-start.6 = (s32[128]{0:T(128)S(1)}, s32[128]{0:T(128)}, u32[]{:S(2)}) copy-start(s32[128]{0:T(128)} %param.11) | copy-start | bytes 1540
  55.5 36.9 %copy-start.4 = (s32[64]{0:T(128)S(1)}, s32[64]{0:T(128)}, u32[]{:S(2)}) copy-start(s32[64]{0:T(128)} %param.15) | copy-start | bytes 772
  55.5 37.0 %copy-start.2 = (f32[64,2]{0,1:T(2,128)S(1)}, f32[64,2]{0,1:T(2,128)}, u32[]{:S(2)}) copy-start(f32[64,2]{0,1:T(2,128)} %param.14) | copy-start | bytes 1540
  55.6 37.8 %copy-start.3 = (f32[128,2]{0,1:T(2,128)S(1)}, f32[128,2]{0,1:T(2,128)}, u32[]{:S(2)}) copy-start(f32[128,2]{0,1:T(2,128)} %param.13) | copy-start | bytes 3076
  55.6 38.3 %copy-start.5 = (s32[128]{0:T(128)S(1)}, s32[128]{0:T(128)}, u32[]{:S(2)}) copy-start(s32[128]{0:T(128)} %param.12) | copy-start | bytes 1540
where the time goes:
time: 103 us
  blocking collectives  38.6 us (37%)
  local copies, waits for them, and re-layouts  35.2 us (34%)
  other arithmetic  26.1 us (25%)
  matrix products  2.93 us (3%)
    all_gather x1, blocking collectives, shards(): lax.all_gather(stacked, 'stn', axis=0, tiled=True)  32.2 us
    reduce_sum x1, other arithmetic, shards(): tile_beam_real = product_real.reshape(channel_list, sample_values, tile_l...  19.8 us
    convert_element_type x1, local copies, waits for them, and re-layouts, shards(): volt_re = volts[:, 0].astype(jnp.float32)  14.7 us
    convert_element_type x1, local copies, waits for them, and re-layouts, shards(): volt_im = volts[:, 1].astype(jnp.float32)  13.1 us
    all_to_all x1, blocking collectives, shards(): lax.all_to_all(rounded, 'chan', split_axis=0, concat_axis=1, tiled=True)  6.38 us
    all_gather x1, local copies, waits for them, and re-layouts, shards(): lax.all_gather(stacked, 'stn', axis=0, tiled=True)  4.58 us
    convert_element_type x1, other arithmetic, shards(): volt_re = volts[:, 0].astype(jnp.float32)  4.48 us

commit v1 on v0

v1 whole, which is shorter than its diff:
```python
import functools
import math

import jax
import jax.numpy as jnp
from jax import lax
from jax.experimental import pallas as pl
from jax.experimental.pallas import tpu as pltpu
from jax.sharding import PartitionSpec as P

TILE_ANTENNAS = 16
TPS = 16
GROUPS = 4
CB = 8
CHUNK = 256
NT = (((1,), (1,)), ((), ()))
SIN = [(-1) ** i * (2 * math.pi) ** (2 * i + 1) / math.factorial(2 * i + 1) for i in range(7)]


def dot_nt(a, b):
    return lax.dot_general(a, b, NT, preferred_element_type=jnp.float32)


def iota(shape, dim):
    return lax.broadcasted_iota(jnp.int32, shape, dim)


def beam_columns(order_ref, dir_ref, start, rows):
    beams = order_ref.shape[1]
    order = order_ref[...].astype(jnp.float32)
    lane = iota((rows, beams), 1)
    own = lane == iota((rows, beams), 0) + start
    ids = jnp.sum(jnp.where(own, order, 0.0), axis=1, keepdims=True)
    pick = lane.astype(jnp.float32) == ids
    east = jnp.sum(jnp.where(pick, dir_ref[0:1, :], 0.0), axis=1, keepdims=True)
    north = jnp.sum(jnp.where(pick, dir_ref[1:2, :], 0.0), axis=1, keepdims=True)
    group = ids - GROUPS * jnp.floor(ids * (1.0 / GROUPS))
    return east, north, group


def station_rows(pos_ref, group_ref, stations, lanes):
    total = group_ref.shape[1]
    first = lax.axis_index("stn") * stations
    own = iota((stations, total), 1) == iota((stations, total), 0) + first
    spread = iota((stations, lanes), 0) == iota((stations, lanes), 1) % stations

    def turn(row):
        column = jnp.sum(jnp.where(own, row, 0.0), axis=1, keepdims=True)
        return jnp.sum(jnp.where(spread, column, 0.0), axis=0, keepdims=True)

    return turn(pos_ref[0:1, :]), turn(pos_ref[1:2, :]), turn(group_ref[...].astype(jnp.float32))


def cos_turns(t):
    y = t - jnp.floor(t + 0.5)
    z = 0.25 - jnp.abs(y)
    z2 = z * z
    value = jnp.full_like(z, SIN[-1])
    for coefficient in SIN[-2::-1]:
        value = value * z2 + coefficient
    return value * z


def kernel(
    volt_hbm, aw_ref, sw_ref, ts_ref, group_ref, pos_ref, dir_ref, order_ref, out_ref, volts, sems
):
    channels, _, samples, antennas = volt_hbm.shape
    tiles = sw_ref.shape[2]
    stations = tiles // TPS
    chunks = antennas // CHUNK
    per_chunk = CHUNK // TILE_ANTENNAS
    groups = channels // CB
    rows_c = 2 * samples
    beams = order_ref.shape[1]
    lanes = CB * 2 * stations
    scale = 1.0 / math.sqrt(group_ref.shape[1])

    copies = []
    for g in range(groups):
        part = pl.ds(g * CB, CB)
        copy = pltpu.make_async_copy(volt_hbm.at[part], volts.at[part], sems.at[g])
        copy.start()
        copies.append(copy)

    east_s, north_s, group_s = station_rows(pos_ref, group_ref, stations, lanes)
    lane = iota((1, lanes), 1)
    channel_lane = lane // (2 * stations)
    quarter = 0.25 * ((lane // stations) % 2).astype(jnp.float32)
    first_chan = lax.axis_index("chan") * channels
    total_chans = channels * lax.axis_size("chan")
    block = min(64, beams)

    mask16 = (iota((per_chunk, CHUNK), 1) // TILE_ANTENNAS == iota((per_chunk, CHUNK), 0)).astype(
        jnp.float32
    )
    member_table = (iota((stations, tiles), 0) == ts_ref[...] % stations).astype(jnp.float32)
    own_channel = iota((CB * rows_c, lanes), 0) // rows_c == iota((CB * rows_c, lanes), 1) // (
        2 * stations
    )
    lane_chunk = iota((rows_c, 2 * tiles), 1) // per_chunk % chunks

    for g in range(groups):
        channel0 = g * CB
        weights = aw_ref[channel0 : channel0 + CB].astype(jnp.float32)
        copies[g].wait()
        found = [None] * CB
        for step in range(chunks):
            left = jnp.concatenate(
                [
                    volts[
                        channel0 + c,
                        :,
                        :,
                        (c + step) % chunks * CHUNK : ((c + step) % chunks + 1) * CHUNK,
                    ].reshape(rows_c, CHUNK)
                    for c in range(CB)
                ],
                axis=0,
            )
            right = jnp.concatenate(
                [
                    (
                        weights[(q - step) % CB, part : part + 1, q * CHUNK : (q + 1) * CHUNK]
                        * mask16
                    ).astype(jnp.bfloat16)
                    for part in range(2)
                    for q in range(chunks)
                ],
                axis=0,
            )
            product = dot_nt(left, right)
            for c in range(CB):
                mine = product[c * rows_c : (c + 1) * rows_c]
                if step == 0:
                    found[c] = mine
                else:
                    found[c] = jnp.where(lane_chunk == (c + step) % chunks, mine, found[c])
        left = []
        for c in range(CB):
            real, imag = found[c][:samples], found[c][samples:]
            tile_re = (real[:, :tiles] - imag[:, tiles:]).astype(jnp.bfloat16)
            tile_im = (imag[:, :tiles] + real[:, tiles:]).astype(jnp.bfloat16)
            left.append(jnp.concatenate([tile_re, tile_im], axis=1))
            left.append(jnp.concatenate([tile_im, -tile_re], axis=1))
        right = []
        swt = sw_ref[channel0 : channel0 + CB].astype(jnp.float32)
        for c in range(CB):
            re = swt[c, 0:1] * member_table
            im = swt[c, 1:2] * member_table
            right.append(jnp.concatenate([re, -im], axis=1))
            right.append(jnp.concatenate([im, re], axis=1))
        station = dot_nt(
            jnp.concatenate(left, axis=0), jnp.concatenate(right, axis=0).astype(jnp.bfloat16)
        )
        station = jnp.where(own_channel, station, 0.0).astype(jnp.bfloat16)

        freq = 1.0 + (first_chan + channel0 + channel_lane).astype(jnp.float32) / total_chans

        def tied_rows(start):
            east, north, group = beam_columns(order_ref, dir_ref, start, block)
            delay = east * east_s + north * north_s
            wave = cos_turns(delay * freq - quarter)
            tied_weight = wave * jnp.where(group == group_s, scale, 0.0)
            return dot_nt(tied_weight.astype(jnp.bfloat16), station).astype(jnp.bfloat16)

        columns = slice(channel0 * rows_c, (channel0 + CB) * rows_c)
        if beams == block:
            out_ref[:, columns] = tied_rows(0)
        else:

            def body(i, carry):
                start = pl.multiple_of(i * block, block)
                out_ref[pl.ds(start, block), columns] = tied_rows(start)
                return carry

            lax.fori_loop(0, beams // block, body, 0)


def shards(
    volts,
    antenna_tile_weights,
    station_weights,
    tile_station,
    station_group,
    station_pos,
    beam_dir,
    beam_order,
):
    channels, _, samples, _ = volts.shape
    beams = beam_order.shape[0]
    n_stn, n_chan = lax.axis_size("stn"), lax.axis_size("chan")
    rows = beams // (n_stn * n_chan)
    width = channels * 2 * samples
    vmem = pl.BlockSpec(memory_space=pltpu.VMEM)
    partial = pl.pallas_call(
        kernel,
        out_shape=jax.ShapeDtypeStruct((beams, width), jnp.bfloat16),
        in_specs=[pl.BlockSpec(memory_space=pl.ANY)] + [vmem] * 7,
        out_specs=vmem,
        scratch_shapes=[
            pltpu.VMEM(volts.shape, volts.dtype),
            pltpu.SemaphoreType.DMA((channels // CB,)),
        ],
        compiler_params=pltpu.CompilerParams(vmem_limit_bytes=32 * 2**20),
        name="partial_tied",
    )(
        volts,
        antenna_tile_weights,
        station_weights,
        tile_station[None, :],
        station_group[None, :],
        station_pos.T,
        beam_dir.T,
        beam_order[None, :],
    )
    partial = partial.reshape(n_stn * n_chan, rows, width)
    parts = lax.all_to_all(partial, ("stn", "chan"), split_axis=0, concat_axis=0, tiled=True)
    parts = parts.reshape(n_stn, n_chan, rows, channels, 2 * samples)
    tied = jnp.sum(parts.astype(jnp.float32), axis=0).astype(jnp.bfloat16)
    return tied.transpose(1, 0, 2, 3).reshape(rows, n_chan * channels, 2 * samples)


def solution(mesh):
    in_specs = (
        P("chan", None, None, "stn"),
        P("chan", None, "stn"),
        P("chan", None, "stn"),
        P("stn"),
        P(),
        P(),
        P(),
        P(),
    )
    out_specs = P(("stn", "chan"), None, None)
    return jax.shard_map(shards, mesh=mesh, in_specs=in_specs, out_specs=out_specs, check_vma=False)
```

time: 103 us -> 26 us (0.25)
  local copies, waits for them, and re-layouts: 35.2 us -> 7.78 us
  other arithmetic: 26.1 us -> 0.09 us
  blocking collectives: 38.6 us -> 15.2 us
  matrix products: 2.93 us -> 0 us
  Pallas kernels: 0 us -> 2.57 us
    all_gather x1 -> x0, blocking collectives: 32.2 us -> none  [shards(): lax.all_gather(stacked, 'stn', axis=0, tiled=True)]
    convert_element_type x3 -> x0, local copies, waits for them, and re-layouts: 27.7 us -> none  [the longest x1 14.7 us: shards(): volt_re = volts[:, 0].astype(jnp.float32)]
    reduce_sum x1, other arithmetic: 19.8 us -> 0.09 us  [shards(): tied = jnp.sum(parts.astype(jnp.float32), axis=0).astype(jnp.bfloat16)]
    all_to_all x1, blocking collectives: 6.38 us -> 15.2 us  [shards(): lax.all_to_all(partial, ('stn', 'chan'), split_axis=0, concat_axis=0, til...]
    unnamed x17 -> x16, local copies, waits for them, and re-layouts: 0.31 us -> 6.84 us
    all_gather x1 -> x0, local copies, waits for them, and re-layouts: 4.58 us -> none  [shards(): lax.all_gather(stacked, 'stn', axis=0, tiled=True)]
    convert_element_type x1 -> x0, other arithmetic: 4.48 us -> none  [shards(): volt_re = volts[:, 0].astype(jnp.float32)]
    dot_general x3 -> x0, matrix products: 2.93 us -> none  [the longest x1 1.72 us: shards(): jnp.einsum('bscp,scpx->bcx', weights, lax.all_gather(stacked, 'stn', axis...]
where the time goes in v1:
time: 26 us; the launch traced here: 25.7 us
  blocking collectives  15.2 us (58%)
  local copies, waits for them, and re-layouts  7.78 us (30%)
  Pallas kernels  2.57 us (10%)
    all_to_all x1, blocking collectives, shards(): lax.all_to_all(partial, ('stn', 'chan'), split_axis=0, concat_axis=0, til...  15.2 us
    unnamed x16, local copies, waits for them, and re-layouts  6.84 us
    pallas_call x1, Pallas kernels, shards(): pl.pallas_call(kernel, out_shape=jax.ShapeDtypeStruct((beams, width), jnp...  2.57 us
    reshape x1, local copies, waits for them, and re-layouts, shards(): tied.transpose(1, 0, 2, 3).reshape(rows, n_chan * channels, 2 * samples)  0.69 us

profile of v1, /device:TPU:0, one launch (start us, length us, event | category | flops | bytes accessed | tf_op | source)
XLA Modules:
  0.0 25.7 jit_solution(15053853998990960714)
XLA Ops:
  0.0 0.0 copy-start
  0.0 1.9 %copy-done = bf16[24,2,16,2048]{3,2,1,0:T(8,128)(2,1)S(1)} copy-done((bf16[24,2,16,2048]{3,2,1,0:T(8,128)(2,1)S(1)}, bf16[24,2,16,2048]{3,2,1,0:T(8,128)(2,1)}, u32[]{:S(2)}) %copy-start) | copy-done | bytes 3145752
  1.9 0.0 copy-start.1
  1.9 0.9 %copy-done.1 = bf16[24,2,2048]{2,1,0:T(2,128)(2,1)S(1)} copy-done((bf16[24,2,2048]{2,1,0:T(2,128)(2,1)S(1)}, bf16[24,2,2048]{2,1,0:T(2,128)(2,1)}, u32[]{:S(2)}) %copy-start.1) | copy-done | bytes 196632
  2.8 0.0 copy-start.2
  2.8 0.7 %copy-done.2 = bf16[24,2,128]{2,1,0:T(2,128)(2,1)S(1)} copy-done((bf16[24,2,128]{2,1,0:T(2,128)(2,1)S(1)}, bf16[24,2,128]{2,1,0:T(2,128)(2,1)}, u32[]{:S(2)}) %copy-start.2) | copy-done | bytes 12312
  3.5 0.0 copy-start.3
  3.5 0.7 %copy-done.3 = f32[128,2]{0,1:T(2,128)S(1)} copy-done((f32[128,2]{0,1:T(2,128)S(1)}, f32[128,2]{0,1:T(2,128)}, u32[]{:S(2)}) %copy-start.3) | copy-done | bytes 1048
  4.2 0.0 copy-start.4
  4.2 0.7 %copy-done.4 = f32[64,2]{0,1:T(2,128)S(1)} copy-done((f32[64,2]{0,1:T(2,128)S(1)}, f32[64,2]{0,1:T(2,128)}, u32[]{:S(2)}) %copy-start.4) | copy-done | bytes 536
  4.9 0.0 copy-start.5
  4.9 0.7 %copy-done.5 = s32[128]{0:T(128)S(1)} copy-done((s32[128]{0:T(128)S(1)}, s32[128]{0:T(128)}, u32[]{:S(2)}) %copy-start.5) | copy-done | bytes 536
  5.5 0.0 copy-start.6
  5.5 0.7 %copy-done.6 = s32[128]{0:T(128)S(1)} copy-done((s32[128]{0:T(128)S(1)}, s32[128]{0:T(128)}, u32[]{:S(2)}) %copy-start.6) | copy-done | bytes 536
  6.2 0.0 copy-start.7
  6.2 0.7 %copy-done.7 = s32[64]{0:T(128)S(1)} copy-done((s32[64]{0:T(128)S(1)}, s32[64]{0:T(128)}, u32[]{:S(2)}) %copy-start.7) | copy-done | bytes 280
  6.9 2.6 %partial_tied.1 = bf16[64,768]{1,0:T(8,128)(2,1)S(1)} custom-call(bf16[24,2,16,2048]{3,2,1,0:T(8,128)(2,1)S(1)} %copy-done, bf16[24,2,2048]{2,1,0:T(2,128)(2,1)S(1)} %copy-done.1, bf16[24,2,128]{2,1,0:T(2,128)(2,1)S(1)} %copy-done.2, s32[1,128]{1,0:T(1,128)S(1)} %bitcast.9, s32[1,128]{1,0:T(1,128)S(1)} %bitcast.10, f32[2,128]{1,0:T(2,128)S(1)} %bitcast.7, ...), custom_call_target="tpu_custom_call" | custom-call | tf_op jit(solution)/shard_map/partial_tied/pallas_call | solution.py:195
  9.5 15.2 %all_to_all.5 = bf16[32,2,768]{2,1,0:T(2,128)(2,1)S(1)} all-to-all(bf16[32,2,768]{2,1,0:T(2,128)(2,1)S(1)} %reshape.9), channel_id=1, replica_groups=mesh['stn'=16,'chan'=2] {'stn','chan'}, dimensions={0} | all-to-all | bytes 196608 | tf_op jit(solution)/shard_map/all_to_all | solution.py:217
  24.7 0.2 reshape.10
  24.9 0.1 reduce_sum.12
  25.0 0.7 %copy.11 = bf16[2,48,32]{1,2,0:T(8,128)(2,1)} copy(bf16[2,48,32]{2,1,0:T(8,128)(2,1)S(1)} %bitcast.13) | data formatting | bytes 12288 | tf_op jit(solution)/shard_map/reshape | solution.py:220
  (2 shorter events, 0.0 us)
Async XLA Ops:
  0.0 1.9 %copy-start = (bf16[24,2,16,2048]{3,2,1,0:T(8,128)(2,1)S(1)}, bf16[24,2,16,2048]{3,2,1,0:T(8,128)(2,1)}, u32[]{:S(2)}) copy-start(bf16[24,2,16,2048]{3,2,1,0:T(8,128)(2,1)} %volt_hbm.1) | copy-start | bytes 9437188
  1.9 0.9 %copy-start.1 = (bf16[24,2,2048]{2,1,0:T(2,128)(2,1)S(1)}, bf16[24,2,2048]{2,1,0:T(2,128)(2,1)}, u32[]{:S(2)}) copy-start(bf16[24,2,2048]{2,1,0:T(2,128)(2,1)} %aw_ref.1) | copy-start | bytes 589828
  2.8 0.7 %copy-start.2 = (bf16[24,2,128]{2,1,0:T(2,128)(2,1)S(1)}, bf16[24,2,128]{2,1,0:T(2,128)(2,1)}, u32[]{:S(2)}) copy-start(bf16[24,2,128]{2,1,0:T(2,128)(2,1)} %sw_ref.1) | copy-start | bytes 36868
  3.5 0.7 %copy-start.3 = (f32[128,2]{0,1:T(2,128)S(1)}, f32[128,2]{0,1:T(2,128)}, u32[]{:S(2)}) copy-start(f32[128,2]{0,1:T(2,128)} %param.13) | copy-start | bytes 3076
  4.2 0.7 %copy-start.4 = (f32[64,2]{0,1:T(2,128)S(1)}, f32[64,2]{0,1:T(2,128)}, u32[]{:S(2)}) copy-start(f32[64,2]{0,1:T(2,128)} %param.14) | copy-start | bytes 1540
  4.9 0.7 %copy-start.5 = (s32[128]{0:T(128)S(1)}, s32[128]{0:T(128)}, u32[]{:S(2)}) copy-start(s32[128]{0:T(128)} %param.11) | copy-start | bytes 1540
  5.5 0.7 %copy-start.6 = (s32[128]{0:T(128)S(1)}, s32[128]{0:T(128)}, u32[]{:S(2)}) copy-start(s32[128]{0:T(128)} %param.12) | copy-start | bytes 1540
  6.2 0.7 %copy-start.7 = (s32[64]{0:T(128)S(1)}, s32[64]{0:T(128)}, u32[]{:S(2)}) copy-start(s32[64]{0:T(128)} %param.15) | copy-start | bytes 772

commit v2 on v1

--- a/solution.py
+++ b/solution.py
@@ -62,7 +62,25 @@
 
 
 def kernel(
-    volt_hbm, aw_ref, sw_ref, ts_ref, group_ref, pos_ref, dir_ref, order_ref, out_ref, volts, sems
+    volt_hbm,
+    aw_hbm,
+    sw_hbm,
+    ts_hbm,
+    group_hbm,
+    pos_hbm,
+    dir_hbm,
+    order_hbm,
+    out_ref,
+    volts,
+    aw_ref,
+    sw_ref,
+    ts_ref,
+    group_ref,
+    pos_ref,
+    dir_ref,
+    order_ref,
+    tied_ref,
+    sems,
 ):
     channels, _, samples, antennas = volt_hbm.shape
     tiles = sw_ref.shape[2]
@@ -75,12 +93,31 @@
     lanes = CB * 2 * stations
     scale = 1.0 / math.sqrt(group_ref.shape[1])
 
-    copies = []
-    for g in range(groups):
-        part = pl.ds(g * CB, CB)
-        copy = pltpu.make_async_copy(volt_hbm.at[part], volts.at[part], sems.at[g])
+    def start(source, target, k):
+        copy = pltpu.make_async_copy(source, target, sems.at[k])
         copy.start()
-        copies.append(copy)
+        return copy
+
+    small = [
+        start(source, target, k)
+        for k, (source, target) in enumerate(
+            [
+                (order_hbm, order_ref),
+                (dir_hbm, dir_ref),
+                (pos_hbm, pos_ref),
+                (group_hbm, group_ref),
+                (ts_hbm, ts_ref),
+                (sw_hbm, sw_ref),
+                (aw_hbm, aw_ref),
+            ]
+        )
+    ]
+    large = []
+    for k in range(2 * groups):
+        part = pl.ds(k * CB // 2, CB // 2)
+        large.append(start(volt_hbm.at[part], volts.at[part], len(small) + k))
+    for copy in small[:4]:
+        copy.wait()
 
     east_s, north_s, group_s = station_rows(pos_ref, group_ref, stations, lanes)
     lane = iota((1, lanes), 1)
@@ -90,6 +127,29 @@
     total_chans = channels * lax.axis_size("chan")
     block = min(64, beams)
 
+    def tied_rows(first):
+        east, north, group = beam_columns(order_ref, dir_ref, first, block)
+        delay = east * east_s + north * north_s
+        member = jnp.where(group == group_s, scale, 0.0)
+        for g in range(groups):
+            freq = 1.0 + (first_chan + g * CB + channel_lane).astype(jnp.float32) / total_chans
+            wave = cos_turns(delay * freq - quarter)
+            tied_ref[pl.ds(first, block), g * lanes : (g + 1) * lanes] = (wave * member).astype(
+                jnp.bfloat16
+            )
+
+    if beams == block:
+        tied_rows(0)
+    else:
+
+        def body(i, carry):
+            tied_rows(pl.multiple_of(i * block, block))
+            return carry
+
+        lax.fori_loop(0, beams // block, body, 0)
+
+    for copy in small[4:]:
+        copy.wait()
     mask16 = (iota((per_chunk, CHUNK), 1) // TILE_ANTENNAS == iota((per_chunk, CHUNK), 0)).astype(
         jnp.float32
     )
@@ -102,7 +162,8 @@
     for g in range(groups):
         channel0 = g * CB
         weights = aw_ref[channel0 : channel0 + CB].astype(jnp.float32)
-        copies[g].wait()
+        large[2 * g].wait()
+        large[2 * g + 1].wait()
         found = [None] * CB
         for step in range(chunks):
             left = jnp.concatenate(
@@ -153,27 +214,11 @@
             jnp.concatenate(left, axis=0), jnp.concatenate(right, axis=0).astype(jnp.bfloat16)
         )
         station = jnp.where(own_channel, station, 0.0).astype(jnp.bfloat16)
-
-        freq = 1.0 + (first_chan + channel0 + channel_lane).astype(jnp.float32) / total_chans
-
-        def tied_rows(start):
-            east, north, group = beam_columns(order_ref, dir_ref, start, block)
-            delay = east * east_s + north * north_s
-            wave = cos_turns(delay * freq - quarter)
-            tied_weight = wave * jnp.where(group == group_s, scale, 0.0)
-            return dot_nt(tied_weight.astype(jnp.bfloat16), station).astype(jnp.bfloat16)
-
-        columns = slice(channel0 * rows_c, (channel0 + CB) * rows_c)
-        if beams == block:
-            out_ref[:, columns] = tied_rows(0)
-        else:
-
-            def body(i, carry):
-                start = pl.multiple_of(i * block, block)
-                out_ref[pl.ds(start, block), columns] = tied_rows(start)
-                return carry
-
-            lax.fori_loop(0, beams // block, body, 0)
+        tied = dot_nt(tied_ref[:, g * lanes : (g + 1) * lanes], station)
+        devices, rows, _ = out_ref.shape
+        out_ref[:, :, channel0 * rows_c : (channel0 + CB) * rows_c] = tied.astype(
+            jnp.bfloat16
+        ).reshape(devices, rows, CB * rows_c)
 
 
 def shards(
@@ -191,19 +236,7 @@
     n_stn, n_chan = lax.axis_size("stn"), lax.axis_size("chan")
     rows = beams // (n_stn * n_chan)
     width = channels * 2 * samples
-    vmem = pl.BlockSpec(memory_space=pltpu.VMEM)
-    partial = pl.pallas_call(
-        kernel,
-        out_shape=jax.ShapeDtypeStruct((beams, width), jnp.bfloat16),
-        in_specs=[pl.BlockSpec(memory_space=pl.ANY)] + [vmem] * 7,
-        out_specs=vmem,
-        scratch_shapes=[
-            pltpu.VMEM(volts.shape, volts.dtype),
-            pltpu.SemaphoreType.DMA((channels // CB,)),
-        ],
-        compiler_params=pltpu.CompilerParams(vmem_limit_bytes=32 * 2**20),
-        name="partial_tied",
-    )(
+    operands = (
         volts,
         antenna_tile_weights,
         station_weights,
@@ -213,7 +246,20 @@
         beam_dir.T,
         beam_order[None, :],
     )
-    partial = partial.reshape(n_stn * n_chan, rows, width)
+    groups = channels // CB
+    partial = pl.pallas_call(
+        kernel,
+        out_shape=jax.ShapeDtypeStruct((n_stn * n_chan, rows, width), jnp.bfloat16),
+        in_specs=[pl.BlockSpec(memory_space=pltpu.HBM)] * len(operands),
+        out_specs=pl.BlockSpec(memory_space=pltpu.VMEM),
+        scratch_shapes=[pltpu.VMEM(x.shape, x.dtype) for x in operands]
+        + [
+            pltpu.VMEM((beams, channels * 2 * (station_weights.shape[2] // TPS)), jnp.bfloat16),
+            pltpu.SemaphoreType.DMA((len(operands) - 1 + 2 * groups,)),
+        ],
+        compiler_params=pltpu.CompilerParams(vmem_limit_bytes=60 * 2**20),
+        name="partial_tied",
+    )(*operands)
     parts = lax.all_to_all(partial, ("stn", "chan"), split_axis=0, concat_axis=0, tiled=True)
     parts = parts.reshape(n_stn, n_chan, rows, channels, 2 * samples)
     tied = jnp.sum(parts.astype(jnp.float32), axis=0).astype(jnp.bfloat16)

time: 26 us -> 21 us (0.81)
  local copies, waits for them, and re-layouts: 7.78 us -> 0.89 us
  Pallas kernels: 2.57 us -> 4.38 us
    unnamed x16 -> x0, local copies, waits for them, and re-layouts: 6.84 us -> none
    pallas_call x1, Pallas kernels: 2.57 us -> 4.38 us  [shards(): pl.pallas_call(kernel, out_shape=jax.ShapeDtypeStruct((n_stn * n_chan, ro...]
where the time goes in v2:
time: 21 us; the launch traced here: 20.8 us
  blocking collectives  15.4 us (73%)
  Pallas kernels  4.38 us (21%)
  local copies, waits for them, and re-layouts  0.89 us (4%)
    all_to_all x1, blocking collectives, shards(): lax.all_to_all(partial, ('stn', 'chan'), split_axis=0, concat_axis=0, til...  15.4 us
    pallas_call x1, Pallas kernels, shards(): pl.pallas_call(kernel, out_shape=jax.ShapeDtypeStruct((n_stn * n_chan, ro...  4.38 us
    reshape x1, local copies, waits for them, and re-layouts, shards(): tied.transpose(1, 0, 2, 3).reshape(rows, n_chan * channels, 2 * samples)  0.69 us

profile of v2, /device:TPU:0, one launch (start us, length us, event | category | flops | bytes accessed | tf_op | source)
XLA Modules:
  0.0 20.8 jit_solution(14886768780270237056)
XLA Ops:
  0.0 4.4 %partial_tied.1 = bf16[32,2,768]{2,1,0:T(2,128)(2,1)} custom-call(bf16[24,2,16,2048]{3,2,1,0:T(8,128)(2,1)} %volt_hbm.1, bf16[24,2,2048]{2,1,0:T(2,128)(2,1)} %aw_hbm.1, bf16[24,2,128]{2,1,0:T(2,128)(2,1)} %sw_hbm.1, s32[1,128]{1,0:T(1,128)} %bitcast.11, s32[1,128]{1,0:T(1,128)} %bitcast.12, f32[2,128]{1,0:T(2,128)} %bitcast.9, f32[2,64]{1,0:T(2,128)} %bitcast.10, ...), custom_call_target="tpu_custom_call" | custom-call | tf_op jit(solution)/shard_map/partial_tied/pallas_call | solution.py:250
  4.4 15.4 %all_to_all.5 = bf16[32,2,768]{2,1,0:T(2,128)(2,1)S(1)} all-to-all(bf16[32,2,768]{2,1,0:T(2,128)(2,1)} %partial_tied.1), channel_id=1, replica_groups=mesh['stn'=16,'chan'=2] {'stn','chan'}, dimensions={0} | all-to-all | bytes 196608 | tf_op jit(solution)/shard_map/all_to_all | solution.py:263
  19.8 0.2 reshape.6
  20.0 0.1 reduce_sum.12
  20.1 0.7 %copy.11 = bf16[2,48,32]{1,2,0:T(8,128)(2,1)} copy(bf16[2,48,32]{2,1,0:T(8,128)(2,1)S(1)} %bitcast.8) | data formatting | bytes 12288 | tf_op jit(solution)/shard_map/reshape | solution.py:266
  (1 shorter events, 0.0 us)

commit v3 on v2

--- a/solution.py
+++ b/solution.py
@@ -23,32 +23,6 @@
 
 def iota(shape, dim):
     return lax.broadcasted_iota(jnp.int32, shape, dim)
-
-
-def beam_columns(order_ref, dir_ref, start, rows):
-    beams = order_ref.shape[1]
-    order = order_ref[...].astype(jnp.float32)
-    lane = iota((rows, beams), 1)
-    own = lane == iota((rows, beams), 0) + start
-    ids = jnp.sum(jnp.where(own, order, 0.0), axis=1, keepdims=True)
-    pick = lane.astype(jnp.float32) == ids
-    east = jnp.sum(jnp.where(pick, dir_ref[0:1, :], 0.0), axis=1, keepdims=True)
-    north = jnp.sum(jnp.where(pick, dir_ref[1:2, :], 0.0), axis=1, keepdims=True)
-    group = ids - GROUPS * jnp.floor(ids * (1.0 / GROUPS))
-    return east, north, group
-
-
-def station_rows(pos_ref, group_ref, stations, lanes):
-    total = group_ref.shape[1]
-    first = lax.axis_index("stn") * stations
-    own = iota((stations, total), 1) == iota((stations, total), 0) + first
-    spread = iota((stations, lanes), 0) == iota((stations, lanes), 1) % stations
-
-    def turn(row):
-        column = jnp.sum(jnp.where(own, row, 0.0), axis=1, keepdims=True)
-        return jnp.sum(jnp.where(spread, column, 0.0), axis=0, keepdims=True)
-
-    return turn(pos_ref[0:1, :]), turn(pos_ref[1:2, :]), turn(group_ref[...].astype(jnp.float32))
 
 
 def cos_turns(t):
@@ -71,6 +45,7 @@
     dir_hbm,
     order_hbm,
     out_ref,
+    tied_ref,
     volts,
     aw_ref,
     sw_ref,
@@ -79,7 +54,6 @@
     pos_ref,
     dir_ref,
     order_ref,
-    tied_ref,
     sems,
 ):
     channels, _, samples, antennas = volt_hbm.shape
@@ -90,7 +64,8 @@
     groups = channels // CB
     rows_c = 2 * samples
     beams = order_ref.shape[1]
-    lanes = CB * 2 * stations
+    n_chan = lax.axis_size("chan")
+    total_chans = channels * n_chan
     scale = 1.0 / math.sqrt(group_ref.shape[1])
 
     def start(source, target, k):
@@ -119,34 +94,27 @@
     for copy in small[:4]:
         copy.wait()
 
-    east_s, north_s, group_s = station_rows(pos_ref, group_ref, stations, lanes)
-    lane = iota((1, lanes), 1)
-    channel_lane = lane // (2 * stations)
-    quarter = 0.25 * ((lane // stations) % 2).astype(jnp.float32)
-    first_chan = lax.axis_index("chan") * channels
-    total_chans = channels * lax.axis_size("chan")
-    block = min(64, beams)
-
-    def tied_rows(first):
-        east, north, group = beam_columns(order_ref, dir_ref, first, block)
-        delay = east * east_s + north * north_s
-        member = jnp.where(group == group_s, scale, 0.0)
-        for g in range(groups):
-            freq = 1.0 + (first_chan + g * CB + channel_lane).astype(jnp.float32) / total_chans
-            wave = cos_turns(delay * freq - quarter)
-            tied_ref[pl.ds(first, block), g * lanes : (g + 1) * lanes] = (wave * member).astype(
-                jnp.bfloat16
-            )
-
-    if beams == block:
-        tied_rows(0)
-    else:
-
-        def body(i, carry):
-            tied_rows(pl.multiple_of(i * block, block))
-            return carry
-
-        lax.fori_loop(0, beams // block, body, 0)
+    own_beams = tied_ref.shape[0] // (2 * total_chans)
+    order = order_ref[...].astype(jnp.float32)
+    first_beam = (lax.axis_index("stn") * n_chan + lax.axis_index("chan")) * own_beams
+    lane_beam = iota((1, beams), 1)
+    freq_of = iota((CB, 1), 0)
+    waves = [[] for _ in range(total_chans // CB)]
+    for b in range(own_beams):
+        own_id = jnp.sum(jnp.where(lane_beam == first_beam + b, order, 0.0), axis=1, keepdims=True)
+        pick = lane_beam.astype(jnp.float32) == own_id
+        east = jnp.sum(jnp.where(pick, dir_ref[0:1, :], 0.0), axis=1, keepdims=True)
+        north = jnp.sum(jnp.where(pick, dir_ref[1:2, :], 0.0), axis=1, keepdims=True)
+        own_group = own_id - GROUPS * jnp.floor(own_id * (1.0 / GROUPS))
+        delay = east * pos_ref[0:1, :] + north * pos_ref[1:2, :]
+        member = jnp.where(group_ref[...].astype(jnp.float32) == own_group, scale, 0.0)
+        for g, wave in enumerate(waves):
+            turns = (1.0 + (freq_of + g * CB).astype(jnp.float32) / total_chans) * delay
+            wave.append((cos_turns(turns) * member, cos_turns(turns - 0.25) * member))
+    for g, wave in enumerate(waves):
+        rows = [wave[b][part] for part in range(2) for b in range(own_beams)]
+        size = len(rows) * CB
+        tied_ref[g * size : (g + 1) * size, :] = jnp.concatenate(rows, axis=0).astype(jnp.bfloat16)
 
     for copy in small[4:]:
         copy.wait()
@@ -154,9 +122,9 @@
         jnp.float32
     )
     member_table = (iota((stations, tiles), 0) == ts_ref[...] % stations).astype(jnp.float32)
-    own_channel = iota((CB * rows_c, lanes), 0) // rows_c == iota((CB * rows_c, lanes), 1) // (
-        2 * stations
-    )
+    own_channel = iota((CB * stations, CB * rows_c), 0) // stations == iota(
+        (CB * stations, CB * rows_c), 1
+    ) // rows_c
     lane_chunk = iota((rows_c, 2 * tiles), 1) // per_chunk % chunks
 
     for g in range(groups):
@@ -209,16 +177,46 @@
             re = swt[c, 0:1] * member_table
             im = swt[c, 1:2] * member_table
             right.append(jnp.concatenate([re, -im], axis=1))
-            right.append(jnp.concatenate([im, re], axis=1))
         station = dot_nt(
-            jnp.concatenate(left, axis=0), jnp.concatenate(right, axis=0).astype(jnp.bfloat16)
-        )
-        station = jnp.where(own_channel, station, 0.0).astype(jnp.bfloat16)
-        tied = dot_nt(tied_ref[:, g * lanes : (g + 1) * lanes], station)
-        devices, rows, _ = out_ref.shape
-        out_ref[:, :, channel0 * rows_c : (channel0 + CB) * rows_c] = tied.astype(
+            jnp.concatenate(right, axis=0).astype(jnp.bfloat16), jnp.concatenate(left, axis=0)
+        )
+        station = jnp.where(own_channel, station, 0.0).reshape(CB, stations, CB * rows_c)
+        out_ref[:, channel0 * rows_c : (channel0 + CB) * rows_c] = jnp.sum(station, axis=0).astype(
             jnp.bfloat16
-        ).reshape(devices, rows, CB * rows_c)
+        )
+
+
+def tied_kernel(gathered_ref, tied_ref, out_ref):
+    n_stn, n_chan = lax.axis_size("stn"), lax.axis_size("chan")
+    own_beams, rows_c, total_chans = out_ref.shape
+    samples = rows_c // 2
+    stations = gathered_ref.shape[0] // (n_stn * n_chan)
+    per_chan = total_chans // n_chan // CB
+    width = CB * rows_c
+    gathered = gathered_ref[...].reshape(n_stn, n_chan, stations, per_chan * width)
+    diagonal = iota((CB, width), 0) == iota((CB, width), 1) // rows_c
+    real_lane = iota((CB, width), 1) % rows_c < samples
+    beams = [[] for _ in range(own_beams)]
+    size = 2 * own_beams * CB
+    for g in range(total_chans // CB):
+        chan, column = g // per_chan, g % per_chan * width
+        station = gathered[:, chan, :, column : column + width].reshape(n_stn * stations, width)
+        sums = jnp.dot(
+            tied_ref[g * size : (g + 1) * size, :], station, preferred_element_type=jnp.float32
+        )
+        for b in range(own_beams):
+            by_cos = sums[b * CB : (b + 1) * CB]
+            by_sin = sums[(own_beams + b) * CB : (own_beams + b + 1) * CB]
+            turned = jnp.where(
+                real_lane,
+                pltpu.roll(by_sin, width - samples, 1),
+                -pltpu.roll(by_sin, samples, 1),
+            )
+            beams[b].append(jnp.where(diagonal, by_cos + turned, 0.0))
+    spread = (iota((rows_c, width), 0) == iota((rows_c, width), 1) % rows_c).astype(jnp.bfloat16)
+    for b in range(own_beams):
+        rows = jnp.concatenate(beams[b], axis=0).astype(jnp.bfloat16)
+        out_ref[b] = dot_nt(spread, rows).astype(jnp.bfloat16)
 
 
 def shards(
@@ -247,23 +245,31 @@
         beam_order[None, :],
     )
     groups = channels // CB
-    partial = pl.pallas_call(
+    vmem = pl.BlockSpec(memory_space=pltpu.VMEM)
+    tied_shape = (2 * rows * n_chan * channels, station_group.shape[0])
+    stations, tied_weight = pl.pallas_call(
         kernel,
-        out_shape=jax.ShapeDtypeStruct((n_stn * n_chan, rows, width), jnp.bfloat16),
+        out_shape=(
+            jax.ShapeDtypeStruct((station_weights.shape[2] // TPS, width), jnp.bfloat16),
+            jax.ShapeDtypeStruct(tied_shape, jnp.bfloat16),
+        ),
         in_specs=[pl.BlockSpec(memory_space=pltpu.HBM)] * len(operands),
-        out_specs=pl.BlockSpec(memory_space=pltpu.VMEM),
+        out_specs=(vmem, vmem),
         scratch_shapes=[pltpu.VMEM(x.shape, x.dtype) for x in operands]
-        + [
-            pltpu.VMEM((beams, channels * 2 * (station_weights.shape[2] // TPS)), jnp.bfloat16),
-            pltpu.SemaphoreType.DMA((len(operands) - 1 + 2 * groups,)),
-        ],
+        + [pltpu.SemaphoreType.DMA((len(operands) - 1 + 2 * groups,))],
         compiler_params=pltpu.CompilerParams(vmem_limit_bytes=60 * 2**20),
-        name="partial_tied",
+        name="station_beams",
     )(*operands)
-    parts = lax.all_to_all(partial, ("stn", "chan"), split_axis=0, concat_axis=0, tiled=True)
-    parts = parts.reshape(n_stn, n_chan, rows, channels, 2 * samples)
-    tied = jnp.sum(parts.astype(jnp.float32), axis=0).astype(jnp.bfloat16)
-    return tied.transpose(1, 0, 2, 3).reshape(rows, n_chan * channels, 2 * samples)
+    gathered = lax.all_gather(stations, ("stn", "chan"), axis=0, tiled=True)
+    tied = pl.pallas_call(
+        tied_kernel,
+        out_shape=jax.ShapeDtypeStruct((rows, 2 * samples, n_chan * channels), jnp.bfloat16),
+        in_specs=[vmem, vmem],
+        out_specs=vmem,
+        compiler_params=pltpu.CompilerParams(vmem_limit_bytes=32 * 2**20),
+        name="tied_beams",
+    )(gathered, tied_weight)
+    return tied.transpose(0, 2, 1)
 
 
 def solution(mesh):

time: 21 us -> 78.2 us (3.72)
  blocking collectives: 15.4 us -> 72.2 us
    all_gather x0 -> x1, blocking collectives: none -> 72.2 us  [shards(): gathered = lax.all_gather(stations, ('stn', 'chan'), axis=0, tiled=True)]
    all_to_all x1 -> x0, blocking collectives: 15.4 us -> none  [shards(): lax.all_to_all(partial, ('stn', 'chan'), split_axis=0, concat_axis=0, til...]
    reshape x2 -> x0, local copies, waits for them, and re-layouts: 0.89 us -> none  [the longest x1 0.69 us: shards(): tied.transpose(1, 0, 2, 3).reshape(rows, n_chan * channels, 2 * samples)]
    unnamed x0 -> x2, local copies, waits for them, and re-layouts: none -> 0.8 us
    pallas_call x1 -> x2, Pallas kernels: 4.38 us -> 4.99 us  [the longest x1 4 us: shards(): pl.pallas_call(kernel, out_shape=(jax.ShapeDtypeStruct((station_weights.s...]
where the time goes in v3:
time: 78.2 us; the launch traced here: 78 us
  blocking collectives  72.2 us (92%)
  Pallas kernels  4.99 us (6%)
  local copies, waits for them, and re-layouts  0.8 us (1%)
    all_gather x1, blocking collectives, shards(): gathered = lax.all_gather(stations, ('stn', 'chan'), axis=0, tiled=True)  72.2 us
    pallas_call x1, Pallas kernels, shards(): pl.pallas_call(kernel, out_shape=(jax.ShapeDtypeStruct((station_weights.s...  4 us

profile of v3, /device:TPU:0, one launch (start us, length us, event | category | flops | bytes accessed | tf_op | source)
XLA Modules:
  0.0 78.0 jit_solution(11706840340138914367)
XLA Ops:
  0.0 4.0 %station_beams.1 = (bf16[8,768]{1,0:T(8,128)(2,1)}, bf16[192,128]{1,0:T(8,128)(2,1)}) custom-call(bf16[24,2,16,2048]{3,2,1,0:T(8,128)(2,1)} %volt_hbm.1, bf16[24,2,2048]{2,1,0:T(2,128)(2,1)} %aw_hbm.1, bf16[24,2,128]{2,1,0:T(2,128)(2,1)} %sw_hbm.1, s32[1,128]{1,0:T(1,128)} %bitcast.8, s32[1,128]{1,0:T(1,128)} %bitcast.9, f32[2,128]{1,0:T(2,128)} %bitcast.6, ...), custom_call_target="tpu_custom_call" | custom-call | tf_op jit(solution)/shard_map/station_beams/pallas_call | solution.py:250
  4.0 72.2 %all_gather.3.gathered_ref = bf16[256,768]{1,0:T(8,128)(2,1)S(1)} all-gather(bf16[8,768]{1,0:T(8,128)(2,1)} %get-tuple-element.7), channel_id=1, replica_groups=mesh['stn'=16,'chan'=2] {'stn','chan'}, dimensions={0}, use_global_device_ids=true | all-gather | bytes 405504 | tf_op jit(solution)/shard_map/all_gather | solution.py:263
  76.2 0.0 copy-start
  76.2 0.8 %copy-done = bf16[192,128]{1,0:T(8,128)(2,1)S(1)} copy-done((bf16[192,128]{1,0:T(8,128)(2,1)S(1)}, bf16[192,128]{1,0:T(8,128)(2,1)}, u32[]{:S(2)}) %copy-start) | copy-done | bytes 49176
  77.0 1.0 %tied_beams.1 = bf16[2,32,48]{2,1,0:T(8,128)(2,1)} custom-call(bf16[256,768]{1,0:T(8,128)(2,1)S(1)} %all_gather.3.gathered_ref, bf16[192,128]{1,0:T(8,128)(2,1)S(1)} %copy-done), custom_call_target="tpu_custom_call" | custom-call | tf_op jit(solution)/shard_map/tied_beams/pallas_call | solution.py:264
Async XLA Ops:
  76.2 0.8 %copy-start = (bf16[192,128]{1,0:T(8,128)(2,1)S(1)}, bf16[192,128]{1,0:T(8,128)(2,1)}, u32[]{:S(2)}) copy-start(bf16[192,128]{1,0:T(8,128)(2,1)} %get-tuple-element.8.tied_ref) | copy-start | bytes 147460

commit v4 on v2

--- a/solution.py
+++ b/solution.py
@@ -25,11 +25,23 @@
     return lax.broadcasted_iota(jnp.int32, shape, dim)
 
 
+def split_devices():
+    devices = lax.axis_size("stn") * lax.axis_size("chan")
+    near = lax.axis_size("chan") * min(4, lax.axis_size("stn"))
+    return devices // near, near
+
+
 def beam_columns(order_ref, dir_ref, start, rows):
     beams = order_ref.shape[1]
     order = order_ref[...].astype(jnp.float32)
     lane = iota((rows, beams), 1)
-    own = lane == iota((rows, beams), 0) + start
+    far, near = split_devices()
+    each = beams // (far * near)
+    device = lax.axis_index("stn") * lax.axis_size("chan") + lax.axis_index("chan")
+    slot = iota((rows, beams), 0) + start
+    slot_near = (slot // (far * each)) ^ (device % near)
+    slot_far = (slot // each % far) ^ (device // near)
+    own = lane == (slot_far * near + slot_near) * each + slot % each
     ids = jnp.sum(jnp.where(own, order, 0.0), axis=1, keepdims=True)
     pick = lane.astype(jnp.float32) == ids
     east = jnp.sum(jnp.where(pick, dir_ref[0:1, :], 0.0), axis=1, keepdims=True)
@@ -70,18 +82,21 @@
     pos_hbm,
     dir_hbm,
     order_hbm,
-    out_ref,
-    volts,
-    aw_ref,
-    sw_ref,
-    ts_ref,
-    group_ref,
-    pos_ref,
-    dir_ref,
-    order_ref,
-    tied_ref,
-    sems,
+    *refs,
 ):
+    out_refs = refs[: split_devices()[1]]
+    (
+        volts,
+        aw_ref,
+        sw_ref,
+        ts_ref,
+        group_ref,
+        pos_ref,
+        dir_ref,
+        order_ref,
+        tied_ref,
+        sems,
+    ) = refs[split_devices()[1] :]
     channels, _, samples, antennas = volt_hbm.shape
     tiles = sw_ref.shape[2]
     stations = tiles // TPS
@@ -215,10 +230,30 @@
         )
         station = jnp.where(own_channel, station, 0.0).astype(jnp.bfloat16)
         tied = dot_nt(tied_ref[:, g * lanes : (g + 1) * lanes], station)
-        devices, rows, _ = out_ref.shape
-        out_ref[:, :, channel0 * rows_c : (channel0 + CB) * rows_c] = tied.astype(
-            jnp.bfloat16
-        ).reshape(devices, rows, CB * rows_c)
+        tied = tied.astype(jnp.bfloat16)
+        rows = beams // len(out_refs)
+        for k, out_ref in enumerate(out_refs):
+            out_ref[:, channel0 * rows_c : (channel0 + CB) * rows_c] = tied[
+                k * rows : (k + 1) * rows
+            ]
+
+
+def last_kernel(*refs):
+    parts, out_ref = refs[:-1], refs[-1]
+    n_chan = lax.axis_size("chan")
+    own_beams, rows_c, total_chans = out_ref.shape
+    channels = total_chans // n_chan
+    width = channels * rows_c
+    diagonal = iota((channels, width), 0) == iota((channels, width), 1) // rows_c
+    spread = (iota((rows_c, width), 0) == iota((rows_c, width), 1) % rows_c).astype(jnp.bfloat16)
+    for b in range(own_beams):
+        blocks = []
+        for chan in range(n_chan):
+            offset = lax.axis_index("chan") ^ chan
+            row = sum(part[offset, b : b + 1, :].astype(jnp.float32) for part in parts)
+            blocks.append(jnp.where(diagonal, row, 0.0))
+        rows = jnp.concatenate(blocks, axis=0).astype(jnp.bfloat16)
+        out_ref[b] = dot_nt(spread, rows).astype(jnp.bfloat16)
 
 
 def shards(
@@ -247,11 +282,14 @@
         beam_order[None, :],
     )
     groups = channels // CB
-    partial = pl.pallas_call(
+    far, near = split_devices()
+    axes = ("stn", "chan")
+    vmem = pl.BlockSpec(memory_space=pltpu.VMEM)
+    partial = list(pl.pallas_call(
         kernel,
-        out_shape=jax.ShapeDtypeStruct((n_stn * n_chan, rows, width), jnp.bfloat16),
+        out_shape=[jax.ShapeDtypeStruct((far * rows, width), jnp.bfloat16)] * near,
         in_specs=[pl.BlockSpec(memory_space=pltpu.HBM)] * len(operands),
-        out_specs=pl.BlockSpec(memory_space=pltpu.VMEM),
+        out_specs=[vmem] * near,
         scratch_shapes=[pltpu.VMEM(x.shape, x.dtype) for x in operands]
         + [
             pltpu.VMEM((beams, channels * 2 * (station_weights.shape[2] // TPS)), jnp.bfloat16),
@@ -259,11 +297,29 @@
         ],
         compiler_params=pltpu.CompilerParams(vmem_limit_bytes=60 * 2**20),
         name="partial_tied",
-    )(*operands)
-    parts = lax.all_to_all(partial, ("stn", "chan"), split_axis=0, concat_axis=0, tiled=True)
-    parts = parts.reshape(n_stn, n_chan, rows, channels, 2 * samples)
-    tied = jnp.sum(parts.astype(jnp.float32), axis=0).astype(jnp.bfloat16)
-    return tied.transpose(1, 0, 2, 3).reshape(rows, n_chan * channels, 2 * samples)
+    )(*operands))
+    for k in range(1, near):
+        perm = [(d, d ^ k) for d in range(far * near)]
+        partial[k] = lax.ppermute(partial[k], axes, perm)
+    sums = [
+        sum(block.astype(jnp.float32) for block in partial[chan::n_chan])
+        .astype(jnp.bfloat16)
+        .reshape(far, rows, width)
+        for chan in range(n_chan)
+    ]
+    parts = [jnp.stack([block[m] for block in sums]) for m in range(far)]
+    for m in range(1, far):
+        perm = [(d, d ^ (m * near)) for d in range(far * near)]
+        parts[m] = lax.ppermute(parts[m], axes, perm)
+    tied = pl.pallas_call(
+        last_kernel,
+        out_shape=jax.ShapeDtypeStruct((rows, 2 * samples, n_chan * channels), jnp.bfloat16),
+        in_specs=[vmem] * far,
+        out_specs=vmem,
+        compiler_params=pltpu.CompilerParams(vmem_limit_bytes=16 * 2**20),
+        name="tied_beams",
+    )(*parts)
+    return tied.transpose(0, 2, 1)
 
 
 def solution(mesh):

time: 21 us -> 27.1 us (1.29)
  blocking collectives: 15.4 us -> 0 us
  starting transfers between devices: 0 us -> 12.2 us
  waiting for transfers between devices: 0 us -> 8.55 us
  local copies, waits for them, and re-layouts: 0.89 us -> 0.03 us
  Pallas kernels: 4.38 us -> 5.16 us
  other arithmetic: 0.09 us -> 0.78 us
    all_to_all x1 -> x0, blocking collectives: 15.4 us -> none  [shards(): lax.all_to_all(partial, ('stn', 'chan'), split_axis=0, concat_axis=0, til...]
    ppermute x0 -> x10, starting transfers between devices: none -> 12.2 us  [the longest x7 7.64 us: shards(): partial[k] = lax.ppermute(partial[k], axes, perm)]
    ppermute x0 -> x10, waiting for transfers between devices: none -> 8.55 us  [the longest x3 5.2 us: shards(): parts[m] = lax.ppermute(parts[m], axes, perm)]
    reshape x2 -> x0, local copies, waits for them, and re-layouts: 0.89 us -> none  [the longest x1 0.69 us: shards(): tied.transpose(1, 0, 2, 3).reshape(rows, n_chan * channels, 2 * samples)]
    pallas_call x1 -> x2, Pallas kernels: 4.38 us -> 5.16 us  [the longest x1 4.37 us: shards(): pl.pallas_call(kernel, out_shape=[jax.ShapeDtypeStruct((far * rows, width...]
    convert_element_type x0 -> x2, other arithmetic: none -> 0.73 us  [shards(): sums = [sum((block.astype(jnp.float32) for block in partial[chan::n_chan]...]
  transfers between devices with their start and end apart: 0 -> 10, of which waited for: 0 -> 4; matrix products, arithmetic and copies ran while one was open for 0% -> 3% of each run, Pallas kernels for 0% -> 0%
where the time goes in v4:
time: 27.1 us; the launch traced here: 26.8 us
  starting transfers between devices  12.2 us (45%)
  waiting for transfers between devices  8.55 us (32%)
  Pallas kernels  5.16 us (19%)
  other arithmetic  0.78 us (3%)
    ppermute x7, starting transfers between devices, shards(): partial[k] = lax.ppermute(partial[k], axes, perm)  7.64 us
    ppermute x3, waiting for transfers between devices, shards(): parts[m] = lax.ppermute(parts[m], axes, perm)  5.2 us
    ppermute x3, starting transfers between devices, shards(): parts[m] = lax.ppermute(parts[m], axes, perm)  4.58 us
    pallas_call x1, Pallas kernels, shards(): pl.pallas_call(kernel, out_shape=[jax.ShapeDtypeStruct((far * rows, width...  4.37 us
    ppermute x7, waiting for transfers between devices, shards(): partial[k] = lax.ppermute(partial[k], axes, perm)  3.36 us
    pallas_call x1, Pallas kernels, shards(): pl.pallas_call(last_kernel, out_shape=jax.ShapeDtypeStruct((rows, 2 * sam...  0.79 us
    convert_element_type x2, other arithmetic, shards(): sums = [sum((block.astype(jnp.float32) for block in partial[chan::n_chan]...  0.73 us
  transfers between devices with their start and end apart: 10, of which 4 were waited for; matrix products, arithmetic and copies ran while one was open for 3% of the time, Pallas kernels for 0%

profile of v4, /device:TPU:0, one launch (start us, length us, event | category | flops | bytes accessed | tf_op | source)
XLA Modules:
  0.0 26.8 jit_solution(14388544757438359319)
XLA Ops:
  0.0 4.4 %partial_tied.1 = (bf16[8,768]{1,0:T(8,128)(2,1)}, bf16[8,768]{1,0:T(8,128)(2,1)}, bf16[8,768]{1,0:T(8,128)(2,1)}, bf16[8,768]{1,0:T(8,128)(2,1)}, bf16[8,768]{1...) custom-call(bf16[24,2,16,2048]{3,2,1,0:T(8,128)(2,1)} %volt_hbm.1, ...), custom_call_target="tpu_custom_call" | custom-call | tf_op jit(solution)/shard_map/partial_tied/pallas_call | solution.py:288
  4.4 0.5 %collective-permute-start = (bf16[8,768]{1,0:T(8,128)(2,1)}, bf16[8,768]{1,0:T(8,128)(2,1)S(1)}, u32[]{:S(2)}, u32[]{:S(2)}) collective-permute-start(bf16[8,768]{1,0:T(8,128)(2,1)} %get-tuple-element.14), channel_id=1, source_target_pairs={{0,2},{1,3},{2,0},{3,1},{4,6},{5,7},{6,4},{7,5},{8,10},{9,11},{10,... | collective-permute-start | bytes 36872 | tf_op jit(solution)/shard_map/ppermute | solution.py:303
  4.9 2.6 %collective-permute-start.1 = (bf16[8,768]{1,0:T(8,128)(2,1)}, bf16[8,768]{1,0:T(8,128)(2,1)S(1)}, u32[]{:S(2)}, u32[]{:S(2)}) collective-permute-start(bf16[8,768]{1,0:T(8,128)(2,1)} %get-tuple-element.15), channel_id=1, source_target_pairs={{0,4},{1,5},{2,6},{3,7},{4,0},{5,1},{6,2},{7,3},{8,12},{9,13},{10,... | collective-permute-start | bytes 36872 | tf_op jit(solution)/shard_map/ppermute | solution.py:303
  7.5 0.1 collective-permute-start.2
  7.6 1.7 %collective-permute-start.3 = (bf16[8,768]{1,0:T(8,128)(2,1)}, bf16[8,768]{1,0:T(8,128)(2,1)S(1)}, u32[]{:S(2)}, u32[]{:S(2)}) collective-permute-start(bf16[8,768]{1,0:T(8,128)(2,1)} %get-tuple-element.17), channel_id=1, source_target_pairs={{0,1},{1,0},{2,3},{3,2},{4,5},{5,4},{6,7},{7,6},{8,9},{9,8},{10,11... | collective-permute-start | bytes 36872 | tf_op jit(solution)/shard_map/ppermute | solution.py:303
  9.3 0.0 collective-permute-start.4
  9.3 0.0 collective-permute-done
  9.3 2.6 %collective-permute-start.5 = (bf16[8,768]{1,0:T(8,128)(2,1)}, bf16[8,768]{1,0:T(8,128)(2,1)S(1)}, u32[]{:S(2)}, u32[]{:S(2)}) collective-permute-start(bf16[8,768]{1,0:T(8,128)(2,1)} %get-tuple-element.19), channel_id=1, source_target_pairs={{0,5},{1,4},{2,7},{3,6},{4,1},{5,0},{6,3},{7,2},{8,13},{9,12},{10,... | collective-permute-start | bytes 36872 | tf_op jit(solution)/shard_map/ppermute | solution.py:303
  11.9 0.0 collective-permute-done.1
  11.9 0.1 collective-permute-start.6
  12.0 0.0 collective-permute-done.2
  12.0 0.7 %add_convert_fusion.1 = bf16[8,768]{1,0:T(8,128)(2,1)S(1)} fusion(bf16[8,768]{1,0:T(8,128)(2,1)S(1)} %collective-permute-done.2, bf16[8,768]{1,0:T(8,128)(2,1)S(1)} %collective-permute-done.1, bf16[8,768]{1,0:T(8,128)(2,1)S(1)} %collective-permute-done, bf16[8,768]{1,0:T(8,128)(2,1)} %get-tuple-element.13), kind=kLoop, calls=%fused_computation.1 | loop fusion | flops 49152 | bytes 61440 | tf_op jit(solution)/shard_map/convert_element_type | solution.py:306
  12.8 0.0 collective-permute-done.3
  12.8 0.0 collective-permute-done.4
  12.8 1.3 %collective-permute-done.5 = bf16[8,768]{1,0:T(8,128)(2,1)S(1)} collective-permute-done((bf16[8,768]{1,0:T(8,128)(2,1)}, bf16[8,768]{1,0:T(8,128)(2,1)S(1)}, u32[]{:S(2)}, u32[]{:S(2)}) %collective-permute-start.5) | collective-permute-done | bytes 12320 | tf_op jit(solution)/shard_map/ppermute | solution.py:303
  14.1 2.1 %collective-permute-done.6 = bf16[8,768]{1,0:T(8,128)(2,1)S(1)} collective-permute-done((bf16[8,768]{1,0:T(8,128)(2,1)}, bf16[8,768]{1,0:T(8,128)(2,1)S(1)}, u32[]{:S(2)}, u32[]{:S(2)}) %collective-permute-start.6) | collective-permute-done | bytes 12320 | tf_op jit(solution)/shard_map/ppermute | solution.py:303
  16.2 1.6 %collective-permute-start.7 = (bf16[2,2,768]{2,1,0:T(2,128)(2,1)S(1)}, bf16[2,2,768]{2,1,0:T(2,128)(2,1)S(1)}, u32[]{:S(2)}, u32[]{:S(2)}) collective-permute-start(bf16[2,2,768]{2,1,0:T(2,128)(2,1)S(1)} %pad_maximum_fusion.1), channel_id=1, source_target_pairs={{0,8},{1,9},{2,10},{3,11},{4,12},{5,13},{6,14},{7,15},{8,0},{9,1},... | collective-permute-start | bytes 18440 | tf_op jit(solution)/shard_map/ppermute | solution.py:313
  17.9 2.7 %collective-permute-start.8 = (bf16[2,2,768]{2,1,0:T(2,128)(2,1)S(1)}, bf16[2,2,768]{2,1,0:T(2,128)(2,1)S(1)}, u32[]{:S(2)}, u32[]{:S(2)}) collective-permute-start(bf16[2,2,768]{2,1,0:T(2,128)(2,1)S(1)} %pad_maximum_fusion.2), channel_id=1, source_target_pairs={{0,16},{1,17},{2,18},{3,19},{4,20},{5,21},{6,22},{7,23},{8,24},{9,... | collective-permute-start | bytes 18440 | tf_op jit(solution)/shard_map/ppermute | solution.py:313
  20.5 0.3 %collective-permute-start.9 = (bf16[2,2,768]{2,1,0:T(2,128)(2,1)S(1)}, bf16[2,2,768]{2,1,0:T(2,128)(2,1)S(1)}, u32[]{:S(2)}, u32[]{:S(2)}) collective-permute-start(bf16[2,2,768]{2,1,0:T(2,128)(2,1)S(1)} %pad_maximum_fusion.3), channel_id=1, source_target_pairs={{0,24},{1,25},{2,26},{3,27},{4,28},{5,29},{6,30},{7,31},{8,16},{9,... | collective-permute-start | bytes 18440 | tf_op jit(solution)/shard_map/ppermute | solution.py:313
  20.8 0.0 collective-permute-done.7.refs_1_
  20.8 1.6 %collective-permute-done.8.refs_2_ = bf16[2,2,768]{2,1,0:T(2,128)(2,1)S(1)} collective-permute-done((bf16[2,2,768]{2,1,0:T(2,128)(2,1)S(1)}, bf16[2,2,768]{2,1,0:T(2,128)(2,1)S(1)}, u32[]{:S(2)}, u32[]{:S(2)}) %collective-permute-start.8) | collective-permute-done | bytes 6176 | tf_op jit(solution)/shard_map/ppermute | solution.py:313
  22.5 3.6 %collective-permute-done.9.refs_3_ = bf16[2,2,768]{2,1,0:T(2,128)(2,1)S(1)} collective-permute-done((bf16[2,2,768]{2,1,0:T(2,128)(2,1)S(1)}, bf16[2,2,768]{2,1,0:T(2,128)(2,1)S(1)}, u32[]{:S(2)}, u32[]{:S(2)}) %collective-permute-start.9) | collective-permute-done | bytes 6176 | tf_op jit(solution)/shard_map/ppermute | solution.py:313
  26.0 0.8 %tied_beams.1 = bf16[2,32,48]{2,1,0:T(8,128)(2,1)} custom-call(bf16[2,2,768]{2,1,0:T(2,128)(2,1)S(1)} %pad_maximum_fusion.refs_0_, bf16[2,2,768]{2,1,0:T(2,128)(2,1)S(1)} %collective-permute-done.7.refs_1_, bf16[2,2,768]{2,1,0:T(2,128)(2,1)S(1)} %collective-permute-done.8.refs_2_, bf16[2,2,768]{2,1,0:T(2,128)(2,1)S(1)} %collective-permute-done.9.refs_3_), custom_call_target="tpu_custom_call" | custom-call | tf_op jit(solution)/shard_map/tied_beams/pallas_call | solution.py:314
  (7 shorter events, 0.1 us)
Async XLA Ops:
  4.4 4.9 %collective-permute-start = (bf16[8,768]{1,0:T(8,128)(2,1)}, bf16[8,768]{1,0:T(8,128)(2,1)S(1)}, u32[]{:S(2)}, u32[]{:S(2)}) collective-permute-start(bf16[8,768]{1,0:T(8,128)(2,1)} %get-tuple-element.14), channel_id=1, source_target_pairs={{0,2},{1,3},{2,0},{3,1},{4,6},{5,7},{6,4},{7,5},{8,10},{9,11},{10,... | collective-permute-start | bytes 36872 | tf_op jit(solution)/shard_map/ppermute | solution.py:303
  4.9 7.0 %collective-permute-start.1 = (bf16[8,768]{1,0:T(8,128)(2,1)}, bf16[8,768]{1,0:T(8,128)(2,1)S(1)}, u32[]{:S(2)}, u32[]{:S(2)}) collective-permute-start(bf16[8,768]{1,0:T(8,128)(2,1)} %get-tuple-element.15), channel_id=1, source_target_pairs={{0,4},{1,5},{2,6},{3,7},{4,0},{5,1},{6,2},{7,3},{8,12},{9,13},{10,... | collective-permute-start | bytes 36872 | tf_op jit(solution)/shard_map/ppermute | solution.py:303
  7.5 4.5 %collective-permute-start.2 = (bf16[8,768]{1,0:T(8,128)(2,1)}, bf16[8,768]{1,0:T(8,128)(2,1)S(1)}, u32[]{:S(2)}, u32[]{:S(2)}) collective-permute-start(bf16[8,768]{1,0:T(8,128)(2,1)} %get-tuple-element.16), channel_id=1, source_target_pairs={{0,6},{1,7},{2,4},{3,5},{4,2},{5,3},{6,0},{7,1},{8,14},{9,15},{10,... | collective-permute-start | bytes 36872 | tf_op jit(solution)/shard_map/ppermute | solution.py:303
  7.6 5.2 %collective-permute-start.3 = (bf16[8,768]{1,0:T(8,128)(2,1)}, bf16[8,768]{1,0:T(8,128)(2,1)S(1)}, u32[]{:S(2)}, u32[]{:S(2)}) collective-permute-start(bf16[8,768]{1,0:T(8,128)(2,1)} %get-tuple-element.17), channel_id=1, source_target_pairs={{0,1},{1,0},{2,3},{3,2},{4,5},{5,4},{6,7},{7,6},{8,9},{9,8},{10,11... | collective-permute-start | bytes 36872 | tf_op jit(solution)/shard_map/ppermute | solution.py:303
  9.3 3.5 %collective-permute-start.4 = (bf16[8,768]{1,0:T(8,128)(2,1)}, bf16[8,768]{1,0:T(8,128)(2,1)S(1)}, u32[]{:S(2)}, u32[]{:S(2)}) collective-permute-start(bf16[8,768]{1,0:T(8,128)(2,1)} %get-tuple-element.18), channel_id=1, source_target_pairs={{0,3},{1,2},{2,1},{3,0},{4,7},{5,6},{6,5},{7,4},{8,11},{9,10},{10,... | collective-permute-start | bytes 36872 | tf_op jit(solution)/shard_map/ppermute | solution.py:303
  9.3 4.8 %collective-permute-start.5 = (bf16[8,768]{1,0:T(8,128)(2,1)}, bf16[8,768]{1,0:T(8,128)(2,1)S(1)}, u32[]{:S(2)}, u32[]{:S(2)}) collective-permute-start(bf16[8,768]{1,0:T(8,128)(2,1)} %get-tuple-element.19), channel_id=1, source_target_pairs={{0,5},{1,4},{2,7},{3,6},{4,1},{5,0},{6,3},{7,2},{8,13},{9,12},{10,... | collective-permute-start | bytes 36872 | tf_op jit(solution)/shard_map/ppermute | solution.py:303
  11.9 4.2 %collective-permute-start.6 = (bf16[8,768]{1,0:T(8,128)(2,1)}, bf16[8,768]{1,0:T(8,128)(2,1)S(1)}, u32[]{:S(2)}, u32[]{:S(2)}) collective-permute-start(bf16[8,768]{1,0:T(8,128)(2,1)} %get-tuple-element.20), channel_id=1, source_target_pairs={{0,7},{1,6},{2,5},{3,4},{4,3},{5,2},{6,1},{7,0},{8,15},{9,14},{10,... | collective-permute-start | bytes 36872 | tf_op jit(solution)/shard_map/ppermute | solution.py:303
  16.2 4.6 %collective-permute-start.7 = (bf16[2,2,768]{2,1,0:T(2,128)(2,1)S(1)}, bf16[2,2,768]{2,1,0:T(2,128)(2,1)S(1)}, u32[]{:S(2)}, u32[]{:S(2)}) collective-permute-start(bf16[2,2,768]{2,1,0:T(2,128)(2,1)S(1)} %pad_maximum_fusion.1), channel_id=1, source_target_pairs={{0,8},{1,9},{2,10},{3,11},{4,12},{5,13},{6,14},{7,15},{8,0},{9,1},... | collective-permute-start | bytes 18440 | tf_op jit(solution)/shard_map/ppermute | solution.py:313
  17.9 4.6 %collective-permute-start.8 = (bf16[2,2,768]{2,1,0:T(2,128)(2,1)S(1)}, bf16[2,2,768]{2,1,0:T(2,128)(2,1)S(1)}, u32[]{:S(2)}, u32[]{:S(2)}) collective-permute-start(bf16[2,2,768]{2,1,0:T(2,128)(2,1)S(1)} %pad_maximum_fusion.2), channel_id=1, source_target_pairs={{0,16},{1,17},{2,18},{3,19},{4,20},{5,21},{6,22},{7,23},{8,24},{9,... | collective-permute-start | bytes 18440 | tf_op jit(solution)/shard_map/ppermute | solution.py:313
  20.5 5.5 %collective-permute-start.9 = (bf16[2,2,768]{2,1,0:T(2,128)(2,1)S(1)}, bf16[2,2,768]{2,1,0:T(2,128)(2,1)S(1)}, u32[]{:S(2)}, u32[]{:S(2)}) collective-permute-start(bf16[2,2,768]{2,1,0:T(2,128)(2,1)S(1)} %pad_maximum_fusion.3), channel_id=1, source_target_pairs={{0,24},{1,25},{2,26},{3,27},{4,28},{5,29},{6,30},{7,31},{8,16},{9,... | collective-permute-start | bytes 18440 | tf_op jit(solution)/shard_map/ppermute | solution.py:313

commit v5 on v2

--- a/solution.py
+++ b/solution.py
@@ -12,7 +12,6 @@
 TPS = 16
 GROUPS = 4
 CB = 8
-CHUNK = 256
 NT = (((1,), (1,)), ((), ()))
 SIN = [(-1) ** i * (2 * math.pi) ** (2 * i + 1) / math.factorial(2 * i + 1) for i in range(7)]
 
@@ -80,13 +79,12 @@
     dir_ref,
     order_ref,
     tied_ref,
+    sum_ref,
     sems,
 ):
     channels, _, samples, antennas = volt_hbm.shape
     tiles = sw_ref.shape[2]
     stations = tiles // TPS
-    chunks = antennas // CHUNK
-    per_chunk = CHUNK // TILE_ANTENNAS
     groups = channels // CB
     rows_c = 2 * samples
     beams = order_ref.shape[1]
@@ -148,59 +146,34 @@
 
         lax.fori_loop(0, beams // block, body, 0)
 
+    antenna_tile = iota((antennas, tiles), 0) // TILE_ANTENNAS == iota((antennas, tiles), 1)
+    sum_ref[...] = antenna_tile.astype(jnp.bfloat16)
     for copy in small[4:]:
         copy.wait()
-    mask16 = (iota((per_chunk, CHUNK), 1) // TILE_ANTENNAS == iota((per_chunk, CHUNK), 0)).astype(
-        jnp.float32
-    )
     member_table = (iota((stations, tiles), 0) == ts_ref[...] % stations).astype(jnp.float32)
-    own_channel = iota((CB * rows_c, lanes), 0) // rows_c == iota((CB * rows_c, lanes), 1) // (
-        2 * stations
-    )
-    lane_chunk = iota((rows_c, 2 * tiles), 1) // per_chunk % chunks
+    own_channel = iota((lanes, CB * rows_c), 0) // (2 * stations) == iota(
+        (lanes, CB * rows_c), 1
+    ) // rows_c
 
     for g in range(groups):
         channel0 = g * CB
         weights = aw_ref[channel0 : channel0 + CB].astype(jnp.float32)
         large[2 * g].wait()
         large[2 * g + 1].wait()
-        found = [None] * CB
-        for step in range(chunks):
-            left = jnp.concatenate(
-                [
-                    volts[
-                        channel0 + c,
-                        :,
-                        :,
-                        (c + step) % chunks * CHUNK : ((c + step) % chunks + 1) * CHUNK,
-                    ].reshape(rows_c, CHUNK)
-                    for c in range(CB)
-                ],
-                axis=0,
-            )
-            right = jnp.concatenate(
-                [
-                    (
-                        weights[(q - step) % CB, part : part + 1, q * CHUNK : (q + 1) * CHUNK]
-                        * mask16
-                    ).astype(jnp.bfloat16)
-                    for part in range(2)
-                    for q in range(chunks)
-                ],
-                axis=0,
-            )
-            product = dot_nt(left, right)
-            for c in range(CB):
-                mine = product[c * rows_c : (c + 1) * rows_c]
-                if step == 0:
-                    found[c] = mine
-                else:
-                    found[c] = jnp.where(lane_chunk == (c + step) % chunks, mine, found[c])
+        products = []
+        for c in range(CB):
+            w_re = jnp.broadcast_to(weights[c, 0:1], (samples, antennas)).astype(jnp.bfloat16)
+            w_im = jnp.broadcast_to(weights[c, 1:2], (samples, antennas)).astype(jnp.bfloat16)
+            v_re, v_im = volts[channel0 + c, 0], volts[channel0 + c, 1]
+            products.append(w_re * v_re - w_im * v_im)
+            products.append(w_re * v_im + w_im * v_re)
+        beams_tile = jnp.dot(
+            jnp.concatenate(products, axis=0), sum_ref[...], preferred_element_type=jnp.float32
+        ).astype(jnp.bfloat16)
         left = []
         for c in range(CB):
-            real, imag = found[c][:samples], found[c][samples:]
-            tile_re = (real[:, :tiles] - imag[:, tiles:]).astype(jnp.bfloat16)
-            tile_im = (imag[:, :tiles] + real[:, tiles:]).astype(jnp.bfloat16)
+            tile_re = beams_tile[c * rows_c : c * rows_c + samples]
+            tile_im = beams_tile[c * rows_c + samples : (c + 1) * rows_c]
             left.append(jnp.concatenate([tile_re, tile_im], axis=1))
             left.append(jnp.concatenate([tile_im, -tile_re], axis=1))
         right = []
@@ -211,14 +184,31 @@
             right.append(jnp.concatenate([re, -im], axis=1))
             right.append(jnp.concatenate([im, re], axis=1))
         station = dot_nt(
-            jnp.concatenate(left, axis=0), jnp.concatenate(right, axis=0).astype(jnp.bfloat16)
+            jnp.concatenate(right, axis=0).astype(jnp.bfloat16), jnp.concatenate(left, axis=0)
         )
         station = jnp.where(own_channel, station, 0.0).astype(jnp.bfloat16)
-        tied = dot_nt(tied_ref[:, g * lanes : (g + 1) * lanes], station)
+        tied = jnp.dot(
+            tied_ref[:, g * lanes : (g + 1) * lanes], station, preferred_element_type=jnp.float32
+        )
         devices, rows, _ = out_ref.shape
         out_ref[:, :, channel0 * rows_c : (channel0 + CB) * rows_c] = tied.astype(
             jnp.bfloat16
         ).reshape(devices, rows, CB * rows_c)
+
+
+def last_kernel(parts_ref, out_ref):
+    n_stn, n_chan = lax.axis_size("stn"), lax.axis_size("chan")
+    own_beams, rows_c, total_chans = out_ref.shape
+    channels = total_chans // n_chan
+    width = channels * rows_c
+    parts = parts_ref[...].astype(jnp.float32).reshape(n_stn, n_chan, own_beams, width)
+    tied = jnp.sum(parts, axis=0)
+    diagonal = iota((channels, width), 0) == iota((channels, width), 1) // rows_c
+    spread = (iota((rows_c, width), 0) == iota((rows_c, width), 1) % rows_c).astype(jnp.bfloat16)
+    for b in range(own_beams):
+        rows = [jnp.where(diagonal, tied[chan, b : b + 1], 0.0) for chan in range(n_chan)]
+        rows = jnp.concatenate(rows, axis=0).astype(jnp.bfloat16)
+        out_ref[b] = dot_nt(spread, rows).astype(jnp.bfloat16)
 
 
 def shards(
@@ -255,15 +245,23 @@
         scratch_shapes=[pltpu.VMEM(x.shape, x.dtype) for x in operands]
         + [
             pltpu.VMEM((beams, channels * 2 * (station_weights.shape[2] // TPS)), jnp.bfloat16),
+            pltpu.VMEM((volts.shape[3], station_weights.shape[2]), jnp.bfloat16),
             pltpu.SemaphoreType.DMA((len(operands) - 1 + 2 * groups,)),
         ],
         compiler_params=pltpu.CompilerParams(vmem_limit_bytes=60 * 2**20),
         name="partial_tied",
     )(*operands)
     parts = lax.all_to_all(partial, ("stn", "chan"), split_axis=0, concat_axis=0, tiled=True)
-    parts = parts.reshape(n_stn, n_chan, rows, channels, 2 * samples)
-    tied = jnp.sum(parts.astype(jnp.float32), axis=0).astype(jnp.bfloat16)
-    return tied.transpose(1, 0, 2, 3).reshape(rows, n_chan * channels, 2 * samples)
+    vmem = pl.BlockSpec(memory_space=pltpu.VMEM)
+    tied = pl.pallas_call(
+        last_kernel,
+        out_shape=jax.ShapeDtypeStruct((rows, 2 * samples, n_chan * channels), jnp.bfloat16),
+        in_specs=[vmem],
+        out_specs=vmem,
+        compiler_params=pltpu.CompilerParams(vmem_limit_bytes=16 * 2**20),
+        name="tied_beams",
+    )(parts)
+    return tied.transpose(0, 2, 1)
 
 
 def solution(mesh):

time: 21 us -> 20.8 us (level)
  local copies, waits for them, and re-layouts: 0.89 us -> 0 us
  Pallas kernels: 4.38 us -> 5.18 us
    reshape x2 -> x0, local copies, waits for them, and re-layouts: 0.89 us -> none  [the longest x1 0.69 us: shards(): tied.transpose(1, 0, 2, 3).reshape(rows, n_chan * channels, 2 * samples)]
    pallas_call x0 -> x1, Pallas kernels: none -> 0.86 us  [shards(): pl.pallas_call(last_kernel, out_shape=jax.ShapeDtypeStruct((rows, 2 * sam...]
where the time goes in v5:
time: 20.8 us; the launch traced here: 20.6 us
  blocking collectives  15.4 us (74%)
  Pallas kernels  5.18 us (25%)
    all_to_all x1, blocking collectives, shards(): lax.all_to_all(partial, ('stn', 'chan'), split_axis=0, concat_axis=0, til...  15.4 us
    pallas_call x1, Pallas kernels, shards(): pl.pallas_call(kernel, out_shape=jax.ShapeDtypeStruct((n_stn * n_chan, ro...  4.32 us
    pallas_call x1, Pallas kernels, shards(): pl.pallas_call(last_kernel, out_shape=jax.ShapeDtypeStruct((rows, 2 * sam...  0.86 us

profile of v5, /device:TPU:0, one launch (start us, length us, event | category | flops | bytes accessed | tf_op | source)
XLA Modules:
  0.0 20.6 jit_solution(1618799469051774239)
XLA Ops:
  0.0 4.3 %partial_tied.1 = bf16[32,2,768]{2,1,0:T(2,128)(2,1)} custom-call(bf16[24,2,16,2048]{3,2,1,0:T(8,128)(2,1)} %volt_hbm.1, bf16[24,2,2048]{2,1,0:T(2,128)(2,1)} %aw_hbm.1, bf16[24,2,128]{2,1,0:T(2,128)(2,1)} %sw_hbm.1, s32[1,128]{1,0:T(1,128)} %bitcast.8, s32[1,128]{1,0:T(1,128)} %bitcast.9, f32[2,128]{1,0:T(2,128)} %bitcast.6, f32[2,64]{1,0:T(2,128)} %bitcast.7, ...), custom_call_target="tpu_custom_call" | custom-call | tf_op jit(solution)/shard_map/partial_tied/pallas_call | solution.py:240
  4.3 15.4 %all_to_all.5.parts_ref = bf16[32,2,768]{2,1,0:T(2,128)(2,1)S(1)} all-to-all(bf16[32,2,768]{2,1,0:T(2,128)(2,1)} %partial_tied.1), channel_id=1, replica_groups=mesh['stn'=16,'chan'=2] {'stn','chan'}, dimensions={0} | all-to-all | bytes 196608 | tf_op jit(solution)/shard_map/all_to_all | solution.py:254
  19.8 0.9 %tied_beams.1 = bf16[2,32,48]{2,1,0:T(8,128)(2,1)} custom-call(bf16[32,2,768]{2,1,0:T(2,128)(2,1)S(1)} %all_to_all.5.parts_ref), custom_call_target="tpu_custom_call" | custom-call | tf_op jit(solution)/shard_map/tied_beams/pallas_call | solution.py:256

commit v6 on v5

--- a/solution.py
+++ b/solution.py
@@ -236,10 +236,11 @@
         beam_dir.T,
         beam_order[None, :],
     )
+    operands = [pltpu.with_memory_space_constraint(x, pltpu.HBM) for x in operands]
     groups = channels // CB
     partial = pl.pallas_call(
         kernel,
-        out_shape=jax.ShapeDtypeStruct((n_stn * n_chan, rows, width), jnp.bfloat16),
+        out_shape=pltpu.VMEM((n_stn * n_chan, rows, width), jnp.bfloat16),
         in_specs=[pl.BlockSpec(memory_space=pltpu.HBM)] * len(operands),
         out_specs=pl.BlockSpec(memory_space=pltpu.VMEM),
         scratch_shapes=[pltpu.VMEM(x.shape, x.dtype) for x in operands]
@@ -248,7 +249,7 @@
             pltpu.VMEM((volts.shape[3], station_weights.shape[2]), jnp.bfloat16),
             pltpu.SemaphoreType.DMA((len(operands) - 1 + 2 * groups,)),
         ],
-        compiler_params=pltpu.CompilerParams(vmem_limit_bytes=60 * 2**20),
+        compiler_params=pltpu.CompilerParams(vmem_limit_bytes=24 * 2**20),
         name="partial_tied",
     )(*operands)
     parts = lax.all_to_all(partial, ("stn", "chan"), split_axis=0, concat_axis=0, tiled=True)

time: 20.8 us -> 19.9 us (0.957)
  Pallas kernels: 5.18 us -> 4.56 us
    pallas_call x1, Pallas kernels: 4.32 us -> 3.7 us  [shards(): pl.pallas_call(kernel, out_shape=pltpu.VMEM((n_stn * n_chan, rows, width)...]
    all_to_all x1, blocking collectives: 15.4 us -> 15.2 us  [shards(): lax.all_to_all(partial, ('stn', 'chan'), split_axis=0, concat_axis=0, til...]
where the time goes in v6:
time: 19.9 us; the launch traced here: 19.8 us
  blocking collectives  15.2 us (76%)
  Pallas kernels  4.56 us (23%)
    all_to_all x1, blocking collectives, shards(): lax.all_to_all(partial, ('stn', 'chan'), split_axis=0, concat_axis=0, til...  15.2 us
    pallas_call x1, Pallas kernels, shards(): pl.pallas_call(kernel, out_shape=pltpu.VMEM((n_stn * n_chan, rows, width)...  3.7 us
    pallas_call x1, Pallas kernels, shards(): pl.pallas_call(last_kernel, out_shape=jax.ShapeDtypeStruct((rows, 2 * sam...  0.86 us

profile of v6, /device:TPU:0, one launch (start us, length us, event | category | flops | bytes accessed | tf_op | source)
XLA Modules:
  0.0 19.8 jit_solution(13514583538820509836)
XLA Ops:
  0.0 3.7 %partial_tied.1 = bf16[32,2,768]{2,1,0:T(2,128)(2,1)S(1)} custom-call(bf16[24,2,16,2048]{3,2,1,0:T(8,128)(2,1)} %volt_hbm.1, bf16[24,2,2048]{2,1,0:T(2,128)(2,1)} %aw_hbm.1, bf16[24,2,128]{2,1,0:T(2,128)(2,1)} %sw_hbm.1, s32[1,128]{1,0:T(1,128)} %bitcast.8, s32[1,128]{1,0:T(1,128)} %bitcast.9, f32[2,128]{1,0:T(2,128)} %bitcast.6, f32[2,64]{1,0:T(2,128)} %bitcast.7, ...), custom_call_target="tpu_custom_call" | custom-call | tf_op jit(solution)/shard_map/partial_tied/pallas_call | solution.py:241
  3.7 15.2 %all_to_all.5.parts_ref = bf16[32,2,768]{2,1,0:T(2,128)(2,1)S(1)} all-to-all(bf16[32,2,768]{2,1,0:T(2,128)(2,1)S(1)} %partial_tied.1), channel_id=1, replica_groups=mesh['stn'=16,'chan'=2] {'stn','chan'}, dimensions={0} | all-to-all | bytes 196608 | tf_op jit(solution)/shard_map/all_to_all | solution.py:255
  18.9 0.9 %tied_beams.1 = bf16[2,32,48]{2,1,0:T(8,128)(2,1)} custom-call(bf16[32,2,768]{2,1,0:T(2,128)(2,1)S(1)} %all_to_all.5.parts_ref), custom_call_target="tpu_custom_call" | custom-call | tf_op jit(solution)/shard_map/tied_beams/pallas_call | solution.py:257

commit v7 on v6

--- a/solution.py
+++ b/solution.py
@@ -28,7 +28,12 @@
     beams = order_ref.shape[1]
     order = order_ref[...].astype(jnp.float32)
     lane = iota((rows, beams), 1)
-    own = lane == iota((rows, beams), 0) + start
+    n_chan = lax.axis_size("chan")
+    each = beams // (n_chan * lax.axis_size("stn"))
+    slot = iota((rows, beams), 0) + start
+    low = (slot // (beams // 2)) ^ (lax.axis_index("stn") % 2)
+    pair, rest = slot % (beams // 2) // (n_chan * each), slot % (n_chan * each)
+    own = lane == (pair * 2 + low) * (n_chan * each) + rest
     ids = jnp.sum(jnp.where(own, order, 0.0), axis=1, keepdims=True)
     pick = lane.astype(jnp.float32) == ids
     east = jnp.sum(jnp.where(pick, dir_ref[0:1, :], 0.0), axis=1, keepdims=True)
@@ -69,7 +74,8 @@
     pos_hbm,
     dir_hbm,
     order_hbm,
-    out_ref,
+    keep_ref,
+    send_ref,
     volts,
     aw_ref,
     sw_ref,
@@ -190,18 +196,21 @@
         tied = jnp.dot(
             tied_ref[:, g * lanes : (g + 1) * lanes], station, preferred_element_type=jnp.float32
         )
-        devices, rows, _ = out_ref.shape
-        out_ref[:, :, channel0 * rows_c : (channel0 + CB) * rows_c] = tied.astype(
-            jnp.bfloat16
-        ).reshape(devices, rows, CB * rows_c)
+        tied = tied.astype(jnp.bfloat16)
+        columns = slice(channel0 * rows_c, (channel0 + CB) * rows_c)
+        for half, out_ref in enumerate((keep_ref, send_ref)):
+            devices, rows, _ = out_ref.shape
+            part = tied[half * devices * rows : (half + 1) * devices * rows]
+            out_ref[:, :, columns] = part.reshape(devices, rows, CB * rows_c)
 
 
 def last_kernel(parts_ref, out_ref):
-    n_stn, n_chan = lax.axis_size("stn"), lax.axis_size("chan")
+    n_chan = lax.axis_size("chan")
+    pairs = lax.axis_size("stn") // 2
     own_beams, rows_c, total_chans = out_ref.shape
     channels = total_chans // n_chan
     width = channels * rows_c
-    parts = parts_ref[...].astype(jnp.float32).reshape(n_stn, n_chan, own_beams, width)
+    parts = parts_ref[...].astype(jnp.float32).reshape(pairs, n_chan, own_beams, width)
     tied = jnp.sum(parts, axis=0)
     diagonal = iota((channels, width), 0) == iota((channels, width), 1) // rows_c
     spread = (iota((rows_c, width), 0) == iota((rows_c, width), 1) % rows_c).astype(jnp.bfloat16)
@@ -238,11 +247,11 @@
     )
     operands = [pltpu.with_memory_space_constraint(x, pltpu.HBM) for x in operands]
     groups = channels // CB
-    partial = pl.pallas_call(
+    keep, send = pl.pallas_call(
         kernel,
-        out_shape=pltpu.VMEM((n_stn * n_chan, rows, width), jnp.bfloat16),
+        out_shape=[pltpu.VMEM((n_stn // 2 * n_chan, rows, width), jnp.bfloat16)] * 2,
         in_specs=[pl.BlockSpec(memory_space=pltpu.HBM)] * len(operands),
-        out_specs=pl.BlockSpec(memory_space=pltpu.VMEM),
+        out_specs=[pl.BlockSpec(memory_space=pltpu.VMEM)] * 2,
         scratch_shapes=[pltpu.VMEM(x.shape, x.dtype) for x in operands]
         + [
             pltpu.VMEM((beams, channels * 2 * (station_weights.shape[2] // TPS)), jnp.bfloat16),
@@ -252,7 +261,14 @@
         compiler_params=pltpu.CompilerParams(vmem_limit_bytes=24 * 2**20),
         name="partial_tied",
     )(*operands)
-    parts = lax.all_to_all(partial, ("stn", "chan"), split_axis=0, concat_axis=0, tiled=True)
+    axes = ("stn", "chan")
+    flat = range(n_stn * n_chan)
+    received = lax.ppermute(send, axes, [(d, d ^ n_chan) for d in flat])
+    pair_sum = (keep.astype(jnp.float32) + received.astype(jnp.float32)).astype(jnp.bfloat16)
+    groups = [[d for d in flat if d // n_chan % 2 == low] for low in range(2)]
+    parts = lax.all_to_all(
+        pair_sum, axes, split_axis=0, concat_axis=0, axis_index_groups=groups, tiled=True
+    )
     vmem = pl.BlockSpec(memory_space=pltpu.VMEM)
     tied = pl.pallas_call(
         last_kernel,

time: 19.9 us -> 21.6 us (1.085)
  waiting for transfers between devices: 0 us -> 0.88 us
  starting transfers between devices: 0 us -> 0.52 us
  blocking collectives: 15.2 us -> 15.5 us
    ppermute x0 -> x1, waiting for transfers between devices: none -> 0.88 us  [shards(): received = lax.ppermute(send, axes, [(d, d ^ n_chan) for d in flat])]
    ppermute x0 -> x1, starting transfers between devices: none -> 0.52 us  [shards(): received = lax.ppermute(send, axes, [(d, d ^ n_chan) for d in flat])]
    all_to_all x1, blocking collectives: 15.2 us -> 15.5 us  [shards(): lax.all_to_all(pair_sum, axes, split_axis=0, concat_axis=0, axis_index_gr...]
  transfers between devices with their start and end apart: 0 -> 1, of which waited for: 0 -> 1; matrix products, arithmetic and copies ran while one was open for 0% -> 0% of each run, Pallas kernels for 0% -> 0%
where the time goes in v7:
time: 21.6 us; the launch traced here: 21.4 us
  blocking collectives  15.5 us (72%)
  Pallas kernels  4.51 us (21%)
  waiting for transfers between devices  0.88 us (4%)
  starting transfers between devices  0.52 us (2%)
    all_to_all x1, blocking collectives, shards(): lax.all_to_all(pair_sum, axes, split_axis=0, concat_axis=0, axis_index_gr...  15.5 us
    pallas_call x1, Pallas kernels, shards(): pl.pallas_call(kernel, out_shape=[pltpu.VMEM((n_stn // 2 * n_chan, rows,...  3.7 us
    ppermute x1, waiting for transfers between devices, shards(): received = lax.ppermute(send, axes, [(d, d ^ n_chan) for d in flat])  0.88 us
    pallas_call x1, Pallas kernels, shards(): pl.pallas_call(last_kernel, out_shape=jax.ShapeDtypeStruct((rows, 2 * sam...  0.81 us
    ppermute x1, starting transfers between devices, shards(): received = lax.ppermute(send, axes, [(d, d ^ n_chan) for d in flat])  0.52 us
  transfers between devices with their start and end apart: 1, of which 1 were waited for; matrix products, arithmetic and copies ran while one was open for 0% of the time, Pallas kernels for 0%

profile of v7, /device:TPU:0, one launch (start us, length us, event | category | flops | bytes accessed | tf_op | source)
XLA Modules:
  0.0 21.4 jit_solution(11865660194416902585)
XLA Ops:
  0.0 3.7 %partial_tied.1 = (bf16[16,2,768]{2,1,0:T(2,128)(2,1)S(1)}, bf16[16,2,768]{2,1,0:T(2,128)(2,1)S(1)}) custom-call(bf16[24,2,16,2048]{3,2,1,0:T(8,128)(2,1)} %volt_hbm.1, bf16[24,2,2048]{2,1,0:T(2,128)(2,1)} %aw_hbm.1, bf16[24,2,128]{2,1,0:T(2,128)(2,1)} %sw_hbm.1, s32[1,128]{1,0:T(1,128)} %bitcast.8, s32[1,128]{1,0:T(1,128)} %bitcast.9, f32[2,128]{1,0:T(2,128)} %bitcast.6, ...), custom_call_target="tpu_custom_call" | custom-call | tf_op jit(solution)/shard_map/partial_tied/pallas_call | solution.py:250
  3.7 0.5 %collective-permute-start = (bf16[16,2,768]{2,1,0:T(2,128)(2,1)S(1)}, bf16[16,2,768]{2,1,0:T(2,128)(2,1)S(1)}, u32[]{:S(2)}, u32[]{:S(2)}) collective-permute-start(bf16[16,2,768]{2,1,0:T(2,128)(2,1)S(1)} %get-tuple-element.8), channel_id=1, source_target_pairs={{0,2},{1,3},{2,0},{3,1},{4,6},{5,7},{6,4},{7,5},{8,10},{9,11},{10,... | collective-permute-start | bytes 147464 | tf_op jit(solution)/shard_map/ppermute | solution.py:266
  4.2 0.9 %collective-permute-done = bf16[16,2,768]{2,1,0:T(2,128)(2,1)S(1)} collective-permute-done((bf16[16,2,768]{2,1,0:T(2,128)(2,1)S(1)}, bf16[16,2,768]{2,1,0:T(2,128)(2,1)S(1)}, u32[]{:S(2)}, u32[]{:S(2)}) %collective-permute-start) | collective-permute-done | bytes 49184 | tf_op jit(solution)/shard_map/ppermute | solution.py:266
  5.1 0.1 add_convert_fusion
  5.2 15.5 %all_to_all.5.parts_ref = bf16[16,2,768]{2,1,0:T(2,128)(2,1)S(1)} all-to-all(bf16[16,2,768]{2,1,0:T(2,128)(2,1)S(1)} %add_convert_fusion), channel_id=1, replica_groups={{0,1,4,5,8,9,12,13,16,17,20,21,24,25,28,29},{2,3,6,7,10,11,14,15,18,19,..., dimensions={0} | all-to-all | bytes 98304 | tf_op jit(solution)/shard_map/all_to_all | solution.py:269
  20.6 0.8 %tied_beams.1 = bf16[2,32,48]{2,1,0:T(8,128)(2,1)} custom-call(bf16[16,2,768]{2,1,0:T(2,128)(2,1)S(1)} %all_to_all.5.parts_ref), custom_call_target="tpu_custom_call" | custom-call | tf_op jit(solution)/shard_map/tied_beams/pallas_call | solution.py:273
Async XLA Ops:
  3.7 1.4 %collective-permute-start = (bf16[16,2,768]{2,1,0:T(2,128)(2,1)S(1)}, bf16[16,2,768]{2,1,0:T(2,128)(2,1)S(1)}, u32[]{:S(2)}, u32[]{:S(2)}) collective-permute-start(bf16[16,2,768]{2,1,0:T(2,128)(2,1)S(1)} %get-tuple-element.8), channel_id=1, source_target_pairs={{0,2},{1,3},{2,0},{3,1},{4,6},{5,7},{6,4},{7,5},{8,10},{9,11},{10,... | collective-permute-start | bytes 147464 | tf_op jit(solution)/shard_map/ppermute | solution.py:266

commit v8 on v7

--- a/solution.py
+++ b/solution.py
@@ -28,12 +28,16 @@
     beams = order_ref.shape[1]
     order = order_ref[...].astype(jnp.float32)
     lane = iota((rows, beams), 1)
-    n_chan = lax.axis_size("chan")
-    each = beams // (n_chan * lax.axis_size("stn"))
+    n_stn, n_chan = lax.axis_size("stn"), lax.axis_size("chan")
+    each = beams // (n_stn * n_chan)
     slot = iota((rows, beams), 0) + start
-    low = (slot // (beams // 2)) ^ (lax.axis_index("stn") % 2)
-    pair, rest = slot % (beams // 2) // (n_chan * each), slot % (n_chan * each)
-    own = lane == (pair * 2 + low) * (n_chan * each) + rest
+    device = slot // each
+    bits = n_stn.bit_length() - 1
+    stn = lax.axis_index("stn")
+    for bit in range(bits):
+        stn = stn ^ (((device // n_chan) >> (bits - 1 - bit)) % 2 << bit)
+    chan = device % n_chan ^ lax.axis_index("chan")
+    own = lane == (stn * n_chan + chan) * each + slot % each
     ids = jnp.sum(jnp.where(own, order, 0.0), axis=1, keepdims=True)
     pick = lane.astype(jnp.float32) == ids
     east = jnp.sum(jnp.where(pick, dir_ref[0:1, :], 0.0), axis=1, keepdims=True)
@@ -204,18 +208,23 @@
             out_ref[:, :, columns] = part.reshape(devices, rows, CB * rows_c)
 
 
-def last_kernel(parts_ref, out_ref):
-    n_chan = lax.axis_size("chan")
-    pairs = lax.axis_size("stn") // 2
+def last_kernel(*refs):
+    parts, out_ref = refs[:-1], refs[-1]
+    n_chan = len(parts)
     own_beams, rows_c, total_chans = out_ref.shape
     channels = total_chans // n_chan
     width = channels * rows_c
-    parts = parts_ref[...].astype(jnp.float32).reshape(pairs, n_chan, own_beams, width)
-    tied = jnp.sum(parts, axis=0)
     diagonal = iota((channels, width), 0) == iota((channels, width), 1) // rows_c
     spread = (iota((rows_c, width), 0) == iota((rows_c, width), 1) % rows_c).astype(jnp.bfloat16)
+    values = [part[...].astype(jnp.float32).reshape(own_beams, width) for part in parts]
+    own_chan = lax.axis_index("chan")
     for b in range(own_beams):
-        rows = [jnp.where(diagonal, tied[chan, b : b + 1], 0.0) for chan in range(n_chan)]
+        rows = []
+        for chan in range(n_chan):
+            row = values[0][b : b + 1]
+            for offset in range(1, n_chan):
+                row = jnp.where(own_chan ^ offset == chan, values[offset][b : b + 1], row)
+            rows.append(jnp.where(diagonal, row, 0.0))
         rows = jnp.concatenate(rows, axis=0).astype(jnp.bfloat16)
         out_ref[b] = dot_nt(spread, rows).astype(jnp.bfloat16)
 
@@ -263,21 +272,28 @@
     )(*operands)
     axes = ("stn", "chan")
     flat = range(n_stn * n_chan)
-    received = lax.ppermute(send, axes, [(d, d ^ n_chan) for d in flat])
-    pair_sum = (keep.astype(jnp.float32) + received.astype(jnp.float32)).astype(jnp.bfloat16)
-    groups = [[d for d in flat if d // n_chan % 2 == low] for low in range(2)]
-    parts = lax.all_to_all(
-        pair_sum, axes, split_axis=0, concat_axis=0, axis_index_groups=groups, tiled=True
-    )
+    bit = n_chan
+    while True:
+        received = lax.ppermute(send, axes, [(d, d ^ bit) for d in flat])
+        keep = (keep.astype(jnp.float32) + received.astype(jnp.float32)).astype(jnp.bfloat16)
+        bit *= 2
+        if bit == n_stn * n_chan:
+            break
+        half = keep.shape[0] // 2
+        keep, send = keep[:half], keep[half:]
+    parts = [keep[:1]]
+    for offset in range(1, n_chan):
+        perm = [(d, d ^ offset) for d in flat]
+        parts.append(lax.ppermute(keep[offset : offset + 1], axes, perm))
     vmem = pl.BlockSpec(memory_space=pltpu.VMEM)
     tied = pl.pallas_call(
         last_kernel,
         out_shape=jax.ShapeDtypeStruct((rows, 2 * samples, n_chan * channels), jnp.bfloat16),
-        in_specs=[vmem],
+        in_specs=[vmem] * n_chan,
         out_specs=vmem,
         compiler_params=pltpu.CompilerParams(vmem_limit_bytes=16 * 2**20),
         name="tied_beams",
-    )(parts)
+    )(*parts)
     return tied.transpose(0, 2, 1)
 
 

time: 21.6 us -> 23.2 us (1.074)
  blocking collectives: 15.5 us -> 0 us
  starting transfers between devices: 0.52 us -> 10.6 us
  waiting for transfers between devices: 0.88 us -> 7.74 us
    all_to_all x1 -> x0, blocking collectives: 15.5 us -> none  [shards(): lax.all_to_all(pair_sum, axes, split_axis=0, concat_axis=0, axis_index_gr...]
    ppermute x1 -> x5, starting transfers between devices: 0.52 us -> 10.6 us  [the longest x4 8.68 us: shards(): received = lax.ppermute(send, axes, [(d, d ^ bit) for d in flat])]
    ppermute x1 -> x5, waiting for transfers between devices: 0.88 us -> 7.74 us  [the longest x4 5.97 us: shards(): received = lax.ppermute(send, axes, [(d, d ^ bit) for d in flat])]
  transfers between devices with their start and end apart: 1 -> 5, of which waited for: 1 -> 5; matrix products, arithmetic and copies ran while one was open for 0% -> 0% of each run, Pallas kernels for 0% -> 0%
where the time goes in v8:
time: 23.2 us; the launch traced here: 23 us
  starting transfers between devices  10.6 us (46%)
  waiting for transfers between devices  7.74 us (33%)
  Pallas kernels  4.49 us (19%)
    ppermute x4, starting transfers between devices, shards(): received = lax.ppermute(send, axes, [(d, d ^ bit) for d in flat])  8.68 us
    ppermute x4, waiting for transfers between devices, shards(): received = lax.ppermute(send, axes, [(d, d ^ bit) for d in flat])  5.97 us
    pallas_call x1, Pallas kernels, shards(): pl.pallas_call(kernel, out_shape=[pltpu.VMEM((n_stn // 2 * n_chan, rows,...  3.7 us
    ppermute x1, starting transfers between devices, shards(): parts.append(lax.ppermute(keep[offset:offset + 1], axes, perm))  1.89 us
    ppermute x1, waiting for transfers between devices, shards(): parts.append(lax.ppermute(keep[offset:offset + 1], axes, perm))  1.77 us
    pallas_call x1, Pallas kernels, shards(): pl.pallas_call(last_kernel, out_shape=jax.ShapeDtypeStruct((rows, 2 * sam...  0.79 us
  transfers between devices with their start and end apart: 5, of which 5 were waited for; matrix products, arithmetic and copies ran while one was open for 0% of the time, Pallas kernels for 0%

profile of v8, /device:TPU:0, one launch (start us, length us, event | category | flops | bytes accessed | tf_op | source)
XLA Modules:
  0.0 23.0 jit_solution(12862732507974540032)
XLA Ops:
  0.0 3.7 %partial_tied.1 = (bf16[16,2,768]{2,1,0:T(2,128)(2,1)S(1)}, bf16[16,2,768]{2,1,0:T(2,128)(2,1)S(1)}) custom-call(bf16[24,2,16,2048]{3,2,1,0:T(8,128)(2,1)} %volt_hbm.1, bf16[24,2,2048]{2,1,0:T(2,128)(2,1)} %aw_hbm.1, bf16[24,2,128]{2,1,0:T(2,128)(2,1)} %sw_hbm.1, s32[1,128]{1,0:T(1,128)} %bitcast.8, s32[1,128]{1,0:T(1,128)} %bitcast.9, f32[2,128]{1,0:T(2,128)} %bitcast.6, ...), custom_call_target="tpu_custom_call" | custom-call | tf_op jit(solution)/shard_map/partial_tied/pallas_call | solution.py:259
  3.7 0.5 %collective-permute-start = (bf16[16,2,768]{2,1,0:T(2,128)(2,1)S(1)}, bf16[16,2,768]{2,1,0:T(2,128)(2,1)S(1)}, u32[]{:S(2)}, u32[]{:S(2)}) collective-permute-start(bf16[16,2,768]{2,1,0:T(2,128)(2,1)S(1)} %get-tuple-element.8), channel_id=1, source_target_pairs={{0,2},{1,3},{2,0},{3,1},{4,6},{5,7},{6,4},{7,5},{8,10},{9,11},{10,... | collective-permute-start | bytes 147464 | tf_op jit(solution)/shard_map/ppermute | solution.py:277
  4.2 0.9 %collective-permute-done = bf16[16,2,768]{2,1,0:T(2,128)(2,1)S(1)} collective-permute-done((bf16[16,2,768]{2,1,0:T(2,128)(2,1)S(1)}, bf16[16,2,768]{2,1,0:T(2,128)(2,1)S(1)}, u32[]{:S(2)}, u32[]{:S(2)}) %collective-permute-start) | collective-permute-done | bytes 49184 | tf_op jit(solution)/shard_map/ppermute | solution.py:277
  5.1 0.1 add_convert_fusion
  5.2 2.9 %collective-permute-start.1 = (bf16[8,2,768]{2,1,0:T(2,128)(2,1)S(1)}, bf16[8,2,768]{2,1,0:T(2,128)(2,1)S(1)}, u32[]{:S(2)}, u32[]{:S(2)}) collective-permute-start(bf16[8,2,768]{2,1,0:T(2,128)(2,1)S(1)} %slice.33), channel_id=1, source_target_pairs={{0,4},{1,5},{2,6},{3,7},{4,0},{5,1},{6,2},{7,3},{8,12},{9,13},{10,... | collective-permute-start | bytes 73736 | tf_op jit(solution)/shard_map/ppermute | solution.py:277
  8.1 1.8 %collective-permute-done.1 = bf16[8,2,768]{2,1,0:T(2,128)(2,1)S(1)} collective-permute-done((bf16[8,2,768]{2,1,0:T(2,128)(2,1)S(1)}, bf16[8,2,768]{2,1,0:T(2,128)(2,1)S(1)}, u32[]{:S(2)}, u32[]{:S(2)}) %collective-permute-start.1) | collective-permute-done | bytes 24608 | tf_op jit(solution)/shard_map/ppermute | solution.py:277
  10.0 2.1 %collective-permute-start.2 = (bf16[4,2,768]{2,1,0:T(2,128)(2,1)S(1)}, bf16[4,2,768]{2,1,0:T(2,128)(2,1)S(1)}, u32[]{:S(2)}, u32[]{:S(2)}) collective-permute-start(bf16[4,2,768]{2,1,0:T(2,128)(2,1)S(1)} %slice.35), channel_id=1, source_target_pairs={{0,8},{1,9},{2,10},{3,11},{4,12},{5,13},{6,14},{7,15},{8,0},{9,1},... | collective-permute-start | bytes 36872 | tf_op jit(solution)/shard_map/ppermute | solution.py:277
  12.1 1.7 %collective-permute-done.2 = bf16[4,2,768]{2,1,0:T(2,128)(2,1)S(1)} collective-permute-done((bf16[4,2,768]{2,1,0:T(2,128)(2,1)S(1)}, bf16[4,2,768]{2,1,0:T(2,128)(2,1)S(1)}, u32[]{:S(2)}, u32[]{:S(2)}) %collective-permute-start.2) | collective-permute-done | bytes 12320 | tf_op jit(solution)/shard_map/ppermute | solution.py:277
  13.8 3.1 %collective-permute-start.3 = (bf16[2,2,768]{2,1,0:T(2,128)(2,1)S(1)}, bf16[2,2,768]{2,1,0:T(2,128)(2,1)S(1)}, u32[]{:S(2)}, u32[]{:S(2)}) collective-permute-start(bf16[2,2,768]{2,1,0:T(2,128)(2,1)S(1)} %slice.37), channel_id=1, source_target_pairs={{0,16},{1,17},{2,18},{3,19},{4,20},{5,21},{6,22},{7,23},{8,24},{9,... | collective-permute-start | bytes 18440 | tf_op jit(solution)/shard_map/ppermute | solution.py:277
  16.9 1.6 %collective-permute-done.3 = bf16[2,2,768]{2,1,0:T(2,128)(2,1)S(1)} collective-permute-done((bf16[2,2,768]{2,1,0:T(2,128)(2,1)S(1)}, bf16[2,2,768]{2,1,0:T(2,128)(2,1)S(1)}, u32[]{:S(2)}, u32[]{:S(2)}) %collective-permute-start.3) | collective-permute-done | bytes 6176 | tf_op jit(solution)/shard_map/ppermute | solution.py:277
  18.6 1.9 %collective-permute-start.4 = (bf16[1,2,768]{2,1,0:T(2,128)(2,1)S(1)}, bf16[1,2,768]{2,1,0:T(2,128)(2,1)S(1)}, u32[]{:S(2)}, u32[]{:S(2)}) collective-permute-start(bf16[1,2,768]{2,1,0:T(2,128)(2,1)S(1)} %get-tuple-element.9), channel_id=1, source_target_pairs={{0,1},{1,0},{2,3},{3,2},{4,5},{5,4},{6,7},{7,6},{8,9},{9,8},{10,11... | collective-permute-start | bytes 9224 | tf_op jit(solution)/shard_map/ppermute | solution.py:287
  20.5 1.8 %collective-permute-done.4.refs_1_ = bf16[1,2,768]{2,1,0:T(2,128)(2,1)S(1)} collective-permute-done((bf16[1,2,768]{2,1,0:T(2,128)(2,1)S(1)}, bf16[1,2,768]{2,1,0:T(2,128)(2,1)S(1)}, u32[]{:S(2)}, u32[]{:S(2)}) %collective-permute-start.4) | collective-permute-done | bytes 3104 | tf_op jit(solution)/shard_map/ppermute | solution.py:287
  22.2 0.8 %tied_beams.1 = bf16[2,32,48]{2,1,0:T(8,128)(2,1)} custom-call(bf16[1,2,768]{2,1,0:T(2,128)(2,1)S(1)} %get-tuple-element.10.refs_0_, bf16[1,2,768]{2,1,0:T(2,128)(2,1)S(1)} %collective-permute-done.4.refs_1_), custom_call_target="tpu_custom_call" | custom-call | tf_op jit(solution)/shard_map/tied_beams/pallas_call | solution.py:289
  (7 shorter events, 0.1 us)
Async XLA Ops:
  3.7 1.4 %collective-permute-start = (bf16[16,2,768]{2,1,0:T(2,128)(2,1)S(1)}, bf16[16,2,768]{2,1,0:T(2,128)(2,1)S(1)}, u32[]{:S(2)}, u32[]{:S(2)}) collective-permute-start(bf16[16,2,768]{2,1,0:T(2,128)(2,1)S(1)} %get-tuple-element.8), channel_id=1, source_target_pairs={{0,2},{1,3},{2,0},{3,1},{4,6},{5,7},{6,4},{7,5},{8,10},{9,11},{10,... | collective-permute-start | bytes 147464 | tf_op jit(solution)/shard_map/ppermute | solution.py:277
  5.2 4.7 %collective-permute-start.1 = (bf16[8,2,768]{2,1,0:T(2,128)(2,1)S(1)}, bf16[8,2,768]{2,1,0:T(2,128)(2,1)S(1)}, u32[]{:S(2)}, u32[]{:S(2)}) collective-permute-start(bf16[8,2,768]{2,1,0:T(2,128)(2,1)S(1)} %slice.33), channel_id=1, source_target_pairs={{0,4},{1,5},{2,6},{3,7},{4,0},{5,1},{6,2},{7,3},{8,12},{9,13},{10,... | collective-permute-start | bytes 73736 | tf_op jit(solution)/shard_map/ppermute | solution.py:277
  10.0 3.8 %collective-permute-start.2 = (bf16[4,2,768]{2,1,0:T(2,128)(2,1)S(1)}, bf16[4,2,768]{2,1,0:T(2,128)(2,1)S(1)}, u32[]{:S(2)}, u32[]{:S(2)}) collective-permute-start(bf16[4,2,768]{2,1,0:T(2,128)(2,1)S(1)} %slice.35), channel_id=1, source_target_pairs={{0,8},{1,9},{2,10},{3,11},{4,12},{5,13},{6,14},{7,15},{8,0},{9,1},... | collective-permute-start | bytes 36872 | tf_op jit(solution)/shard_map/ppermute | solution.py:277
  13.8 4.7 %collective-permute-start.3 = (bf16[2,2,768]{2,1,0:T(2,128)(2,1)S(1)}, bf16[2,2,768]{2,1,0:T(2,128)(2,1)S(1)}, u32[]{:S(2)}, u32[]{:S(2)}) collective-permute-start(bf16[2,2,768]{2,1,0:T(2,128)(2,1)S(1)} %slice.37), channel_id=1, source_target_pairs={{0,16},{1,17},{2,18},{3,19},{4,20},{5,21},{6,22},{7,23},{8,24},{9,... | collective-permute-start | bytes 18440 | tf_op jit(solution)/shard_map/ppermute | solution.py:277
  18.6 3.7 %collective-permute-start.4 = (bf16[1,2,768]{2,1,0:T(2,128)(2,1)S(1)}, bf16[1,2,768]{2,1,0:T(2,128)(2,1)S(1)}, u32[]{:S(2)}, u32[]{:S(2)}) collective-permute-start(bf16[1,2,768]{2,1,0:T(2,128)(2,1)S(1)} %get-tuple-element.9), channel_id=1, source_target_pairs={{0,1},{1,0},{2,3},{3,2},{4,5},{5,4},{6,7},{7,6},{8,9},{9,8},{10,11... | collective-permute-start | bytes 9224 | tf_op jit(solution)/shard_map/ppermute | solution.py:287

commit v9 on v6

--- a/solution.py
+++ b/solution.py
@@ -11,6 +11,7 @@
 TILE_ANTENNAS = 16
 TPS = 16
 GROUPS = 4
+LANES = 128
 CB = 8
 NT = (((1,), (1,)), ((), ()))
 SIN = [(-1) ** i * (2 * math.pi) ** (2 * i + 1) / math.factorial(2 * i + 1) for i in range(7)]
@@ -58,6 +59,18 @@
     for coefficient in SIN[-2::-1]:
         value = value * z2 + coefficient
     return value * z
+
+
+def fold(x):
+    half = x.shape[1] // 2
+    low = iota((x.shape[0], LANES), 1) % TILE_ANTENNAS < TILE_ANTENNAS // 2
+    out = []
+    for start in range(0, half, LANES):
+        a, b = x[:, start : start + LANES], x[:, half + start : half + start + LANES]
+        a = a + pltpu.roll(a, LANES - TILE_ANTENNAS // 2, 1)
+        b = b + pltpu.roll(b, TILE_ANTENNAS // 2, 1)
+        out.append(jnp.where(low, a, b))
+    return jnp.concatenate(out, axis=1)
 
 
 def kernel(
@@ -146,8 +159,9 @@
 
         lax.fori_loop(0, beams // block, body, 0)
 
-    antenna_tile = iota((antennas, tiles), 0) // TILE_ANTENNAS == iota((antennas, tiles), 1)
-    sum_ref[...] = antenna_tile.astype(jnp.bfloat16)
+    row, tile = iota(sum_ref.shape, 0), iota(sum_ref.shape, 1)
+    right_half = row // (TILE_ANTENNAS // 2) % 2 * (tiles // 2)
+    sum_ref[...] = (row // TILE_ANTENNAS + right_half == tile).astype(jnp.bfloat16)
     for copy in small[4:]:
         copy.wait()
     member_table = (iota((stations, tiles), 0) == ts_ref[...] % stations).astype(jnp.float32)
@@ -167,6 +181,7 @@
             v_re, v_im = volts[channel0 + c, 0], volts[channel0 + c, 1]
             products.append(w_re * v_re - w_im * v_im)
             products.append(w_re * v_im + w_im * v_re)
+        products = [fold(x) for x in products]
         beams_tile = jnp.dot(
             jnp.concatenate(products, axis=0), sum_ref[...], preferred_element_type=jnp.float32
         ).astype(jnp.bfloat16)
@@ -246,7 +261,7 @@
         scratch_shapes=[pltpu.VMEM(x.shape, x.dtype) for x in operands]
         + [
             pltpu.VMEM((beams, channels * 2 * (station_weights.shape[2] // TPS)), jnp.bfloat16),
-            pltpu.VMEM((volts.shape[3], station_weights.shape[2]), jnp.bfloat16),
+            pltpu.VMEM((volts.shape[3] // 2, station_weights.shape[2]), jnp.bfloat16),
             pltpu.SemaphoreType.DMA((len(operands) - 1 + 2 * groups,)),
         ],
         compiler_params=pltpu.CompilerParams(vmem_limit_bytes=24 * 2**20),

time: 19.9 us -> 20.1 us (1.010)
  no operation moved by 1% of the time
where the time goes in v9:
time: 20.1 us; the launch traced here: 19.9 us
  blocking collectives  15.2 us (76%)
  Pallas kernels  4.72 us (23%)
    all_to_all x1, blocking collectives, shards(): lax.all_to_all(partial, ('stn', 'chan'), split_axis=0, concat_axis=0, til...  15.2 us
    pallas_call x1, Pallas kernels, shards(): pl.pallas_call(kernel, out_shape=pltpu.VMEM((n_stn * n_chan, rows, width)...  3.85 us
    pallas_call x1, Pallas kernels, shards(): pl.pallas_call(last_kernel, out_shape=jax.ShapeDtypeStruct((rows, 2 * sam...  0.86 us

profile of v9, /device:TPU:0, one launch (start us, length us, event | category | flops | bytes accessed | tf_op | source)
XLA Modules:
  0.0 19.9 jit_solution(16919223937780318521)
XLA Ops:
  0.0 3.9 %partial_tied.1 = bf16[32,2,768]{2,1,0:T(2,128)(2,1)S(1)} custom-call(bf16[24,2,16,2048]{3,2,1,0:T(8,128)(2,1)} %volt_hbm.1, bf16[24,2,2048]{2,1,0:T(2,128)(2,1)} %aw_hbm.1, bf16[24,2,128]{2,1,0:T(2,128)(2,1)} %sw_hbm.1, s32[1,128]{1,0:T(1,128)} %bitcast.8, s32[1,128]{1,0:T(1,128)} %bitcast.9, f32[2,128]{1,0:T(2,128)} %bitcast.6, f32[2,64]{1,0:T(2,128)} %bitcast.7, ...), custom_call_target="tpu_custom_call" | custom-call | tf_op jit(solution)/shard_map/partial_tied/pallas_call | solution.py:256
  3.9 15.2 %all_to_all.5.parts_ref = bf16[32,2,768]{2,1,0:T(2,128)(2,1)S(1)} all-to-all(bf16[32,2,768]{2,1,0:T(2,128)(2,1)S(1)} %partial_tied.1), channel_id=1, replica_groups=mesh['stn'=16,'chan'=2] {'stn','chan'}, dimensions={0} | all-to-all | bytes 196608 | tf_op jit(solution)/shard_map/all_to_all | solution.py:270
  19.1 0.9 %tied_beams.1 = bf16[2,32,48]{2,1,0:T(8,128)(2,1)} custom-call(bf16[32,2,768]{2,1,0:T(2,128)(2,1)S(1)} %all_to_all.5.parts_ref), custom_call_target="tpu_custom_call" | custom-call | tf_op jit(solution)/shard_map/tied_beams/pallas_call | solution.py:272

commit v10 on v6

--- a/solution.py
+++ b/solution.py
@@ -114,6 +114,8 @@
     for k in range(2 * groups):
         part = pl.ds(k * CB // 2, CB // 2)
         large.append(start(volt_hbm.at[part], volts.at[part], len(small) + k))
+    antenna_tile = iota((antennas, tiles), 0) // TILE_ANTENNAS == iota((antennas, tiles), 1)
+    sum_ref[...] = antenna_tile.astype(jnp.bfloat16)
     for copy in small[:4]:
         copy.wait()
 
@@ -146,8 +148,6 @@
 
         lax.fori_loop(0, beams // block, body, 0)
 
-    antenna_tile = iota((antennas, tiles), 0) // TILE_ANTENNAS == iota((antennas, tiles), 1)
-    sum_ref[...] = antenna_tile.astype(jnp.bfloat16)
     for copy in small[4:]:
         copy.wait()
     member_table = (iota((stations, tiles), 0) == ts_ref[...] % stations).astype(jnp.float32)
@@ -155,45 +155,56 @@
         (lanes, CB * rows_c), 1
     ) // rows_c
 
+    station_rows_of = []
     for g in range(groups):
-        channel0 = g * CB
-        weights = aw_ref[channel0 : channel0 + CB].astype(jnp.float32)
-        large[2 * g].wait()
-        large[2 * g + 1].wait()
+        swt = sw_ref[g * CB : (g + 1) * CB].astype(jnp.float32)
+        right = []
+        for c in range(CB):
+            re = swt[c, 0:1] * member_table
+            im = swt[c, 1:2] * member_table
+            right.append(jnp.concatenate([re, -im], axis=1))
+            right.append(jnp.concatenate([im, re], axis=1))
+        station_rows_of.append(jnp.concatenate(right, axis=0).astype(jnp.bfloat16))
+
+    def tile_beams(g):
         products = []
+        weights = aw_ref[g * CB : (g + 1) * CB].astype(jnp.float32)
         for c in range(CB):
             w_re = jnp.broadcast_to(weights[c, 0:1], (samples, antennas)).astype(jnp.bfloat16)
             w_im = jnp.broadcast_to(weights[c, 1:2], (samples, antennas)).astype(jnp.bfloat16)
-            v_re, v_im = volts[channel0 + c, 0], volts[channel0 + c, 1]
+            v_re, v_im = volts[g * CB + c, 0], volts[g * CB + c, 1]
             products.append(w_re * v_re - w_im * v_im)
             products.append(w_re * v_im + w_im * v_re)
-        beams_tile = jnp.dot(
+        return jnp.dot(
             jnp.concatenate(products, axis=0), sum_ref[...], preferred_element_type=jnp.float32
         ).astype(jnp.bfloat16)
+
+    def tied_beams(g, beams_tile):
         left = []
         for c in range(CB):
             tile_re = beams_tile[c * rows_c : c * rows_c + samples]
             tile_im = beams_tile[c * rows_c + samples : (c + 1) * rows_c]
             left.append(jnp.concatenate([tile_re, tile_im], axis=1))
             left.append(jnp.concatenate([tile_im, -tile_re], axis=1))
-        right = []
-        swt = sw_ref[channel0 : channel0 + CB].astype(jnp.float32)
-        for c in range(CB):
-            re = swt[c, 0:1] * member_table
-            im = swt[c, 1:2] * member_table
-            right.append(jnp.concatenate([re, -im], axis=1))
-            right.append(jnp.concatenate([im, re], axis=1))
-        station = dot_nt(
-            jnp.concatenate(right, axis=0).astype(jnp.bfloat16), jnp.concatenate(left, axis=0)
-        )
+        station = dot_nt(station_rows_of[g], jnp.concatenate(left, axis=0))
         station = jnp.where(own_channel, station, 0.0).astype(jnp.bfloat16)
         tied = jnp.dot(
             tied_ref[:, g * lanes : (g + 1) * lanes], station, preferred_element_type=jnp.float32
         )
         devices, rows, _ = out_ref.shape
-        out_ref[:, :, channel0 * rows_c : (channel0 + CB) * rows_c] = tied.astype(
-            jnp.bfloat16
-        ).reshape(devices, rows, CB * rows_c)
+        out_ref[:, :, g * CB * rows_c : (g + 1) * CB * rows_c] = tied.astype(jnp.bfloat16).reshape(
+            devices, rows, CB * rows_c
+        )
+
+    last = None
+    for g in range(groups):
+        large[2 * g].wait()
+        large[2 * g + 1].wait()
+        now = tile_beams(g)
+        if last is not None:
+            tied_beams(g - 1, last)
+        last = now
+    tied_beams(groups - 1, last)
 
 
 def last_kernel(parts_ref, out_ref):

time: 19.9 us -> 19.5 us (0.980)
  Pallas kernels: 4.56 us -> 4.15 us
    pallas_call x1, Pallas kernels: 3.7 us -> 3.29 us  [shards(): pl.pallas_call(kernel, out_shape=pltpu.VMEM((n_stn * n_chan, rows, width)...]
where the time goes in v10:
time: 19.5 us; the launch traced here: 19.4 us
  blocking collectives  15.2 us (78%)
  Pallas kernels  4.15 us (21%)
    all_to_all x1, blocking collectives, shards(): lax.all_to_all(partial, ('stn', 'chan'), split_axis=0, concat_axis=0, til...  15.2 us
    pallas_call x1, Pallas kernels, shards(): pl.pallas_call(kernel, out_shape=pltpu.VMEM((n_stn * n_chan, rows, width)...  3.29 us
    pallas_call x1, Pallas kernels, shards(): pl.pallas_call(last_kernel, out_shape=jax.ShapeDtypeStruct((rows, 2 * sam...  0.86 us

profile of v10, /device:TPU:0, one launch (start us, length us, event | category | flops | bytes accessed | tf_op | source)
XLA Modules:
  0.0 19.4 jit_solution(11006561063420436367)
XLA Ops:
  0.0 3.3 %partial_tied.1 = bf16[32,2,768]{2,1,0:T(2,128)(2,1)S(1)} custom-call(bf16[24,2,16,2048]{3,2,1,0:T(8,128)(2,1)} %volt_hbm.1, bf16[24,2,2048]{2,1,0:T(2,128)(2,1)} %aw_hbm.1, bf16[24,2,128]{2,1,0:T(2,128)(2,1)} %sw_hbm.1, s32[1,128]{1,0:T(1,128)} %bitcast.8, s32[1,128]{1,0:T(1,128)} %bitcast.9, f32[2,128]{1,0:T(2,128)} %bitcast.6, f32[2,64]{1,0:T(2,128)} %bitcast.7, ...), custom_call_target="tpu_custom_call" | custom-call | tf_op jit(solution)/shard_map/partial_tied/pallas_call | solution.py:252
  3.3 15.2 %all_to_all.5.parts_ref = bf16[32,2,768]{2,1,0:T(2,128)(2,1)S(1)} all-to-all(bf16[32,2,768]{2,1,0:T(2,128)(2,1)S(1)} %partial_tied.1), channel_id=1, replica_groups=mesh['stn'=16,'chan'=2] {'stn','chan'}, dimensions={0} | all-to-all | bytes 196608 | tf_op jit(solution)/shard_map/all_to_all | solution.py:266
  18.5 0.9 %tied_beams.1 = bf16[2,32,48]{2,1,0:T(8,128)(2,1)} custom-call(bf16[32,2,768]{2,1,0:T(2,128)(2,1)S(1)} %all_to_all.5.parts_ref), custom_call_target="tpu_custom_call" | custom-call | tf_op jit(solution)/shard_map/tied_beams/pallas_call | solution.py:268

commit v11 on v10

--- a/solution.py
+++ b/solution.py
@@ -116,55 +116,8 @@
         large.append(start(volt_hbm.at[part], volts.at[part], len(small) + k))
     antenna_tile = iota((antennas, tiles), 0) // TILE_ANTENNAS == iota((antennas, tiles), 1)
     sum_ref[...] = antenna_tile.astype(jnp.bfloat16)
-    for copy in small[:4]:
+    for copy in small + large[:2]:
         copy.wait()
-
-    east_s, north_s, group_s = station_rows(pos_ref, group_ref, stations, lanes)
-    lane = iota((1, lanes), 1)
-    channel_lane = lane // (2 * stations)
-    quarter = 0.25 * ((lane // stations) % 2).astype(jnp.float32)
-    first_chan = lax.axis_index("chan") * channels
-    total_chans = channels * lax.axis_size("chan")
-    block = min(64, beams)
-
-    def tied_rows(first):
-        east, north, group = beam_columns(order_ref, dir_ref, first, block)
-        delay = east * east_s + north * north_s
-        member = jnp.where(group == group_s, scale, 0.0)
-        for g in range(groups):
-            freq = 1.0 + (first_chan + g * CB + channel_lane).astype(jnp.float32) / total_chans
-            wave = cos_turns(delay * freq - quarter)
-            tied_ref[pl.ds(first, block), g * lanes : (g + 1) * lanes] = (wave * member).astype(
-                jnp.bfloat16
-            )
-
-    if beams == block:
-        tied_rows(0)
-    else:
-
-        def body(i, carry):
-            tied_rows(pl.multiple_of(i * block, block))
-            return carry
-
-        lax.fori_loop(0, beams // block, body, 0)
-
-    for copy in small[4:]:
-        copy.wait()
-    member_table = (iota((stations, tiles), 0) == ts_ref[...] % stations).astype(jnp.float32)
-    own_channel = iota((lanes, CB * rows_c), 0) // (2 * stations) == iota(
-        (lanes, CB * rows_c), 1
-    ) // rows_c
-
-    station_rows_of = []
-    for g in range(groups):
-        swt = sw_ref[g * CB : (g + 1) * CB].astype(jnp.float32)
-        right = []
-        for c in range(CB):
-            re = swt[c, 0:1] * member_table
-            im = swt[c, 1:2] * member_table
-            right.append(jnp.concatenate([re, -im], axis=1))
-            right.append(jnp.concatenate([im, re], axis=1))
-        station_rows_of.append(jnp.concatenate(right, axis=0).astype(jnp.bfloat16))
 
     def tile_beams(g):
         products = []
@@ -178,6 +131,53 @@
         return jnp.dot(
             jnp.concatenate(products, axis=0), sum_ref[...], preferred_element_type=jnp.float32
         ).astype(jnp.bfloat16)
+
+    last = tile_beams(0)
+
+    east_s, north_s, group_s = station_rows(pos_ref, group_ref, stations, lanes)
+    lane = iota((1, lanes), 1)
+    channel_lane = lane // (2 * stations)
+    quarter = 0.25 * ((lane // stations) % 2).astype(jnp.float32)
+    first_chan = lax.axis_index("chan") * channels
+    total_chans = channels * lax.axis_size("chan")
+    block = min(64, beams)
+
+    def tied_rows(first):
+        east, north, group = beam_columns(order_ref, dir_ref, first, block)
+        delay = east * east_s + north * north_s
+        member = jnp.where(group == group_s, scale, 0.0)
+        for g in range(groups):
+            freq = 1.0 + (first_chan + g * CB + channel_lane).astype(jnp.float32) / total_chans
+            wave = cos_turns(delay * freq - quarter)
+            tied_ref[pl.ds(first, block), g * lanes : (g + 1) * lanes] = (wave * member).astype(
+                jnp.bfloat16
+            )
+
+    if beams == block:
+        tied_rows(0)
+    else:
+
+        def body(i, carry):
+            tied_rows(pl.multiple_of(i * block, block))
+            return carry
+
+        lax.fori_loop(0, beams // block, body, 0)
+
+    member_table = (iota((stations, tiles), 0) == ts_ref[...] % stations).astype(jnp.float32)
+    own_channel = iota((lanes, CB * rows_c), 0) // (2 * stations) == iota(
+        (lanes, CB * rows_c), 1
+    ) // rows_c
+
+    station_rows_of = []
+    for g in range(groups):
+        swt = sw_ref[g * CB : (g + 1) * CB].astype(jnp.float32)
+        right = []
+        for c in range(CB):
+            re = swt[c, 0:1] * member_table
+            im = swt[c, 1:2] * member_table
+            right.append(jnp.concatenate([re, -im], axis=1))
+            right.append(jnp.concatenate([im, re], axis=1))
+        station_rows_of.append(jnp.concatenate(right, axis=0).astype(jnp.bfloat16))
 
     def tied_beams(g, beams_tile):
         left = []
@@ -196,13 +196,11 @@
             devices, rows, CB * rows_c
         )
 
-    last = None
-    for g in range(groups):
+    for g in range(1, groups):
         large[2 * g].wait()
         large[2 * g + 1].wait()
         now = tile_beams(g)
-        if last is not None:
-            tied_beams(g - 1, last)
+        tied_beams(g - 1, last)
         last = now
     tied_beams(groups - 1, last)
 

time: 19.5 us -> 19.7 us (1.010)
  no operation moved by 1% of the time
where the time goes in v11:
time: 19.7 us; the launch traced here: 19.5 us
  blocking collectives  15.2 us (77%)
  Pallas kernels  4.27 us (22%)
    all_to_all x1, blocking collectives, shards(): lax.all_to_all(partial, ('stn', 'chan'), split_axis=0, concat_axis=0, til...  15.2 us
    pallas_call x1, Pallas kernels, shards(): pl.pallas_call(kernel, out_shape=pltpu.VMEM((n_stn * n_chan, rows, width)...  3.41 us
    pallas_call x1, Pallas kernels, shards(): pl.pallas_call(last_kernel, out_shape=jax.ShapeDtypeStruct((rows, 2 * sam...  0.86 us

profile of v11, /device:TPU:0, one launch (start us, length us, event | category | flops | bytes accessed | tf_op | source)
XLA Modules:
  0.0 19.5 jit_solution(5609386705299665770)
XLA Ops:
  0.0 3.4 %partial_tied.1 = bf16[32,2,768]{2,1,0:T(2,128)(2,1)S(1)} custom-call(bf16[24,2,16,2048]{3,2,1,0:T(8,128)(2,1)} %volt_hbm.1, bf16[24,2,2048]{2,1,0:T(2,128)(2,1)} %aw_hbm.1, bf16[24,2,128]{2,1,0:T(2,128)(2,1)} %sw_hbm.1, s32[1,128]{1,0:T(1,128)} %bitcast.8, s32[1,128]{1,0:T(1,128)} %bitcast.9, f32[2,128]{1,0:T(2,128)} %bitcast.6, f32[2,64]{1,0:T(2,128)} %bitcast.7, ...), custom_call_target="tpu_custom_call" | custom-call | tf_op jit(solution)/shard_map/partial_tied/pallas_call | solution.py:250
  3.4 15.2 %all_to_all.5.parts_ref = bf16[32,2,768]{2,1,0:T(2,128)(2,1)S(1)} all-to-all(bf16[32,2,768]{2,1,0:T(2,128)(2,1)S(1)} %partial_tied.1), channel_id=1, replica_groups=mesh['stn'=16,'chan'=2] {'stn','chan'}, dimensions={0} | all-to-all | bytes 196608 | tf_op jit(solution)/shard_map/all_to_all | solution.py:264
  18.6 0.9 %tied_beams.1 = bf16[2,32,48]{2,1,0:T(8,128)(2,1)} custom-call(bf16[32,2,768]{2,1,0:T(2,128)(2,1)S(1)} %all_to_all.5.parts_ref), custom_call_target="tpu_custom_call" | custom-call | tf_op jit(solution)/shard_map/tied_beams/pallas_call | solution.py:266

commit v12 on v10

--- a/solution.py
+++ b/solution.py
@@ -26,9 +26,11 @@
 
 def beam_columns(order_ref, dir_ref, start, rows):
     beams = order_ref.shape[1]
+    each = beams // (lax.axis_size("stn") * lax.axis_size("chan"))
     order = order_ref[...].astype(jnp.float32)
     lane = iota((rows, beams), 1)
-    own = lane == iota((rows, beams), 0) + start
+    slot = iota((rows, beams), 0) + start
+    own = lane == beams - each - slot // each * each + slot % each
     ids = jnp.sum(jnp.where(own, order, 0.0), axis=1, keepdims=True)
     pick = lane.astype(jnp.float32) == ids
     east = jnp.sum(jnp.where(pick, dir_ref[0:1, :], 0.0), axis=1, keepdims=True)
@@ -217,7 +219,7 @@
     diagonal = iota((channels, width), 0) == iota((channels, width), 1) // rows_c
     spread = (iota((rows_c, width), 0) == iota((rows_c, width), 1) % rows_c).astype(jnp.bfloat16)
     for b in range(own_beams):
-        rows = [jnp.where(diagonal, tied[chan, b : b + 1], 0.0) for chan in range(n_chan)]
+        rows = [jnp.where(diagonal, tied[chan, b : b + 1], 0.0) for chan in reversed(range(n_chan))]
         rows = jnp.concatenate(rows, axis=0).astype(jnp.bfloat16)
         out_ref[b] = dot_nt(spread, rows).astype(jnp.bfloat16)
 
@@ -263,7 +265,14 @@
         compiler_params=pltpu.CompilerParams(vmem_limit_bytes=24 * 2**20),
         name="partial_tied",
     )(*operands)
-    parts = lax.all_to_all(partial, ("stn", "chan"), split_axis=0, concat_axis=0, tiled=True)
+    parts = lax.all_to_all(
+        partial,
+        ("stn", "chan"),
+        split_axis=0,
+        concat_axis=0,
+        axis_index_groups=[list(reversed(range(n_stn * n_chan)))],
+        tiled=True,
+    )
     vmem = pl.BlockSpec(memory_space=pltpu.VMEM)
     tied = pl.pallas_call(
         last_kernel,

time: 19.5 us -> 18.8 us (0.964)
  blocking collectives: 15.2 us -> 14.4 us
    all_to_all x1, blocking collectives: 15.2 us -> 14.4 us  [shards(): lax.all_to_all(partial, ('stn', 'chan'), split_axis=0, concat_axis=0, axi...]
where the time goes in v12:
time: 18.8 us; the launch traced here: 18.6 us
  blocking collectives  14.4 us (77%)
  Pallas kernels  4.15 us (22%)
    all_to_all x1, blocking collectives, shards(): lax.all_to_all(partial, ('stn', 'chan'), split_axis=0, concat_axis=0, axi...  14.4 us
    pallas_call x1, Pallas kernels, shards(): pl.pallas_call(kernel, out_shape=pltpu.VMEM((n_stn * n_chan, rows, width)...  3.29 us
    pallas_call x1, Pallas kernels, shards(): pl.pallas_call(last_kernel, out_shape=jax.ShapeDtypeStruct((rows, 2 * sam...  0.86 us

profile of v12, /device:TPU:0, one launch (start us, length us, event | category | flops | bytes accessed | tf_op | source)
XLA Modules:
  0.0 18.6 jit_solution(7121524946844901400)
XLA Ops:
  0.0 3.3 %partial_tied.1 = bf16[32,2,768]{2,1,0:T(2,128)(2,1)S(1)} custom-call(bf16[24,2,16,2048]{3,2,1,0:T(8,128)(2,1)} %volt_hbm.1, bf16[24,2,2048]{2,1,0:T(2,128)(2,1)} %aw_hbm.1, bf16[24,2,128]{2,1,0:T(2,128)(2,1)} %sw_hbm.1, s32[1,128]{1,0:T(1,128)} %bitcast.8, s32[1,128]{1,0:T(1,128)} %bitcast.9, f32[2,128]{1,0:T(2,128)} %bitcast.6, f32[2,64]{1,0:T(2,128)} %bitcast.7, ...), custom_call_target="tpu_custom_call" | custom-call | tf_op jit(solution)/shard_map/partial_tied/pallas_call | solution.py:254
  3.3 14.4 %all_to_all.5.parts_ref = bf16[32,2,768]{2,1,0:T(2,128)(2,1)S(1)} all-to-all(bf16[32,2,768]{2,1,0:T(2,128)(2,1)S(1)} %partial_tied.1), channel_id=1, replica_groups={{31,30,29,28,27,26,25,24,23,22,21,20,19,18,17,16,15,14,13,12,11,10,9,8,..., dimensions={0} | all-to-all | bytes 196608 | tf_op jit(solution)/shard_map/all_to_all | solution.py:268
  17.7 0.9 %tied_beams.1 = bf16[2,32,48]{2,1,0:T(8,128)(2,1)} custom-call(bf16[32,2,768]{2,1,0:T(2,128)(2,1)S(1)} %all_to_all.5.parts_ref), custom_call_target="tpu_custom_call" | custom-call | tf_op jit(solution)/shard_map/tied_beams/pallas_call | solution.py:277

commit v13 on v12

--- a/solution.py
+++ b/solution.py
@@ -12,6 +12,8 @@
 TPS = 16
 GROUPS = 4
 CB = 8
+TB = 4
+COPY = 2
 NT = (((1,), (1,)), ((), ()))
 SIN = [(-1) ** i * (2 * math.pi) ** (2 * i + 1) / math.factorial(2 * i + 1) for i in range(7)]
 
@@ -113,8 +115,8 @@
         )
     ]
     large = []
-    for k in range(2 * groups):
-        part = pl.ds(k * CB // 2, CB // 2)
+    for k in range(channels // COPY):
+        part = pl.ds(k * COPY, COPY)
         large.append(start(volt_hbm.at[part], volts.at[part], len(small) + k))
     antenna_tile = iota((antennas, tiles), 0) // TILE_ANTENNAS == iota((antennas, tiles), 1)
     sum_ref[...] = antenna_tile.astype(jnp.bfloat16)
@@ -153,9 +155,9 @@
     for copy in small[4:]:
         copy.wait()
     member_table = (iota((stations, tiles), 0) == ts_ref[...] % stations).astype(jnp.float32)
-    own_channel = iota((lanes, CB * rows_c), 0) // (2 * stations) == iota(
-        (lanes, CB * rows_c), 1
-    ) // rows_c
+    own_channel = iota((CB * rows_c, lanes), 0) // rows_c == iota((CB * rows_c, lanes), 1) // (
+        2 * stations
+    )
 
     station_rows_of = []
     for g in range(groups):
@@ -166,15 +168,15 @@
             im = swt[c, 1:2] * member_table
             right.append(jnp.concatenate([re, -im], axis=1))
             right.append(jnp.concatenate([im, re], axis=1))
-        station_rows_of.append(jnp.concatenate(right, axis=0).astype(jnp.bfloat16))
-
-    def tile_beams(g):
+        station_rows_of.append(jnp.concatenate(right, axis=0).T.astype(jnp.bfloat16))
+
+    def tile_beams(k):
         products = []
-        weights = aw_ref[g * CB : (g + 1) * CB].astype(jnp.float32)
-        for c in range(CB):
+        weights = aw_ref[k * TB : (k + 1) * TB].astype(jnp.float32)
+        for c in range(TB):
             w_re = jnp.broadcast_to(weights[c, 0:1], (samples, antennas)).astype(jnp.bfloat16)
             w_im = jnp.broadcast_to(weights[c, 1:2], (samples, antennas)).astype(jnp.bfloat16)
-            v_re, v_im = volts[g * CB + c, 0], volts[g * CB + c, 1]
+            v_re, v_im = volts[k * TB + c, 0], volts[k * TB + c, 1]
             products.append(w_re * v_re - w_im * v_im)
             products.append(w_re * v_im + w_im * v_re)
         return jnp.dot(
@@ -188,25 +190,27 @@
             tile_im = beams_tile[c * rows_c + samples : (c + 1) * rows_c]
             left.append(jnp.concatenate([tile_re, tile_im], axis=1))
             left.append(jnp.concatenate([tile_im, -tile_re], axis=1))
-        station = dot_nt(station_rows_of[g], jnp.concatenate(left, axis=0))
+        station = jnp.dot(
+            jnp.concatenate(left, axis=0),
+            station_rows_of[g],
+            preferred_element_type=jnp.float32,
+        )
         station = jnp.where(own_channel, station, 0.0).astype(jnp.bfloat16)
-        tied = jnp.dot(
-            tied_ref[:, g * lanes : (g + 1) * lanes], station, preferred_element_type=jnp.float32
-        )
+        tied = dot_nt(tied_ref[:, g * lanes : (g + 1) * lanes], station)
         devices, rows, _ = out_ref.shape
         out_ref[:, :, g * CB * rows_c : (g + 1) * CB * rows_c] = tied.astype(jnp.bfloat16).reshape(
             devices, rows, CB * rows_c
         )
 
-    last = None
-    for g in range(groups):
-        large[2 * g].wait()
-        large[2 * g + 1].wait()
-        now = tile_beams(g)
-        if last is not None:
-            tied_beams(g - 1, last)
-        last = now
-    tied_beams(groups - 1, last)
+    found = []
+    for k in range(channels // TB):
+        for copy in large[k * TB // COPY : (k + 1) * TB // COPY]:
+            copy.wait()
+        found.append(tile_beams(k))
+        g = k * TB // CB - 1
+        if g >= 0 and k * TB % CB == 0:
+            tied_beams(g, jnp.concatenate(found[g * CB // TB : (g + 1) * CB // TB], axis=0))
+    tied_beams(groups - 1, jnp.concatenate(found[-CB // TB :], axis=0))
 
 
 def last_kernel(parts_ref, out_ref):
@@ -250,7 +254,6 @@
         beam_order[None, :],
     )
     operands = [pltpu.with_memory_space_constraint(x, pltpu.HBM) for x in operands]
-    groups = channels // CB
     partial = pl.pallas_call(
         kernel,
         out_shape=pltpu.VMEM((n_stn * n_chan, rows, width), jnp.bfloat16),
@@ -260,7 +263,7 @@
         + [
             pltpu.VMEM((beams, channels * 2 * (station_weights.shape[2] // TPS)), jnp.bfloat16),
             pltpu.VMEM((volts.shape[3], station_weights.shape[2]), jnp.bfloat16),
-            pltpu.SemaphoreType.DMA((len(operands) - 1 + 2 * groups,)),
+            pltpu.SemaphoreType.DMA((len(operands) - 1 + channels // COPY,)),
         ],
         compiler_params=pltpu.CompilerParams(vmem_limit_bytes=24 * 2**20),
         name="partial_tied",

time: 18.8 us -> 19.4 us (1.032)
  Pallas kernels: 4.15 us -> 4.76 us
    pallas_call x1, Pallas kernels: 3.29 us -> 3.9 us  [shards(): pl.pallas_call(kernel, out_shape=pltpu.VMEM((n_stn * n_chan, rows, width)...]
where the time goes in v13:
time: 19.4 us; the launch traced here: 19.2 us
  blocking collectives  14.4 us (74%)
  Pallas kernels  4.76 us (25%)
    all_to_all x1, blocking collectives, shards(): lax.all_to_all(partial, ('stn', 'chan'), split_axis=0, concat_axis=0, axi...  14.4 us
    pallas_call x1, Pallas kernels, shards(): pl.pallas_call(kernel, out_shape=pltpu.VMEM((n_stn * n_chan, rows, width)...  3.9 us
    pallas_call x1, Pallas kernels, shards(): pl.pallas_call(last_kernel, out_shape=jax.ShapeDtypeStruct((rows, 2 * sam...  0.86 us

profile of v13, /device:TPU:0, one launch (start us, length us, event | category | flops | bytes accessed | tf_op | source)
XLA Modules:
  0.0 19.2 jit_solution(3469789280057036848)
XLA Ops:
  0.0 3.9 %partial_tied.1 = bf16[32,2,768]{2,1,0:T(2,128)(2,1)S(1)} custom-call(bf16[24,2,16,2048]{3,2,1,0:T(8,128)(2,1)} %volt_hbm.1, bf16[24,2,2048]{2,1,0:T(2,128)(2,1)} %aw_hbm.1, bf16[24,2,128]{2,1,0:T(2,128)(2,1)} %sw_hbm.1, s32[1,128]{1,0:T(1,128)} %bitcast.8, s32[1,128]{1,0:T(1,128)} %bitcast.9, f32[2,128]{1,0:T(2,128)} %bitcast.6, f32[2,64]{1,0:T(2,128)} %bitcast.7, ...), custom_call_target="tpu_custom_call" | custom-call | tf_op jit(solution)/shard_map/partial_tied/pallas_call | solution.py:257
  3.9 14.4 %all_to_all.5.parts_ref = bf16[32,2,768]{2,1,0:T(2,128)(2,1)S(1)} all-to-all(bf16[32,2,768]{2,1,0:T(2,128)(2,1)S(1)} %partial_tied.1), channel_id=1, replica_groups={{31,30,29,28,27,26,25,24,23,22,21,20,19,18,17,16,15,14,13,12,11,10,9,8,..., dimensions={0} | all-to-all | bytes 196608 | tf_op jit(solution)/shard_map/all_to_all | solution.py:271
  18.3 0.9 %tied_beams.1 = bf16[2,32,48]{2,1,0:T(8,128)(2,1)} custom-call(bf16[32,2,768]{2,1,0:T(2,128)(2,1)S(1)} %all_to_all.5.parts_ref), custom_call_target="tpu_custom_call" | custom-call | tf_op jit(solution)/shard_map/tied_beams/pallas_call | solution.py:280

commit v14 on v12

--- a/solution.py
+++ b/solution.py
@@ -12,6 +12,7 @@
 TPS = 16
 GROUPS = 4
 CB = 8
+STAGE = 512
 NT = (((1,), (1,)), ((), ()))
 SIN = [(-1) ** i * (2 * math.pi) ** (2 * i + 1) / math.factorial(2 * i + 1) for i in range(7)]
 
@@ -82,6 +83,7 @@
     order_ref,
     tied_ref,
     sum_ref,
+    tile_ref,
     sems,
 ):
     channels, _, samples, antennas = volt_hbm.shape
@@ -113,9 +115,10 @@
         )
     ]
     large = []
-    for k in range(2 * groups):
-        part = pl.ds(k * CB // 2, CB // 2)
-        large.append(start(volt_hbm.at[part], volts.at[part], len(small) + k))
+    stage_slices = [slice(k, k + STAGE) for k in range(0, antennas, STAGE)]
+    for k, part in enumerate(stage_slices):
+        source, target = volt_hbm.at[:, :, :, part], volts.at[:, :, :, part]
+        large.append(start(source, target, len(small) + k))
     antenna_tile = iota((antennas, tiles), 0) // TILE_ANTENNAS == iota((antennas, tiles), 1)
     sum_ref[...] = antenna_tile.astype(jnp.bfloat16)
     for copy in small[:4]:
@@ -168,18 +171,20 @@
             right.append(jnp.concatenate([im, re], axis=1))
         station_rows_of.append(jnp.concatenate(right, axis=0).astype(jnp.bfloat16))
 
-    def tile_beams(g):
+    def tile_sums(part):
         products = []
-        weights = aw_ref[g * CB : (g + 1) * CB].astype(jnp.float32)
-        for c in range(CB):
-            w_re = jnp.broadcast_to(weights[c, 0:1], (samples, antennas)).astype(jnp.bfloat16)
-            w_im = jnp.broadcast_to(weights[c, 1:2], (samples, antennas)).astype(jnp.bfloat16)
-            v_re, v_im = volts[g * CB + c, 0], volts[g * CB + c, 1]
+        for c in range(channels):
+            weights = aw_ref[c, :, part].astype(jnp.float32)
+            w_re = jnp.broadcast_to(weights[0:1], (samples, STAGE)).astype(jnp.bfloat16)
+            w_im = jnp.broadcast_to(weights[1:2], (samples, STAGE)).astype(jnp.bfloat16)
+            v_re, v_im = volts[c, 0, :, part], volts[c, 1, :, part]
             products.append(w_re * v_re - w_im * v_im)
             products.append(w_re * v_im + w_im * v_re)
         return jnp.dot(
-            jnp.concatenate(products, axis=0), sum_ref[...], preferred_element_type=jnp.float32
-        ).astype(jnp.bfloat16)
+            jnp.concatenate(products, axis=0),
+            sum_ref[part, :],
+            preferred_element_type=jnp.float32,
+        )
 
     def tied_beams(g, beams_tile):
         left = []
@@ -198,15 +203,16 @@
             devices, rows, CB * rows_c
         )
 
-    last = None
+    for copy, part in zip(large, stage_slices):
+        copy.wait()
+        sums = tile_sums(part)
+        if part.start == 0:
+            tile_ref[...] = sums
+        else:
+            tile_ref[...] += sums
     for g in range(groups):
-        large[2 * g].wait()
-        large[2 * g + 1].wait()
-        now = tile_beams(g)
-        if last is not None:
-            tied_beams(g - 1, last)
-        last = now
-    tied_beams(groups - 1, last)
+        rows_g = slice(g * CB * rows_c, (g + 1) * CB * rows_c)
+        tied_beams(g, tile_ref[rows_g, :].astype(jnp.bfloat16))
 
 
 def last_kernel(parts_ref, out_ref):
@@ -250,7 +256,6 @@
         beam_order[None, :],
     )
     operands = [pltpu.with_memory_space_constraint(x, pltpu.HBM) for x in operands]
-    groups = channels // CB
     partial = pl.pallas_call(
         kernel,
         out_shape=pltpu.VMEM((n_stn * n_chan, rows, width), jnp.bfloat16),
@@ -260,7 +265,8 @@
         + [
             pltpu.VMEM((beams, channels * 2 * (station_weights.shape[2] // TPS)), jnp.bfloat16),
             pltpu.VMEM((volts.shape[3], station_weights.shape[2]), jnp.bfloat16),
-            pltpu.SemaphoreType.DMA((len(operands) - 1 + 2 * groups,)),
+            pltpu.VMEM((width, station_weights.shape[2]), jnp.float32),
+            pltpu.SemaphoreType.DMA((len(operands) - 1 + volts.shape[3] // STAGE,)),
         ],
         compiler_params=pltpu.CompilerParams(vmem_limit_bytes=24 * 2**20),
         name="partial_tied",

time: 18.8 us -> 19.3 us (1.027)
  Pallas kernels: 4.15 us -> 4.75 us
    pallas_call x1, Pallas kernels: 3.29 us -> 3.88 us  [shards(): pl.pallas_call(kernel, out_shape=pltpu.VMEM((n_stn * n_chan, rows, width)...]
where the time goes in v14:
time: 19.3 us; the launch traced here: 19.2 us
  blocking collectives  14.4 us (75%)
  Pallas kernels  4.75 us (25%)
    all_to_all x1, blocking collectives, shards(): lax.all_to_all(partial, ('stn', 'chan'), split_axis=0, concat_axis=0, axi...  14.4 us
    pallas_call x1, Pallas kernels, shards(): pl.pallas_call(kernel, out_shape=pltpu.VMEM((n_stn * n_chan, rows, width)...  3.88 us
    pallas_call x1, Pallas kernels, shards(): pl.pallas_call(last_kernel, out_shape=jax.ShapeDtypeStruct((rows, 2 * sam...  0.86 us

profile of v14, /device:TPU:0, one launch (start us, length us, event | category | flops | bytes accessed | tf_op | source)
XLA Modules:
  0.0 19.2 jit_solution(2274709444563293406)
XLA Ops:
  0.0 3.9 %partial_tied.1 = bf16[32,2,768]{2,1,0:T(2,128)(2,1)S(1)} custom-call(bf16[24,2,16,2048]{3,2,1,0:T(8,128)(2,1)} %volt_hbm.1, bf16[24,2,2048]{2,1,0:T(2,128)(2,1)} %aw_hbm.1, bf16[24,2,128]{2,1,0:T(2,128)(2,1)} %sw_hbm.1, s32[1,128]{1,0:T(1,128)} %bitcast.8, s32[1,128]{1,0:T(1,128)} %bitcast.9, f32[2,128]{1,0:T(2,128)} %bitcast.6, f32[2,64]{1,0:T(2,128)} %bitcast.7, ...), custom_call_target="tpu_custom_call" | custom-call | tf_op jit(solution)/shard_map/partial_tied/pallas_call | solution.py:259
  3.9 14.4 %all_to_all.5.parts_ref = bf16[32,2,768]{2,1,0:T(2,128)(2,1)S(1)} all-to-all(bf16[32,2,768]{2,1,0:T(2,128)(2,1)S(1)} %partial_tied.1), channel_id=1, replica_groups={{31,30,29,28,27,26,25,24,23,22,21,20,19,18,17,16,15,14,13,12,11,10,9,8,..., dimensions={0} | all-to-all | bytes 196608 | tf_op jit(solution)/shard_map/all_to_all | solution.py:274
  18.3 0.9 %tied_beams.1 = bf16[2,32,48]{2,1,0:T(8,128)(2,1)} custom-call(bf16[32,2,768]{2,1,0:T(2,128)(2,1)S(1)} %all_to_all.5.parts_ref), custom_call_target="tpu_custom_call" | custom-call | tf_op jit(solution)/shard_map/tied_beams/pallas_call | solution.py:283

commit v15 on v12

--- a/solution.py
+++ b/solution.py
@@ -98,24 +98,23 @@
         copy.start()
         return copy
 
-    small = [
-        start(source, target, k)
-        for k, (source, target) in enumerate(
-            [
-                (order_hbm, order_ref),
-                (dir_hbm, dir_ref),
-                (pos_hbm, pos_ref),
-                (group_hbm, group_ref),
-                (ts_hbm, ts_ref),
-                (sw_hbm, sw_ref),
-                (aw_hbm, aw_ref),
-            ]
-        )
-    ]
-    large = []
-    for k in range(2 * groups):
-        part = pl.ds(k * CB // 2, CB // 2)
-        large.append(start(volt_hbm.at[part], volts.at[part], len(small) + k))
+    def voltages(g):
+        part = pl.ds(g * CB, CB)
+        return volt_hbm.at[part], volts.at[part]
+
+    pairs = [
+        (order_hbm, order_ref),
+        (dir_hbm, dir_ref),
+        (pos_hbm, pos_ref),
+        (group_hbm, group_ref),
+        voltages(0),
+        (aw_hbm, aw_ref),
+        (ts_hbm, ts_ref),
+        (sw_hbm, sw_ref),
+    ] + [voltages(g) for g in range(1, groups)]
+    copies = [start(source, target, k) for k, (source, target) in enumerate(pairs)]
+    small = copies[:4] + copies[5:8]
+    large = copies[4:5] + copies[8:]
     antenna_tile = iota((antennas, tiles), 0) // TILE_ANTENNAS == iota((antennas, tiles), 1)
     sum_ref[...] = antenna_tile.astype(jnp.bfloat16)
     for copy in small[:4]:
@@ -200,8 +199,7 @@
 
     last = None
     for g in range(groups):
-        large[2 * g].wait()
-        large[2 * g + 1].wait()
+        large[g].wait()
         now = tile_beams(g)
         if last is not None:
             tied_beams(g - 1, last)
@@ -250,7 +248,6 @@
         beam_order[None, :],
     )
     operands = [pltpu.with_memory_space_constraint(x, pltpu.HBM) for x in operands]
-    groups = channels // CB
     partial = pl.pallas_call(
         kernel,
         out_shape=pltpu.VMEM((n_stn * n_chan, rows, width), jnp.bfloat16),
@@ -260,7 +257,7 @@
         + [
             pltpu.VMEM((beams, channels * 2 * (station_weights.shape[2] // TPS)), jnp.bfloat16),
             pltpu.VMEM((volts.shape[3], station_weights.shape[2]), jnp.bfloat16),
-            pltpu.SemaphoreType.DMA((len(operands) - 1 + 2 * groups,)),
+            pltpu.SemaphoreType.DMA((len(operands) - 1 + channels // CB,)),
         ],
         compiler_params=pltpu.CompilerParams(vmem_limit_bytes=24 * 2**20),
         name="partial_tied",

time: 18.8 us -> 18.7 us (level)
  no operation moved by 1% of the time
where the time goes in v15:
time: 18.7 us; the launch traced here: 18.5 us
  blocking collectives  14.4 us (77%)
  Pallas kernels  4.07 us (22%)
    all_to_all x1, blocking collectives, shards(): lax.all_to_all(partial, ('stn', 'chan'), split_axis=0, concat_axis=0, axi...  14.4 us
    pallas_call x1, Pallas kernels, shards(): pl.pallas_call(kernel, out_shape=pltpu.VMEM((n_stn * n_chan, rows, width)...  3.21 us
    pallas_call x1, Pallas kernels, shards(): pl.pallas_call(last_kernel, out_shape=jax.ShapeDtypeStruct((rows, 2 * sam...  0.86 us

profile of v15, /device:TPU:0, one launch (start us, length us, event | category | flops | bytes accessed | tf_op | source)
XLA Modules:
  0.0 18.5 jit_solution(10196152831224635390)
XLA Ops:
  0.0 3.2 %partial_tied.1 = bf16[32,2,768]{2,1,0:T(2,128)(2,1)S(1)} custom-call(bf16[24,2,16,2048]{3,2,1,0:T(8,128)(2,1)} %volt_hbm.1, bf16[24,2,2048]{2,1,0:T(2,128)(2,1)} %aw_hbm.1, bf16[24,2,128]{2,1,0:T(2,128)(2,1)} %sw_hbm.1, s32[1,128]{1,0:T(1,128)} %bitcast.8, s32[1,128]{1,0:T(1,128)} %bitcast.9, f32[2,128]{1,0:T(2,128)} %bitcast.6, f32[2,64]{1,0:T(2,128)} %bitcast.7, ...), custom_call_target="tpu_custom_call" | custom-call | tf_op jit(solution)/shard_map/partial_tied/pallas_call | solution.py:251
  3.2 14.4 %all_to_all.5.parts_ref = bf16[32,2,768]{2,1,0:T(2,128)(2,1)S(1)} all-to-all(bf16[32,2,768]{2,1,0:T(2,128)(2,1)S(1)} %partial_tied.1), channel_id=1, replica_groups={{31,30,29,28,27,26,25,24,23,22,21,20,19,18,17,16,15,14,13,12,11,10,9,8,..., dimensions={0} | all-to-all | bytes 196608 | tf_op jit(solution)/shard_map/all_to_all | solution.py:265
  17.7 0.9 %tied_beams.1 = bf16[2,32,48]{2,1,0:T(8,128)(2,1)} custom-call(bf16[32,2,768]{2,1,0:T(2,128)(2,1)S(1)} %all_to_all.5.parts_ref), custom_call_target="tpu_custom_call" | custom-call | tf_op jit(solution)/shard_map/tied_beams/pallas_call | solution.py:274

commit v16 on v15

--- a/solution.py
+++ b/solution.py
@@ -176,9 +176,15 @@
             v_re, v_im = volts[g * CB + c, 0], volts[g * CB + c, 1]
             products.append(w_re * v_re - w_im * v_im)
             products.append(w_re * v_im + w_im * v_re)
-        return jnp.dot(
-            jnp.concatenate(products, axis=0), sum_ref[...], preferred_element_type=jnp.float32
-        ).astype(jnp.bfloat16)
+        products = jnp.concatenate(products, axis=0)
+        half = antennas // 2
+        sums = [
+            jnp.dot(
+                products[:, part], sum_ref[part, :], preferred_element_type=jnp.float32
+            )
+            for part in (slice(0, half), slice(half, antennas))
+        ]
+        return (sums[0] + sums[1]).astype(jnp.bfloat16)
 
     def tied_beams(g, beams_tile):
         left = []

time: 18.7 us -> 18.7 us (level)
  no operation moved by 1% of the time
where the time goes in v16:
time: 18.7 us; the launch traced here: 18.5 us
  blocking collectives  14.4 us (77%)
  Pallas kernels  4.07 us (22%)
    all_to_all x1, blocking collectives, shards(): lax.all_to_all(partial, ('stn', 'chan'), split_axis=0, concat_axis=0, axi...  14.4 us
    pallas_call x1, Pallas kernels, shards(): pl.pallas_call(kernel, out_shape=pltpu.VMEM((n_stn * n_chan, rows, width)...  3.21 us
    pallas_call x1, Pallas kernels, shards(): pl.pallas_call(last_kernel, out_shape=jax.ShapeDtypeStruct((rows, 2 * sam...  0.86 us

profile of v16, /device:TPU:0, one launch (start us, length us, event | category | flops | bytes accessed | tf_op | source)
XLA Modules:
  0.0 18.5 jit_solution(425720413691319006)
XLA Ops:
  0.0 3.2 %partial_tied.1 = bf16[32,2,768]{2,1,0:T(2,128)(2,1)S(1)} custom-call(bf16[24,2,16,2048]{3,2,1,0:T(8,128)(2,1)} %volt_hbm.1, bf16[24,2,2048]{2,1,0:T(2,128)(2,1)} %aw_hbm.1, bf16[24,2,128]{2,1,0:T(2,128)(2,1)} %sw_hbm.1, s32[1,128]{1,0:T(1,128)} %bitcast.8, s32[1,128]{1,0:T(1,128)} %bitcast.9, f32[2,128]{1,0:T(2,128)} %bitcast.6, f32[2,64]{1,0:T(2,128)} %bitcast.7, ...), custom_call_target="tpu_custom_call" | custom-call | tf_op jit(solution)/shard_map/partial_tied/pallas_call | solution.py:257
  3.2 14.4 %all_to_all.5.parts_ref = bf16[32,2,768]{2,1,0:T(2,128)(2,1)S(1)} all-to-all(bf16[32,2,768]{2,1,0:T(2,128)(2,1)S(1)} %partial_tied.1), channel_id=1, replica_groups={{31,30,29,28,27,26,25,24,23,22,21,20,19,18,17,16,15,14,13,12,11,10,9,8,..., dimensions={0} | all-to-all | bytes 196608 | tf_op jit(solution)/shard_map/all_to_all | solution.py:271
  17.7 0.9 %tied_beams.1 = bf16[2,32,48]{2,1,0:T(8,128)(2,1)} custom-call(bf16[32,2,768]{2,1,0:T(2,128)(2,1)S(1)} %all_to_all.5.parts_ref), custom_call_target="tpu_custom_call" | custom-call | tf_op jit(solution)/shard_map/tied_beams/pallas_call | solution.py:280

commit v17 on v15

--- a/solution.py
+++ b/solution.py
@@ -103,69 +103,21 @@
         return volt_hbm.at[part], volts.at[part]
 
     pairs = [
+        voltages(0),
+        (aw_hbm, aw_ref),
         (order_hbm, order_ref),
         (dir_hbm, dir_ref),
         (pos_hbm, pos_ref),
         (group_hbm, group_ref),
-        voltages(0),
-        (aw_hbm, aw_ref),
         (ts_hbm, ts_ref),
         (sw_hbm, sw_ref),
     ] + [voltages(g) for g in range(1, groups)]
     copies = [start(source, target, k) for k, (source, target) in enumerate(pairs)]
-    small = copies[:4] + copies[5:8]
-    large = copies[4:5] + copies[8:]
+    large = copies[:1] + copies[8:]
     antenna_tile = iota((antennas, tiles), 0) // TILE_ANTENNAS == iota((antennas, tiles), 1)
     sum_ref[...] = antenna_tile.astype(jnp.bfloat16)
-    for copy in small[:4]:
+    for copy in copies[:2]:
         copy.wait()
-
-    east_s, north_s, group_s = station_rows(pos_ref, group_ref, stations, lanes)
-    lane = iota((1, lanes), 1)
-    channel_lane = lane // (2 * stations)
-    quarter = 0.25 * ((lane // stations) % 2).astype(jnp.float32)
-    first_chan = lax.axis_index("chan") * channels
-    total_chans = channels * lax.axis_size("chan")
-    block = min(64, beams)
-
-    def tied_rows(first):
-        east, north, group = beam_columns(order_ref, dir_ref, first, block)
-        delay = east * east_s + north * north_s
-        member = jnp.where(group == group_s, scale, 0.0)
-        for g in range(groups):
-            freq = 1.0 + (first_chan + g * CB + channel_lane).astype(jnp.float32) / total_chans
-            wave = cos_turns(delay * freq - quarter)
-            tied_ref[pl.ds(first, block), g * lanes : (g + 1) * lanes] = (wave * member).astype(
-                jnp.bfloat16
-            )
-
-    if beams == block:
-        tied_rows(0)
-    else:
-
-        def body(i, carry):
-            tied_rows(pl.multiple_of(i * block, block))
-            return carry
-
-        lax.fori_loop(0, beams // block, body, 0)
-
-    for copy in small[4:]:
-        copy.wait()
-    member_table = (iota((stations, tiles), 0) == ts_ref[...] % stations).astype(jnp.float32)
-    own_channel = iota((lanes, CB * rows_c), 0) // (2 * stations) == iota(
-        (lanes, CB * rows_c), 1
-    ) // rows_c
-
-    station_rows_of = []
-    for g in range(groups):
-        swt = sw_ref[g * CB : (g + 1) * CB].astype(jnp.float32)
-        right = []
-        for c in range(CB):
-            re = swt[c, 0:1] * member_table
-            im = swt[c, 1:2] * member_table
-            right.append(jnp.concatenate([re, -im], axis=1))
-            right.append(jnp.concatenate([im, re], axis=1))
-        station_rows_of.append(jnp.concatenate(right, axis=0).astype(jnp.bfloat16))
 
     def tile_beams(g):
         products = []
@@ -179,6 +131,55 @@
         return jnp.dot(
             jnp.concatenate(products, axis=0), sum_ref[...], preferred_element_type=jnp.float32
         ).astype(jnp.bfloat16)
+
+    last = tile_beams(0)
+    for copy in copies[2:9]:
+        copy.wait()
+
+    east_s, north_s, group_s = station_rows(pos_ref, group_ref, stations, lanes)
+    lane = iota((1, lanes), 1)
+    channel_lane = lane // (2 * stations)
+    quarter = 0.25 * ((lane // stations) % 2).astype(jnp.float32)
+    first_chan = lax.axis_index("chan") * channels
+    total_chans = channels * lax.axis_size("chan")
+    block = min(64, beams)
+
+    def tied_rows(first):
+        east, north, group = beam_columns(order_ref, dir_ref, first, block)
+        delay = east * east_s + north * north_s
+        member = jnp.where(group == group_s, scale, 0.0)
+        for g in range(groups):
+            freq = 1.0 + (first_chan + g * CB + channel_lane).astype(jnp.float32) / total_chans
+            wave = cos_turns(delay * freq - quarter)
+            tied_ref[pl.ds(first, block), g * lanes : (g + 1) * lanes] = (wave * member).astype(
+                jnp.bfloat16
+            )
+
+    if beams == block:
+        tied_rows(0)
+    else:
+
+        def body(i, carry):
+            tied_rows(pl.multiple_of(i * block, block))
+            return carry
+
+        lax.fori_loop(0, beams // block, body, 0)
+
+    member_table = (iota((stations, tiles), 0) == ts_ref[...] % stations).astype(jnp.float32)
+    own_channel = iota((lanes, CB * rows_c), 0) // (2 * stations) == iota(
+        (lanes, CB * rows_c), 1
+    ) // rows_c
+
+    station_rows_of = []
+    for g in range(groups):
+        swt = sw_ref[g * CB : (g + 1) * CB].astype(jnp.float32)
+        right = []
+        for c in range(CB):
+            re = swt[c, 0:1] * member_table
+            im = swt[c, 1:2] * member_table
+            right.append(jnp.concatenate([re, -im], axis=1))
+            right.append(jnp.concatenate([im, re], axis=1))
+        station_rows_of.append(jnp.concatenate(right, axis=0).astype(jnp.bfloat16))
 
     def tied_beams(g, beams_tile):
         left = []
@@ -197,12 +198,11 @@
             devices, rows, CB * rows_c
         )
 
-    last = None
-    for g in range(groups):
-        large[g].wait()
+    for g in range(1, groups):
+        if g > 1:
+            large[g].wait()
         now = tile_beams(g)
-        if last is not None:
-            tied_beams(g - 1, last)
+        tied_beams(g - 1, last)
         last = now
     tied_beams(groups - 1, last)
 

time: 18.7 us -> 18.6 us (level)
  no operation moved by 1% of the time
where the time goes in v17:
time: 18.6 us; the launch traced here: 18.5 us
  blocking collectives  14.4 us (77%)
  Pallas kernels  4.04 us (22%)
    all_to_all x1, blocking collectives, shards(): lax.all_to_all(partial, ('stn', 'chan'), split_axis=0, concat_axis=0, axi...  14.4 us
    pallas_call x1, Pallas kernels, shards(): pl.pallas_call(kernel, out_shape=pltpu.VMEM((n_stn * n_chan, rows, width)...  3.17 us
    pallas_call x1, Pallas kernels, shards(): pl.pallas_call(last_kernel, out_shape=jax.ShapeDtypeStruct((rows, 2 * sam...  0.86 us

profile of v17, /device:TPU:0, one launch (start us, length us, event | category | flops | bytes accessed | tf_op | source)
XLA Modules:
  0.0 18.5 jit_solution(2607778465743667590)
XLA Ops:
  0.0 3.2 %partial_tied.1 = bf16[32,2,768]{2,1,0:T(2,128)(2,1)S(1)} custom-call(bf16[24,2,16,2048]{3,2,1,0:T(8,128)(2,1)} %volt_hbm.1, bf16[24,2,2048]{2,1,0:T(2,128)(2,1)} %aw_hbm.1, bf16[24,2,128]{2,1,0:T(2,128)(2,1)} %sw_hbm.1, s32[1,128]{1,0:T(1,128)} %bitcast.8, s32[1,128]{1,0:T(1,128)} %bitcast.9, f32[2,128]{1,0:T(2,128)} %bitcast.6, f32[2,64]{1,0:T(2,128)} %bitcast.7, ...), custom_call_target="tpu_custom_call" | custom-call | tf_op jit(solution)/shard_map/partial_tied/pallas_call | solution.py:251
  3.2 14.4 %all_to_all.5.parts_ref = bf16[32,2,768]{2,1,0:T(2,128)(2,1)S(1)} all-to-all(bf16[32,2,768]{2,1,0:T(2,128)(2,1)S(1)} %partial_tied.1), channel_id=1, replica_groups={{31,30,29,28,27,26,25,24,23,22,21,20,19,18,17,16,15,14,13,12,11,10,9,8,..., dimensions={0} | all-to-all | bytes 196608 | tf_op jit(solution)/shard_map/all_to_all | solution.py:265
  17.6 0.9 %tied_beams.1 = bf16[2,32,48]{2,1,0:T(8,128)(2,1)} custom-call(bf16[32,2,768]{2,1,0:T(2,128)(2,1)S(1)} %all_to_all.5.parts_ref), custom_call_target="tpu_custom_call" | custom-call | tf_op jit(solution)/shard_map/tied_beams/pallas_call | solution.py:274

commit v18 on v17

--- a/solution.py
+++ b/solution.py
@@ -102,18 +102,19 @@
         part = pl.ds(g * CB, CB)
         return volt_hbm.at[part], volts.at[part]
 
-    pairs = [
-        voltages(0),
-        (aw_hbm, aw_ref),
+    pairs = [voltages(0), (aw_hbm, aw_ref)]
+    pairs += [voltages(g) for g in range(1, groups)]
+    pairs += [
         (order_hbm, order_ref),
         (dir_hbm, dir_ref),
         (pos_hbm, pos_ref),
         (group_hbm, group_ref),
         (ts_hbm, ts_ref),
         (sw_hbm, sw_ref),
-    ] + [voltages(g) for g in range(1, groups)]
+    ]
     copies = [start(source, target, k) for k, (source, target) in enumerate(pairs)]
-    large = copies[:1] + copies[8:]
+    large = copies[:1] + copies[2 : groups + 1]
+    small = copies[groups + 1 :]
     antenna_tile = iota((antennas, tiles), 0) // TILE_ANTENNAS == iota((antennas, tiles), 1)
     sum_ref[...] = antenna_tile.astype(jnp.bfloat16)
     for copy in copies[:2]:
@@ -133,8 +134,9 @@
         ).astype(jnp.bfloat16)
 
     last = tile_beams(0)
-    for copy in copies[2:9]:
+    for copy in small:
         copy.wait()
+    large[1].wait()
 
     east_s, north_s, group_s = station_rows(pos_ref, group_ref, stations, lanes)
     lane = iota((1, lanes), 1)

time: 18.6 us -> 18.8 us (1.011)
  no operation moved by 1% of the time
where the time goes in v18:
time: 18.8 us; the launch traced here: 18.6 us
  blocking collectives  14.4 us (77%)
  Pallas kernels  4.11 us (22%)
    all_to_all x1, blocking collectives, shards(): lax.all_to_all(partial, ('stn', 'chan'), split_axis=0, concat_axis=0, axi...  14.4 us
    pallas_call x1, Pallas kernels, shards(): pl.pallas_call(kernel, out_shape=pltpu.VMEM((n_stn * n_chan, rows, width)...  3.25 us
    pallas_call x1, Pallas kernels, shards(): pl.pallas_call(last_kernel, out_shape=jax.ShapeDtypeStruct((rows, 2 * sam...  0.86 us

profile of v18, /device:TPU:0, one launch (start us, length us, event | category | flops | bytes accessed | tf_op | source)
XLA Modules:
  0.0 18.6 jit_solution(12287530406410628542)
XLA Ops:
  0.0 3.3 %partial_tied.1 = bf16[32,2,768]{2,1,0:T(2,128)(2,1)S(1)} custom-call(bf16[24,2,16,2048]{3,2,1,0:T(8,128)(2,1)} %volt_hbm.1, bf16[24,2,2048]{2,1,0:T(2,128)(2,1)} %aw_hbm.1, bf16[24,2,128]{2,1,0:T(2,128)(2,1)} %sw_hbm.1, s32[1,128]{1,0:T(1,128)} %bitcast.8, s32[1,128]{1,0:T(1,128)} %bitcast.9, f32[2,128]{1,0:T(2,128)} %bitcast.6, f32[2,64]{1,0:T(2,128)} %bitcast.7, ...), custom_call_target="tpu_custom_call" | custom-call | tf_op jit(solution)/shard_map/partial_tied/pallas_call | solution.py:253
  3.3 14.4 %all_to_all.5.parts_ref = bf16[32,2,768]{2,1,0:T(2,128)(2,1)S(1)} all-to-all(bf16[32,2,768]{2,1,0:T(2,128)(2,1)S(1)} %partial_tied.1), channel_id=1, replica_groups={{31,30,29,28,27,26,25,24,23,22,21,20,19,18,17,16,15,14,13,12,11,10,9,8,..., dimensions={0} | all-to-all | bytes 196608 | tf_op jit(solution)/shard_map/all_to_all | solution.py:267
  17.7 0.9 %tied_beams.1 = bf16[2,32,48]{2,1,0:T(8,128)(2,1)} custom-call(bf16[32,2,768]{2,1,0:T(2,128)(2,1)S(1)} %all_to_all.5.parts_ref), custom_call_target="tpu_custom_call" | custom-call | tf_op jit(solution)/shard_map/tied_beams/pallas_call | solution.py:276

commit v19 on v17

--- a/solution.py
+++ b/solution.py
@@ -123,11 +123,11 @@
         products = []
         weights = aw_ref[g * CB : (g + 1) * CB].astype(jnp.float32)
         for c in range(CB):
-            w_re = jnp.broadcast_to(weights[c, 0:1], (samples, antennas)).astype(jnp.bfloat16)
-            w_im = jnp.broadcast_to(weights[c, 1:2], (samples, antennas)).astype(jnp.bfloat16)
-            v_re, v_im = volts[g * CB + c, 0], volts[g * CB + c, 1]
-            products.append(w_re * v_re - w_im * v_im)
-            products.append(w_re * v_im + w_im * v_re)
+            w_re, w_im = weights[c, 0:1], weights[c, 1:2]
+            v_re = volts[g * CB + c, 0].astype(jnp.float32)
+            v_im = volts[g * CB + c, 1].astype(jnp.float32)
+            products.append((w_re * v_re - w_im * v_im).astype(jnp.bfloat16))
+            products.append((w_re * v_im + w_im * v_re).astype(jnp.bfloat16))
         return jnp.dot(
             jnp.concatenate(products, axis=0), sum_ref[...], preferred_element_type=jnp.float32
         ).astype(jnp.bfloat16)

time: 18.6 us -> 19 us (1.022)
  Pallas kernels: 4.04 us -> 4.39 us
    pallas_call x1, Pallas kernels: 3.17 us -> 3.53 us  [shards(): pl.pallas_call(kernel, out_shape=pltpu.VMEM((n_stn * n_chan, rows, width)...]
where the time goes in v19:
time: 19 us; the launch traced here: 18.8 us
  blocking collectives  14.4 us (76%)
  Pallas kernels  4.39 us (23%)
    all_to_all x1, blocking collectives, shards(): lax.all_to_all(partial, ('stn', 'chan'), split_axis=0, concat_axis=0, axi...  14.4 us
    pallas_call x1, Pallas kernels, shards(): pl.pallas_call(kernel, out_shape=pltpu.VMEM((n_stn * n_chan, rows, width)...  3.53 us
    pallas_call x1, Pallas kernels, shards(): pl.pallas_call(last_kernel, out_shape=jax.ShapeDtypeStruct((rows, 2 * sam...  0.86 us

profile of v19, /device:TPU:0, one launch (start us, length us, event | category | flops | bytes accessed | tf_op | source)
XLA Modules:
  0.0 18.8 jit_solution(6630663982264989953)
XLA Ops:
  0.0 3.5 %partial_tied.1 = bf16[32,2,768]{2,1,0:T(2,128)(2,1)S(1)} custom-call(bf16[24,2,16,2048]{3,2,1,0:T(8,128)(2,1)} %volt_hbm.1, bf16[24,2,2048]{2,1,0:T(2,128)(2,1)} %aw_hbm.1, bf16[24,2,128]{2,1,0:T(2,128)(2,1)} %sw_hbm.1, s32[1,128]{1,0:T(1,128)} %bitcast.8, s32[1,128]{1,0:T(1,128)} %bitcast.9, f32[2,128]{1,0:T(2,128)} %bitcast.6, f32[2,64]{1,0:T(2,128)} %bitcast.7, ...), custom_call_target="tpu_custom_call" | custom-call | tf_op jit(solution)/shard_map/partial_tied/pallas_call | solution.py:251
  3.5 14.4 %all_to_all.5.parts_ref = bf16[32,2,768]{2,1,0:T(2,128)(2,1)S(1)} all-to-all(bf16[32,2,768]{2,1,0:T(2,128)(2,1)S(1)} %partial_tied.1), channel_id=1, replica_groups={{31,30,29,28,27,26,25,24,23,22,21,20,19,18,17,16,15,14,13,12,11,10,9,8,..., dimensions={0} | all-to-all | bytes 196608 | tf_op jit(solution)/shard_map/all_to_all | solution.py:265
  18.0 0.9 %tied_beams.1 = bf16[2,32,48]{2,1,0:T(8,128)(2,1)} custom-call(bf16[32,2,768]{2,1,0:T(2,128)(2,1)S(1)} %all_to_all.5.parts_ref), custom_call_target="tpu_custom_call" | custom-call | tf_op jit(solution)/shard_map/tied_beams/pallas_call | solution.py:274

commit v20 on v17

--- a/solution.py
+++ b/solution.py
@@ -121,10 +121,9 @@
 
     def tile_beams(g):
         products = []
-        weights = aw_ref[g * CB : (g + 1) * CB].astype(jnp.float32)
         for c in range(CB):
-            w_re = jnp.broadcast_to(weights[c, 0:1], (samples, antennas)).astype(jnp.bfloat16)
-            w_im = jnp.broadcast_to(weights[c, 1:2], (samples, antennas)).astype(jnp.bfloat16)
+            w_re = jnp.broadcast_to(aw_ref[g * CB + c, 0:1], (samples, antennas))
+            w_im = jnp.broadcast_to(aw_ref[g * CB + c, 1:2], (samples, antennas))
             v_re, v_im = volts[g * CB + c, 0], volts[g * CB + c, 1]
             products.append(w_re * v_re - w_im * v_im)
             products.append(w_re * v_im + w_im * v_re)

time: 18.6 us -> 18.7 us (level)
  no operation moved by 1% of the time
where the time goes in v20:
time: 18.7 us; the launch traced here: 18.5 us
  blocking collectives  14.4 us (77%)
  Pallas kernels  4.05 us (22%)
    all_to_all x1, blocking collectives, shards(): lax.all_to_all(partial, ('stn', 'chan'), split_axis=0, concat_axis=0, axi...  14.4 us
    pallas_call x1, Pallas kernels, shards(): pl.pallas_call(kernel, out_shape=pltpu.VMEM((n_stn * n_chan, rows, width)...  3.19 us
    pallas_call x1, Pallas kernels, shards(): pl.pallas_call(last_kernel, out_shape=jax.ShapeDtypeStruct((rows, 2 * sam...  0.86 us

profile of v20, /device:TPU:0, one launch (start us, length us, event | category | flops | bytes accessed | tf_op | source)
XLA Modules:
  0.0 18.5 jit_solution(16268063814245275958)
XLA Ops:
  0.0 3.2 %partial_tied.1 = bf16[32,2,768]{2,1,0:T(2,128)(2,1)S(1)} custom-call(bf16[24,2,16,2048]{3,2,1,0:T(8,128)(2,1)} %volt_hbm.1, bf16[24,2,2048]{2,1,0:T(2,128)(2,1)} %aw_hbm.1, bf16[24,2,128]{2,1,0:T(2,128)(2,1)} %sw_hbm.1, s32[1,128]{1,0:T(1,128)} %bitcast.8, s32[1,128]{1,0:T(1,128)} %bitcast.9, f32[2,128]{1,0:T(2,128)} %bitcast.6, f32[2,64]{1,0:T(2,128)} %bitcast.7, ...), custom_call_target="tpu_custom_call" | custom-call | tf_op jit(solution)/shard_map/partial_tied/pallas_call | solution.py:250
  3.2 14.4 %all_to_all.5.parts_ref = bf16[32,2,768]{2,1,0:T(2,128)(2,1)S(1)} all-to-all(bf16[32,2,768]{2,1,0:T(2,128)(2,1)S(1)} %partial_tied.1), channel_id=1, replica_groups={{31,30,29,28,27,26,25,24,23,22,21,20,19,18,17,16,15,14,13,12,11,10,9,8,..., dimensions={0} | all-to-all | bytes 196608 | tf_op jit(solution)/shard_map/all_to_all | solution.py:264
  17.6 0.9 %tied_beams.1 = bf16[2,32,48]{2,1,0:T(8,128)(2,1)} custom-call(bf16[32,2,768]{2,1,0:T(2,128)(2,1)S(1)} %all_to_all.5.parts_ref), custom_call_target="tpu_custom_call" | custom-call | tf_op jit(solution)/shard_map/tied_beams/pallas_call | solution.py:273

commit v21 on v19

--- a/solution.py
+++ b/solution.py
@@ -12,6 +12,7 @@
 TPS = 16
 GROUPS = 4
 CB = 8
+PIECE = 512
 NT = (((1,), (1,)), ((), ()))
 SIN = [(-1) ** i * (2 * math.pi) ** (2 * i + 1) / math.factorial(2 * i + 1) for i in range(7)]
 
@@ -120,17 +121,25 @@
         copy.wait()
 
     def tile_beams(g):
-        products = []
         weights = aw_ref[g * CB : (g + 1) * CB].astype(jnp.float32)
-        for c in range(CB):
-            w_re, w_im = weights[c, 0:1], weights[c, 1:2]
-            v_re = volts[g * CB + c, 0].astype(jnp.float32)
-            v_im = volts[g * CB + c, 1].astype(jnp.float32)
-            products.append((w_re * v_re - w_im * v_im).astype(jnp.bfloat16))
-            products.append((w_re * v_im + w_im * v_re).astype(jnp.bfloat16))
-        return jnp.dot(
-            jnp.concatenate(products, axis=0), sum_ref[...], preferred_element_type=jnp.float32
-        ).astype(jnp.bfloat16)
+        sums = None
+        for first in range(0, antennas, PIECE):
+            part = slice(first, first + PIECE)
+            products = []
+            for c in range(CB):
+                w_re = jnp.broadcast_to(weights[c, 0:1, part], (samples, PIECE))
+                w_im = jnp.broadcast_to(weights[c, 1:2, part], (samples, PIECE))
+                w_re, w_im = w_re.astype(jnp.bfloat16), w_im.astype(jnp.bfloat16)
+                v_re, v_im = volts[g * CB + c, 0, :, part], volts[g * CB + c, 1, :, part]
+                products.append(w_re * v_re - w_im * v_im)
+                products.append(w_re * v_im + w_im * v_re)
+            piece = jnp.dot(
+                jnp.concatenate(products, axis=0),
+                sum_ref[part, :],
+                preferred_element_type=jnp.float32,
+            )
+            sums = piece if sums is None else sums + piece
+        return sums.astype(jnp.bfloat16)
 
     last = tile_beams(0)
     for copy in copies[2:9]:

time: 19 us -> 18.6 us (0.979)
  Pallas kernels: 4.39 us -> 4.02 us
    pallas_call x1, Pallas kernels: 3.53 us -> 3.16 us  [shards(): pl.pallas_call(kernel, out_shape=pltpu.VMEM((n_stn * n_chan, rows, width)...]
where the time goes in v21:
time: 18.6 us; the launch traced here: 18.5 us
  blocking collectives  14.5 us (78%)
  Pallas kernels  4.02 us (22%)
    all_to_all x1, blocking collectives, shards(): lax.all_to_all(partial, ('stn', 'chan'), split_axis=0, concat_axis=0, axi...  14.5 us
    pallas_call x1, Pallas kernels, shards(): pl.pallas_call(kernel, out_shape=pltpu.VMEM((n_stn * n_chan, rows, width)...  3.16 us
    pallas_call x1, Pallas kernels, shards(): pl.pallas_call(last_kernel, out_shape=jax.ShapeDtypeStruct((rows, 2 * sam...  0.86 us

profile of v21, /device:TPU:0, one launch (start us, length us, event | category | flops | bytes accessed | tf_op | source)
XLA Modules:
  0.0 18.5 jit_solution(849181070270802919)
XLA Ops:
  0.0 3.2 %partial_tied.1 = bf16[32,2,768]{2,1,0:T(2,128)(2,1)S(1)} custom-call(bf16[24,2,16,2048]{3,2,1,0:T(8,128)(2,1)} %volt_hbm.1, bf16[24,2,2048]{2,1,0:T(2,128)(2,1)} %aw_hbm.1, bf16[24,2,128]{2,1,0:T(2,128)(2,1)} %sw_hbm.1, s32[1,128]{1,0:T(1,128)} %bitcast.8, s32[1,128]{1,0:T(1,128)} %bitcast.9, f32[2,128]{1,0:T(2,128)} %bitcast.6, f32[2,64]{1,0:T(2,128)} %bitcast.7, ...), custom_call_target="tpu_custom_call" | custom-call | tf_op jit(solution)/shard_map/partial_tied/pallas_call | solution.py:260
  3.2 14.5 %all_to_all.5.parts_ref = bf16[32,2,768]{2,1,0:T(2,128)(2,1)S(1)} all-to-all(bf16[32,2,768]{2,1,0:T(2,128)(2,1)S(1)} %partial_tied.1), channel_id=1, replica_groups={{31,30,29,28,27,26,25,24,23,22,21,20,19,18,17,16,15,14,13,12,11,10,9,8,..., dimensions={0} | all-to-all | bytes 196608 | tf_op jit(solution)/shard_map/all_to_all | solution.py:274
  17.6 0.9 %tied_beams.1 = bf16[2,32,48]{2,1,0:T(8,128)(2,1)} custom-call(bf16[32,2,768]{2,1,0:T(2,128)(2,1)S(1)} %all_to_all.5.parts_ref), custom_call_target="tpu_custom_call" | custom-call | tf_op jit(solution)/shard_map/tied_beams/pallas_call | solution.py:283

commit v22 on v17

--- a/solution.py
+++ b/solution.py
@@ -12,6 +12,7 @@
 TPS = 16
 GROUPS = 4
 CB = 8
+QUEUES = (0, 1, 1, 1, 1, 1, 1, 1, 1, 0)
 NT = (((1,), (1,)), ((), ()))
 SIN = [(-1) ** i * (2 * math.pi) ** (2 * i + 1) / math.factorial(2 * i + 1) for i in range(7)]
 
@@ -95,7 +96,7 @@
 
     def start(source, target, k):
         copy = pltpu.make_async_copy(source, target, sems.at[k])
-        copy.start()
+        copy.start(priority=QUEUES[k])
         return copy
 
     def voltages(g):

time: 18.6 us -> 19 us (1.022)
  Pallas kernels: 4.04 us -> 4.38 us
    pallas_call x1, Pallas kernels: 3.17 us -> 3.52 us  [shards(): pl.pallas_call(kernel, out_shape=pltpu.VMEM((n_stn * n_chan, rows, width)...]
where the time goes in v22:
time: 19 us; the launch traced here: 18.8 us
  blocking collectives  14.4 us (76%)
  Pallas kernels  4.38 us (23%)
    all_to_all x1, blocking collectives, shards(): lax.all_to_all(partial, ('stn', 'chan'), split_axis=0, concat_axis=0, axi...  14.4 us
    pallas_call x1, Pallas kernels, shards(): pl.pallas_call(kernel, out_shape=pltpu.VMEM((n_stn * n_chan, rows, width)...  3.52 us
    pallas_call x1, Pallas kernels, shards(): pl.pallas_call(last_kernel, out_shape=jax.ShapeDtypeStruct((rows, 2 * sam...  0.86 us

profile of v22, /device:TPU:0, one launch (start us, length us, event | category | flops | bytes accessed | tf_op | source)
XLA Modules:
  0.0 18.8 jit_solution(6111426510576096575)
XLA Ops:
  0.0 3.5 %partial_tied.1 = bf16[32,2,768]{2,1,0:T(2,128)(2,1)S(1)} custom-call(bf16[24,2,16,2048]{3,2,1,0:T(8,128)(2,1)} %volt_hbm.1, bf16[24,2,2048]{2,1,0:T(2,128)(2,1)} %aw_hbm.1, bf16[24,2,128]{2,1,0:T(2,128)(2,1)} %sw_hbm.1, s32[1,128]{1,0:T(1,128)} %bitcast.8, s32[1,128]{1,0:T(1,128)} %bitcast.9, f32[2,128]{1,0:T(2,128)} %bitcast.6, f32[2,64]{1,0:T(2,128)} %bitcast.7, ...), custom_call_target="tpu_custom_call" | custom-call | tf_op jit(solution)/shard_map/partial_tied/pallas_call | solution.py:252
  3.5 14.4 %all_to_all.5.parts_ref = bf16[32,2,768]{2,1,0:T(2,128)(2,1)S(1)} all-to-all(bf16[32,2,768]{2,1,0:T(2,128)(2,1)S(1)} %partial_tied.1), channel_id=1, replica_groups={{31,30,29,28,27,26,25,24,23,22,21,20,19,18,17,16,15,14,13,12,11,10,9,8,..., dimensions={0} | all-to-all | bytes 196608 | tf_op jit(solution)/shard_map/all_to_all | solution.py:266
  18.0 0.9 %tied_beams.1 = bf16[2,32,48]{2,1,0:T(8,128)(2,1)} custom-call(bf16[32,2,768]{2,1,0:T(2,128)(2,1)S(1)} %all_to_all.5.parts_ref), custom_call_target="tpu_custom_call" | custom-call | tf_op jit(solution)/shard_map/tied_beams/pallas_call | solution.py:275

commit v23 on v18

--- a/solution.py
+++ b/solution.py
@@ -95,7 +95,7 @@
 
     def start(source, target, k):
         copy = pltpu.make_async_copy(source, target, sems.at[k])
-        copy.start()
+        copy.start(priority=int(k > groups))
         return copy
 
     def voltages(g):

time: 18.8 us -> 19.1 us (1.016)
  Pallas kernels: 4.11 us -> 4.38 us
    pallas_call x1, Pallas kernels: 3.25 us -> 3.52 us  [shards(): pl.pallas_call(kernel, out_shape=pltpu.VMEM((n_stn * n_chan, rows, width)...]
where the time goes in v23:
time: 19.1 us; the launch traced here: 18.8 us
  blocking collectives  14.4 us (75%)
  Pallas kernels  4.38 us (23%)
    all_to_all x1, blocking collectives, shards(): lax.all_to_all(partial, ('stn', 'chan'), split_axis=0, concat_axis=0, axi...  14.4 us
    pallas_call x1, Pallas kernels, shards(): pl.pallas_call(kernel, out_shape=pltpu.VMEM((n_stn * n_chan, rows, width)...  3.52 us
    pallas_call x1, Pallas kernels, shards(): pl.pallas_call(last_kernel, out_shape=jax.ShapeDtypeStruct((rows, 2 * sam...  0.86 us

profile of v23, /device:TPU:0, one launch (start us, length us, event | category | flops | bytes accessed | tf_op | source)
XLA Modules:
  0.0 18.8 jit_solution(13803285567025730095)
XLA Ops:
  0.0 3.5 %partial_tied.1 = bf16[32,2,768]{2,1,0:T(2,128)(2,1)S(1)} custom-call(bf16[24,2,16,2048]{3,2,1,0:T(8,128)(2,1)} %volt_hbm.1, bf16[24,2,2048]{2,1,0:T(2,128)(2,1)} %aw_hbm.1, bf16[24,2,128]{2,1,0:T(2,128)(2,1)} %sw_hbm.1, s32[1,128]{1,0:T(1,128)} %bitcast.8, s32[1,128]{1,0:T(1,128)} %bitcast.9, f32[2,128]{1,0:T(2,128)} %bitcast.6, f32[2,64]{1,0:T(2,128)} %bitcast.7, ...), custom_call_target="tpu_custom_call" | custom-call | tf_op jit(solution)/shard_map/partial_tied/pallas_call | solution.py:253
  3.5 14.4 %all_to_all.5.parts_ref = bf16[32,2,768]{2,1,0:T(2,128)(2,1)S(1)} all-to-all(bf16[32,2,768]{2,1,0:T(2,128)(2,1)S(1)} %partial_tied.1), channel_id=1, replica_groups={{31,30,29,28,27,26,25,24,23,22,21,20,19,18,17,16,15,14,13,12,11,10,9,8,..., dimensions={0} | all-to-all | bytes 196608 | tf_op jit(solution)/shard_map/all_to_all | solution.py:267
  18.0 0.9 %tied_beams.1 = bf16[2,32,48]{2,1,0:T(8,128)(2,1)} custom-call(bf16[32,2,768]{2,1,0:T(2,128)(2,1)S(1)} %all_to_all.5.parts_ref), custom_call_target="tpu_custom_call" | custom-call | tf_op jit(solution)/shard_map/tied_beams/pallas_call | solution.py:276

commit v24 on v17

--- a/solution.py
+++ b/solution.py
@@ -24,13 +24,24 @@
     return lax.broadcasted_iota(jnp.int32, shape, dim)
 
 
+def exchange_order(devices):
+    bits = devices.bit_length() - 1
+    return [reversed_bits(devices - 1 - place, bits) for place in range(devices)]
+
+
+def reversed_bits(index, bits):
+    return sum((index >> bit & 1) << (bits - 1 - bit) for bit in range(bits))
+
+
 def beam_columns(order_ref, dir_ref, start, rows):
     beams = order_ref.shape[1]
-    each = beams // (lax.axis_size("stn") * lax.axis_size("chan"))
+    devices = lax.axis_size("stn") * lax.axis_size("chan")
+    each = beams // devices
     order = order_ref[...].astype(jnp.float32)
     lane = iota((rows, beams), 1)
     slot = iota((rows, beams), 0) + start
-    own = lane == beams - each - slot // each * each + slot % each
+    device = reversed_bits(devices - 1 - slot // each, devices.bit_length() - 1)
+    own = lane == device * each + slot % each
     ids = jnp.sum(jnp.where(own, order, 0.0), axis=1, keepdims=True)
     pick = lane.astype(jnp.float32) == ids
     east = jnp.sum(jnp.where(pick, dir_ref[0:1, :], 0.0), axis=1, keepdims=True)
@@ -208,16 +219,20 @@
 
 
 def last_kernel(parts_ref, out_ref):
-    n_stn, n_chan = lax.axis_size("stn"), lax.axis_size("chan")
+    n_chan = lax.axis_size("chan")
     own_beams, rows_c, total_chans = out_ref.shape
     channels = total_chans // n_chan
     width = channels * rows_c
-    parts = parts_ref[...].astype(jnp.float32).reshape(n_stn, n_chan, own_beams, width)
-    tied = jnp.sum(parts, axis=0)
+    parts = parts_ref[...].astype(jnp.float32)
+    order = exchange_order(parts_ref.shape[0])
+    tied = [
+        sum(parts[place] for place, device in enumerate(order) if device % n_chan == chan)
+        for chan in range(n_chan)
+    ]
     diagonal = iota((channels, width), 0) == iota((channels, width), 1) // rows_c
     spread = (iota((rows_c, width), 0) == iota((rows_c, width), 1) % rows_c).astype(jnp.bfloat16)
     for b in range(own_beams):
-        rows = [jnp.where(diagonal, tied[chan, b : b + 1], 0.0) for chan in reversed(range(n_chan))]
+        rows = [jnp.where(diagonal, tied[chan][b : b + 1], 0.0) for chan in range(n_chan)]
         rows = jnp.concatenate(rows, axis=0).astype(jnp.bfloat16)
         out_ref[b] = dot_nt(spread, rows).astype(jnp.bfloat16)
 
@@ -267,7 +282,7 @@
         ("stn", "chan"),
         split_axis=0,
         concat_axis=0,
-        axis_index_groups=[list(reversed(range(n_stn * n_chan)))],
+        axis_index_groups=[exchange_order(n_stn * n_chan)],
         tiled=True,
     )
     vmem = pl.BlockSpec(memory_space=pltpu.VMEM)

time: 18.6 us -> 19.2 us (1.032)
  blocking collectives: 14.4 us -> 15 us
    all_to_all x1, blocking collectives: 14.4 us -> 15 us  [shards(): lax.all_to_all(partial, ('stn', 'chan'), split_axis=0, concat_axis=0, axi...]
where the time goes in v24:
time: 19.2 us; the launch traced here: 19 us
  blocking collectives  15 us (78%)
  Pallas kernels  4 us (21%)
    all_to_all x1, blocking collectives, shards(): lax.all_to_all(partial, ('stn', 'chan'), split_axis=0, concat_axis=0, axi...  15 us
    pallas_call x1, Pallas kernels, shards(): pl.pallas_call(kernel, out_shape=pltpu.VMEM((n_stn * n_chan, rows, width)...  3.2 us
    pallas_call x1, Pallas kernels, shards(): pl.pallas_call(last_kernel, out_shape=jax.ShapeDtypeStruct((rows, 2 * sam...  0.79 us

profile of v24, /device:TPU:0, one launch (start us, length us, event | category | flops | bytes accessed | tf_op | source)
XLA Modules:
  0.0 19.0 jit_solution(3833712924866336329)
XLA Ops:
  0.0 3.2 %partial_tied.1 = bf16[32,2,768]{2,1,0:T(2,128)(2,1)S(1)} custom-call(bf16[24,2,16,2048]{3,2,1,0:T(8,128)(2,1)} %volt_hbm.1, bf16[24,2,2048]{2,1,0:T(2,128)(2,1)} %aw_hbm.1, bf16[24,2,128]{2,1,0:T(2,128)(2,1)} %sw_hbm.1, s32[1,128]{1,0:T(1,128)} %bitcast.8, s32[1,128]{1,0:T(1,128)} %bitcast.9, f32[2,128]{1,0:T(2,128)} %bitcast.6, f32[2,64]{1,0:T(2,128)} %bitcast.7, ...), custom_call_target="tpu_custom_call" | custom-call | tf_op jit(solution)/shard_map/partial_tied/pallas_call | solution.py:266
  3.2 15.0 %all_to_all.5.parts_ref = bf16[32,2,768]{2,1,0:T(2,128)(2,1)S(1)} all-to-all(bf16[32,2,768]{2,1,0:T(2,128)(2,1)S(1)} %partial_tied.1), channel_id=1, replica_groups={{31,15,23,7,27,11,19,3,29,13,21,5,25,9,17,1,30,14,22,6,26,10,18,2,28,12..., dimensions={0} | all-to-all | bytes 196608 | tf_op jit(solution)/shard_map/all_to_all | solution.py:280
  18.2 0.8 %tied_beams.1 = bf16[2,32,48]{2,1,0:T(8,128)(2,1)} custom-call(bf16[32,2,768]{2,1,0:T(2,128)(2,1)S(1)} %all_to_all.5.parts_ref), custom_call_target="tpu_custom_call" | custom-call | tf_op jit(solution)/shard_map/tied_beams/pallas_call | solution.py:289

commit v25 on v24

--- a/solution.py
+++ b/solution.py
@@ -24,24 +24,25 @@
     return lax.broadcasted_iota(jnp.int32, shape, dim)
 
 
-def exchange_order(devices):
-    bits = devices.bit_length() - 1
-    return [reversed_bits(devices - 1 - place, bits) for place in range(devices)]
-
-
-def reversed_bits(index, bits):
-    return sum((index >> bit & 1) << (bits - 1 - bit) for bit in range(bits))
+def exchange_order(n_stn, n_chan):
+    def key(device):
+        stn = device // n_chan
+        return device == n_chan, 2 * (stn // 4) + 3 * (stn % 2) if device else -1, device
+
+    return sorted(range(n_stn * n_chan), key=key, reverse=True)
 
 
 def beam_columns(order_ref, dir_ref, start, rows):
     beams = order_ref.shape[1]
-    devices = lax.axis_size("stn") * lax.axis_size("chan")
-    each = beams // devices
+    n_stn, n_chan = lax.axis_size("stn"), lax.axis_size("chan")
+    each = beams // (n_stn * n_chan)
     order = order_ref[...].astype(jnp.float32)
     lane = iota((rows, beams), 1)
-    slot = iota((rows, beams), 0) + start
-    device = reversed_bits(devices - 1 - slot // each, devices.bit_length() - 1)
-    own = lane == device * each + slot % each
+    slot = iota((rows, 1), 0) + start
+    own_row = jnp.zeros((rows, 1), jnp.int32)
+    for place, device in enumerate(exchange_order(n_stn, n_chan)):
+        own_row = jnp.where(slot // each == place, device * each + slot % each, own_row)
+    own = lane == own_row
     ids = jnp.sum(jnp.where(own, order, 0.0), axis=1, keepdims=True)
     pick = lane.astype(jnp.float32) == ids
     east = jnp.sum(jnp.where(pick, dir_ref[0:1, :], 0.0), axis=1, keepdims=True)
@@ -224,7 +225,7 @@
     channels = total_chans // n_chan
     width = channels * rows_c
     parts = parts_ref[...].astype(jnp.float32)
-    order = exchange_order(parts_ref.shape[0])
+    order = exchange_order(lax.axis_size("stn"), n_chan)
     tied = [
         sum(parts[place] for place, device in enumerate(order) if device % n_chan == chan)
         for chan in range(n_chan)
@@ -282,7 +283,7 @@
         ("stn", "chan"),
         split_axis=0,
         concat_axis=0,
-        axis_index_groups=[exchange_order(n_stn * n_chan)],
+        axis_index_groups=[exchange_order(n_stn, n_chan)],
         tiled=True,
     )
     vmem = pl.BlockSpec(memory_space=pltpu.VMEM)

time: 19.2 us -> 18.8 us (0.979)
  blocking collectives: 15 us -> 14.6 us
    all_to_all x1, blocking collectives: 15 us -> 14.6 us  [shards(): lax.all_to_all(partial, ('stn', 'chan'), split_axis=0, concat_axis=0, axi...]
where the time goes in v25:
time: 18.8 us; the launch traced here: 18.6 us
  blocking collectives  14.6 us (78%)
  Pallas kernels  4 us (21%)
    all_to_all x1, blocking collectives, shards(): lax.all_to_all(partial, ('stn', 'chan'), split_axis=0, concat_axis=0, axi...  14.6 us
    pallas_call x1, Pallas kernels, shards(): pl.pallas_call(kernel, out_shape=pltpu.VMEM((n_stn * n_chan, rows, width)...  3.2 us
    pallas_call x1, Pallas kernels, shards(): pl.pallas_call(last_kernel, out_shape=jax.ShapeDtypeStruct((rows, 2 * sam...  0.8 us

profile of v25, /device:TPU:0, one launch (start us, length us, event | category | flops | bytes accessed | tf_op | source)
XLA Modules:
  0.0 18.6 jit_solution(7008747623774223377)
XLA Ops:
  0.0 3.2 %partial_tied.1 = bf16[32,2,768]{2,1,0:T(2,128)(2,1)S(1)} custom-call(bf16[24,2,16,2048]{3,2,1,0:T(8,128)(2,1)} %volt_hbm.1, bf16[24,2,2048]{2,1,0:T(2,128)(2,1)} %aw_hbm.1, bf16[24,2,128]{2,1,0:T(2,128)(2,1)} %sw_hbm.1, s32[1,128]{1,0:T(1,128)} %bitcast.8, s32[1,128]{1,0:T(1,128)} %bitcast.9, f32[2,128]{1,0:T(2,128)} %bitcast.6, f32[2,64]{1,0:T(2,128)} %bitcast.7, ...), custom_call_target="tpu_custom_call" | custom-call | tf_op jit(solution)/shard_map/partial_tied/pallas_call | solution.py:267
  3.2 14.6 %all_to_all.5.parts_ref = bf16[32,2,768]{2,1,0:T(2,128)(2,1)S(1)} all-to-all(bf16[32,2,768]{2,1,0:T(2,128)(2,1)S(1)} %partial_tied.1), channel_id=1, replica_groups={{2,31,30,27,26,23,22,19,18,29,28,25,24,15,14,11,10,21,20,17,16,7,6,3,13..., dimensions={0} | all-to-all | bytes 196608 | tf_op jit(solution)/shard_map/all_to_all | solution.py:281
  17.8 0.8 %tied_beams.1 = bf16[2,32,48]{2,1,0:T(8,128)(2,1)} custom-call(bf16[32,2,768]{2,1,0:T(2,128)(2,1)S(1)} %all_to_all.5.parts_ref), custom_call_target="tpu_custom_call" | custom-call | tf_op jit(solution)/shard_map/tied_beams/pallas_call | solution.py:290

commit v26 on v20

--- a/solution.py
+++ b/solution.py
@@ -81,7 +81,8 @@
     dir_ref,
     order_ref,
     tied_ref,
-    sum_ref,
+    spread_ref,
+    weights_ref,
     sems,
 ):
     channels, _, samples, antennas = volt_hbm.shape
@@ -103,37 +104,74 @@
         return volt_hbm.at[part], volts.at[part]
 
     pairs = [
+        (aw_hbm, aw_ref),
+        (sw_hbm, sw_ref),
+        (ts_hbm, ts_ref),
         voltages(0),
-        (aw_hbm, aw_ref),
         (order_hbm, order_ref),
         (dir_hbm, dir_ref),
         (pos_hbm, pos_ref),
         (group_hbm, group_ref),
-        (ts_hbm, ts_ref),
-        (sw_hbm, sw_ref),
     ] + [voltages(g) for g in range(1, groups)]
     copies = [start(source, target, k) for k, (source, target) in enumerate(pairs)]
-    large = copies[:1] + copies[8:]
-    antenna_tile = iota((antennas, tiles), 0) // TILE_ANTENNAS == iota((antennas, tiles), 1)
-    sum_ref[...] = antenna_tile.astype(jnp.bfloat16)
-    for copy in copies[:2]:
+    large = copies[3:4] + copies[8:]
+    tile_of = iota((tiles, antennas), 1) // TILE_ANTENNAS == iota((tiles, antennas), 0)
+    spread_ref[...] = tile_of.astype(jnp.bfloat16)
+    own_channel = iota((CB * rows_c, lanes), 0) // rows_c == iota((CB * rows_c, lanes), 1) // (
+        2 * stations
+    )
+    imag_row = iota((CB * rows_c, lanes), 0) // samples % 2
+    imag_lane = iota((CB * rows_c, lanes), 1) // stations % 2
+    sign = jnp.where(imag_row == imag_lane, -1.0, 1.0)
+    for copy in copies[:3]:
         copy.wait()
 
-    def tile_beams(g):
-        products = []
-        for c in range(CB):
-            w_re = jnp.broadcast_to(aw_ref[g * CB + c, 0:1], (samples, antennas))
-            w_im = jnp.broadcast_to(aw_ref[g * CB + c, 1:2], (samples, antennas))
-            v_re, v_im = volts[g * CB + c, 0], volts[g * CB + c, 1]
-            products.append(w_re * v_re - w_im * v_im)
-            products.append(w_re * v_im + w_im * v_re)
-        return jnp.dot(
-            jnp.concatenate(products, axis=0), sum_ref[...], preferred_element_type=jnp.float32
-        ).astype(jnp.bfloat16)
-
-    last = tile_beams(0)
-    for copy in copies[2:9]:
-        copy.wait()
+    member_table = (iota((stations, tiles), 0) == ts_ref[...] % stations).astype(jnp.float32)
+    swt = sw_ref[...].astype(jnp.float32)
+    rows = jnp.concatenate([swt[c] for c in range(channels)] + [member_table], axis=0)
+    spread = jnp.dot(
+        rows.astype(jnp.bfloat16), spread_ref[...], preferred_element_type=jnp.float32
+    )
+    member = spread[2 * channels :]
+
+    def station_weights(g):
+        out = []
+        for c in range(g * CB, (g + 1) * CB):
+            antenna = aw_ref[c].astype(jnp.float32)
+            a_re, a_im = antenna[0:1], antenna[1:2]
+            s_re = spread[2 * c : 2 * c + 1] * member
+            s_im = spread[2 * c + 1 : 2 * c + 2] * member
+            out += [s_re * a_re - s_im * a_im, s_re * a_im + s_im * a_re]
+        weights_ref[g] = jnp.concatenate(out, axis=0).astype(jnp.bfloat16)
+
+    def products(g):
+        left = volts[g * CB : (g + 1) * CB].reshape(CB * rows_c, antennas)
+        return dot_nt(left, weights_ref[g])
+
+    def tied_beams(g, product):
+        other = product.reshape(CB, 2, samples, lanes)
+        other = jnp.concatenate([other[:, 1:], other[:, :1]], axis=1).reshape(CB * rows_c, lanes)
+        other = jnp.where(
+            imag_lane == 0,
+            pltpu.roll(other, lanes - stations, 1),
+            pltpu.roll(other, stations, 1),
+        )
+        station = jnp.where(own_channel, product + sign * other, 0.0).astype(jnp.bfloat16)
+        tied = dot_nt(tied_ref[:, g * lanes : (g + 1) * lanes], station)
+        devices, rows, _ = out_ref.shape
+        out_ref[:, :, g * CB * rows_c : (g + 1) * CB * rows_c] = tied.astype(jnp.bfloat16).reshape(
+            devices, rows, CB * rows_c
+        )
+
+    station_weights(0)
+    found = []
+    for g in range(groups - 1):
+        large[g].wait()
+        if g == groups - 2:
+            for copy in copies[4:8]:
+                copy.wait()
+        found.append(products(g))
+        station_weights(g + 1)
 
     east_s, north_s, group_s = station_rows(pos_ref, group_ref, stations, lanes)
     lane = iota((1, lanes), 1)
@@ -164,46 +202,10 @@
 
         lax.fori_loop(0, beams // block, body, 0)
 
-    member_table = (iota((stations, tiles), 0) == ts_ref[...] % stations).astype(jnp.float32)
-    own_channel = iota((lanes, CB * rows_c), 0) // (2 * stations) == iota(
-        (lanes, CB * rows_c), 1
-    ) // rows_c
-
-    station_rows_of = []
+    large[-1].wait()
+    found.append(products(groups - 1))
     for g in range(groups):
-        swt = sw_ref[g * CB : (g + 1) * CB].astype(jnp.float32)
-        right = []
-        for c in range(CB):
-            re = swt[c, 0:1] * member_table
-            im = swt[c, 1:2] * member_table
-            right.append(jnp.concatenate([re, -im], axis=1))
-            right.append(jnp.concatenate([im, re], axis=1))
-        station_rows_of.append(jnp.concatenate(right, axis=0).astype(jnp.bfloat16))
-
-    def tied_beams(g, beams_tile):
-        left = []
-        for c in range(CB):
-            tile_re = beams_tile[c * rows_c : c * rows_c + samples]
-            tile_im = beams_tile[c * rows_c + samples : (c + 1) * rows_c]
-            left.append(jnp.concatenate([tile_re, tile_im], axis=1))
-            left.append(jnp.concatenate([tile_im, -tile_re], axis=1))
-        station = dot_nt(station_rows_of[g], jnp.concatenate(left, axis=0))
-        station = jnp.where(own_channel, station, 0.0).astype(jnp.bfloat16)
-        tied = jnp.dot(
-            tied_ref[:, g * lanes : (g + 1) * lanes], station, preferred_element_type=jnp.float32
-        )
-        devices, rows, _ = out_ref.shape
-        out_ref[:, :, g * CB * rows_c : (g + 1) * CB * rows_c] = tied.astype(jnp.bfloat16).reshape(
-            devices, rows, CB * rows_c
-        )
-
-    for g in range(1, groups):
-        if g > 1:
-            large[g].wait()
-        now = tile_beams(g)
-        tied_beams(g - 1, last)
-        last = now
-    tied_beams(groups - 1, last)
+        tied_beams(g, found[g])
 
 
 def last_kernel(parts_ref, out_ref):
@@ -211,12 +213,12 @@
     own_beams, rows_c, total_chans = out_ref.shape
     channels = total_chans // n_chan
     width = channels * rows_c
-    parts = parts_ref[...].astype(jnp.float32).reshape(n_stn, n_chan, own_beams, width)
-    tied = jnp.sum(parts, axis=0)
+    parts = parts_ref[...].astype(jnp.float32)
+    tied = [sum(parts[n_chan - 1 - chan + k * n_chan] for k in range(n_stn)) for chan in range(n_chan)]
     diagonal = iota((channels, width), 0) == iota((channels, width), 1) // rows_c
     spread = (iota((rows_c, width), 0) == iota((rows_c, width), 1) % rows_c).astype(jnp.bfloat16)
     for b in range(own_beams):
-        rows = [jnp.where(diagonal, tied[chan, b : b + 1], 0.0) for chan in reversed(range(n_chan))]
+        rows = [jnp.where(diagonal, tied[chan][b : b + 1], 0.0) for chan in range(n_chan)]
         rows = jnp.concatenate(rows, axis=0).astype(jnp.bfloat16)
         out_ref[b] = dot_nt(spread, rows).astype(jnp.bfloat16)
 
@@ -255,7 +257,11 @@
         scratch_shapes=[pltpu.VMEM(x.shape, x.dtype) for x in operands]
         + [
             pltpu.VMEM((beams, channels * 2 * (station_weights.shape[2] // TPS)), jnp.bfloat16),
-            pltpu.VMEM((volts.shape[3], station_weights.shape[2]), jnp.bfloat16),
+            pltpu.VMEM((station_weights.shape[2], volts.shape[3]), jnp.bfloat16),
+            pltpu.VMEM(
+                (channels // CB, CB * 2 * (station_weights.shape[2] // TPS), volts.shape[3]),
+                jnp.bfloat16,
+            ),
             pltpu.SemaphoreType.DMA((len(operands) - 1 + channels // CB,)),
         ],
         compiler_params=pltpu.CompilerParams(vmem_limit_bytes=24 * 2**20),

time: 18.7 us -> 19.4 us (1.037)
  Pallas kernels: 4.05 us -> 4.83 us
    pallas_call x1, Pallas kernels: 3.19 us -> 4.03 us  [shards(): pl.pallas_call(kernel, out_shape=pltpu.VMEM((n_stn * n_chan, rows, width)...]
where the time goes in v26:
time: 19.4 us; the launch traced here: 19.3 us
  blocking collectives  14.4 us (74%)
  Pallas kernels  4.83 us (25%)
    all_to_all x1, blocking collectives, shards(): lax.all_to_all(partial, ('stn', 'chan'), split_axis=0, concat_axis=0, axi...  14.4 us
    pallas_call x1, Pallas kernels, shards(): pl.pallas_call(kernel, out_shape=pltpu.VMEM((n_stn * n_chan, rows, width)...  4.03 us
    pallas_call x1, Pallas kernels, shards(): pl.pallas_call(last_kernel, out_shape=jax.ShapeDtypeStruct((rows, 2 * sam...  0.8 us

profile of v26, /device:TPU:0, one launch (start us, length us, event | category | flops | bytes accessed | tf_op | source)
XLA Modules:
  0.0 19.3 jit_solution(10062511526401856235)
XLA Ops:
  0.0 4.0 %partial_tied.1 = bf16[32,2,768]{2,1,0:T(2,128)(2,1)S(1)} custom-call(bf16[24,2,16,2048]{3,2,1,0:T(8,128)(2,1)} %volt_hbm.1, bf16[24,2,2048]{2,1,0:T(2,128)(2,1)} %aw_hbm.1, bf16[24,2,128]{2,1,0:T(2,128)(2,1)} %sw_hbm.1, s32[1,128]{1,0:T(1,128)} %bitcast.8, s32[1,128]{1,0:T(1,128)} %bitcast.9, f32[2,128]{1,0:T(2,128)} %bitcast.6, f32[2,64]{1,0:T(2,128)} %bitcast.7, ...), custom_call_target="tpu_custom_call" | custom-call | tf_op jit(solution)/shard_map/partial_tied/pallas_call | solution.py:252
  4.0 14.4 %all_to_all.5.parts_ref = bf16[32,2,768]{2,1,0:T(2,128)(2,1)S(1)} all-to-all(bf16[32,2,768]{2,1,0:T(2,128)(2,1)S(1)} %partial_tied.1), channel_id=1, replica_groups={{31,30,29,28,27,26,25,24,23,22,21,20,19,18,17,16,15,14,13,12,11,10,9,8,..., dimensions={0} | all-to-all | bytes 196608 | tf_op jit(solution)/shard_map/all_to_all | solution.py:270
  18.5 0.8 %tied_beams.1 = bf16[2,32,48]{2,1,0:T(8,128)(2,1)} custom-call(bf16[32,2,768]{2,1,0:T(2,128)(2,1)S(1)} %all_to_all.5.parts_ref), custom_call_target="tpu_custom_call" | custom-call | tf_op jit(solution)/shard_map/tied_beams/pallas_call | solution.py:279

commit v27 on v17

--- a/solution.py
+++ b/solution.py
@@ -12,6 +12,7 @@
 TPS = 16
 GROUPS = 4
 CB = 8
+CHUNK = 256
 NT = (((1,), (1,)), ((), ()))
 SIN = [(-1) ** i * (2 * math.pi) ** (2 * i + 1) / math.factorial(2 * i + 1) for i in range(7)]
 
@@ -81,7 +82,6 @@
     dir_ref,
     order_ref,
     tied_ref,
-    sum_ref,
     sems,
 ):
     channels, _, samples, antennas = volt_hbm.shape
@@ -114,8 +114,8 @@
     ] + [voltages(g) for g in range(1, groups)]
     copies = [start(source, target, k) for k, (source, target) in enumerate(pairs)]
     large = copies[:1] + copies[8:]
-    antenna_tile = iota((antennas, tiles), 0) // TILE_ANTENNAS == iota((antennas, tiles), 1)
-    sum_ref[...] = antenna_tile.astype(jnp.bfloat16)
+    antenna_tile = iota((CHUNK // TILE_ANTENNAS, CHUNK), 1) // TILE_ANTENNAS
+    sum_tile = (antenna_tile == iota(antenna_tile.shape, 0)).astype(jnp.bfloat16)
     for copy in copies[:2]:
         copy.wait()
 
@@ -128,9 +128,12 @@
             v_re, v_im = volts[g * CB + c, 0], volts[g * CB + c, 1]
             products.append(w_re * v_re - w_im * v_im)
             products.append(w_re * v_im + w_im * v_re)
-        return jnp.dot(
-            jnp.concatenate(products, axis=0), sum_ref[...], preferred_element_type=jnp.float32
-        ).astype(jnp.bfloat16)
+        products = jnp.concatenate(products, axis=0)
+        sums = [
+            dot_nt(sum_tile, products[:, first : first + CHUNK])
+            for first in range(0, antennas, CHUNK)
+        ]
+        return jnp.concatenate(sums, axis=0)
 
     last = tile_beams(0)
     for copy in copies[2:9]:
@@ -170,6 +173,7 @@
         (lanes, CB * rows_c), 1
     ) // rows_c
 
+    imag_column = iota((tiles, CB * rows_c), 1) // samples % 2 == 1
     station_rows_of = []
     for g in range(groups):
         swt = sw_ref[g * CB : (g + 1) * CB].astype(jnp.float32)
@@ -182,13 +186,14 @@
         station_rows_of.append(jnp.concatenate(right, axis=0).astype(jnp.bfloat16))
 
     def tied_beams(g, beams_tile):
-        left = []
-        for c in range(CB):
-            tile_re = beams_tile[c * rows_c : c * rows_c + samples]
-            tile_im = beams_tile[c * rows_c + samples : (c + 1) * rows_c]
-            left.append(jnp.concatenate([tile_re, tile_im], axis=1))
-            left.append(jnp.concatenate([tile_im, -tile_re], axis=1))
-        station = dot_nt(station_rows_of[g], jnp.concatenate(left, axis=0))
+        width = CB * rows_c
+        other = jnp.where(
+            imag_column,
+            -pltpu.roll(beams_tile, samples, 1),
+            pltpu.roll(beams_tile, width - samples, 1),
+        )
+        left = jnp.concatenate([beams_tile, other], axis=0).astype(jnp.bfloat16)
+        station = jnp.dot(station_rows_of[g], left, preferred_element_type=jnp.float32)
         station = jnp.where(own_channel, station, 0.0).astype(jnp.bfloat16)
         tied = jnp.dot(
             tied_ref[:, g * lanes : (g + 1) * lanes], station, preferred_element_type=jnp.float32
@@ -212,12 +217,12 @@
     own_beams, rows_c, total_chans = out_ref.shape
     channels = total_chans // n_chan
     width = channels * rows_c
-    parts = parts_ref[...].astype(jnp.float32).reshape(n_stn, n_chan, own_beams, width)
-    tied = jnp.sum(parts, axis=0)
+    parts = parts_ref[...].astype(jnp.float32)
+    tied = [sum(parts[n_chan - 1 - chan + k * n_chan] for k in range(n_stn)) for chan in range(n_chan)]
     diagonal = iota((channels, width), 0) == iota((channels, width), 1) // rows_c
     spread = (iota((rows_c, width), 0) == iota((rows_c, width), 1) % rows_c).astype(jnp.bfloat16)
     for b in range(own_beams):
-        rows = [jnp.where(diagonal, tied[chan, b : b + 1], 0.0) for chan in reversed(range(n_chan))]
+        rows = [jnp.where(diagonal, tied[chan][b : b + 1], 0.0) for chan in range(n_chan)]
         rows = jnp.concatenate(rows, axis=0).astype(jnp.bfloat16)
         out_ref[b] = dot_nt(spread, rows).astype(jnp.bfloat16)
 
@@ -256,7 +261,6 @@
         scratch_shapes=[pltpu.VMEM(x.shape, x.dtype) for x in operands]
         + [
             pltpu.VMEM((beams, channels * 2 * (station_weights.shape[2] // TPS)), jnp.bfloat16),
-            pltpu.VMEM((volts.shape[3], station_weights.shape[2]), jnp.bfloat16),
             pltpu.SemaphoreType.DMA((len(operands) - 1 + channels // CB,)),
         ],
         compiler_params=pltpu.CompilerParams(vmem_limit_bytes=24 * 2**20),

time: 18.6 us -> 18.6 us (level)
  no operation moved by 1% of the time
where the time goes in v27:
time: 18.6 us; the launch traced here: 18.4 us
  blocking collectives  14.4 us (77%)
  Pallas kernels  3.99 us (21%)
    all_to_all x1, blocking collectives, shards(): lax.all_to_all(partial, ('stn', 'chan'), split_axis=0, concat_axis=0, axi...  14.4 us
    pallas_call x1, Pallas kernels, shards(): pl.pallas_call(kernel, out_shape=pltpu.VMEM((n_stn * n_chan, rows, width)...  3.2 us
    pallas_call x1, Pallas kernels, shards(): pl.pallas_call(last_kernel, out_shape=jax.ShapeDtypeStruct((rows, 2 * sam...  0.79 us

profile of v27, /device:TPU:0, one launch (start us, length us, event | category | flops | bytes accessed | tf_op | source)
XLA Modules:
  0.0 18.4 jit_solution(14636346628814180344)
XLA Ops:
  0.0 3.2 %partial_tied.1 = bf16[32,2,768]{2,1,0:T(2,128)(2,1)S(1)} custom-call(bf16[24,2,16,2048]{3,2,1,0:T(8,128)(2,1)} %volt_hbm.1, bf16[24,2,2048]{2,1,0:T(2,128)(2,1)} %aw_hbm.1, bf16[24,2,128]{2,1,0:T(2,128)(2,1)} %sw_hbm.1, s32[1,128]{1,0:T(1,128)} %bitcast.8, s32[1,128]{1,0:T(1,128)} %bitcast.9, f32[2,128]{1,0:T(2,128)} %bitcast.6, f32[2,64]{1,0:T(2,128)} %bitcast.7, ...), custom_call_target="tpu_custom_call" | custom-call | tf_op jit(solution)/shard_map/partial_tied/pallas_call | solution.py:256
  3.2 14.4 %all_to_all.5.parts_ref = bf16[32,2,768]{2,1,0:T(2,128)(2,1)S(1)} all-to-all(bf16[32,2,768]{2,1,0:T(2,128)(2,1)S(1)} %partial_tied.1), channel_id=1, replica_groups={{31,30,29,28,27,26,25,24,23,22,21,20,19,18,17,16,15,14,13,12,11,10,9,8,..., dimensions={0} | all-to-all | bytes 196608 | tf_op jit(solution)/shard_map/all_to_all | solution.py:269
  17.6 0.8 %tied_beams.1 = bf16[2,32,48]{2,1,0:T(8,128)(2,1)} custom-call(bf16[32,2,768]{2,1,0:T(2,128)(2,1)S(1)} %all_to_all.5.parts_ref), custom_call_target="tpu_custom_call" | custom-call | tf_op jit(solution)/shard_map/tied_beams/pallas_call | solution.py:278

commit v28 on v27

--- a/solution.py
+++ b/solution.py
@@ -84,8 +84,9 @@
     tied_ref,
     sems,
 ):
-    channels, _, samples, antennas = volt_hbm.shape
-    tiles = sw_ref.shape[2]
+    channels, _, tiles = sw_ref.shape
+    antennas = volt_hbm.shape[1]
+    samples = volt_hbm.shape[0] // (2 * channels)
     stations = tiles // TPS
     groups = channels // CB
     rows_c = 2 * samples
@@ -99,7 +100,7 @@
         return copy
 
     def voltages(g):
-        part = pl.ds(g * CB, CB)
+        part = pl.ds(g * CB * rows_c, CB * rows_c)
         return volt_hbm.at[part], volts.at[part]
 
     pairs = [
@@ -125,7 +126,8 @@
         for c in range(CB):
             w_re = jnp.broadcast_to(weights[c, 0:1], (samples, antennas)).astype(jnp.bfloat16)
             w_im = jnp.broadcast_to(weights[c, 1:2], (samples, antennas)).astype(jnp.bfloat16)
-            v_re, v_im = volts[g * CB + c, 0], volts[g * CB + c, 1]
+            first = (g * CB + c) * rows_c
+            v_re, v_im = volts[first : first + samples], volts[first + samples : first + rows_c]
             products.append(w_re * v_re - w_im * v_im)
             products.append(w_re * v_im + w_im * v_re)
         products = jnp.concatenate(products, axis=0)
@@ -243,7 +245,7 @@
     rows = beams // (n_stn * n_chan)
     width = channels * 2 * samples
     operands = (
-        volts,
+        volts.reshape(-1, volts.shape[3]),
         antenna_tile_weights,
         station_weights,
         tile_station[None, :],

time: 18.6 us -> 18.6 us (level)
  no operation moved by 1% of the time
where the time goes in v28:
time: 18.6 us; the launch traced here: 18.4 us
  blocking collectives  14.4 us (77%)
  Pallas kernels  3.99 us (21%)
    all_to_all x1, blocking collectives, shards(): lax.all_to_all(partial, ('stn', 'chan'), split_axis=0, concat_axis=0, axi...  14.4 us
    pallas_call x1, Pallas kernels, shards(): pl.pallas_call(kernel, out_shape=pltpu.VMEM((n_stn * n_chan, rows, width)...  3.2 us
    pallas_call x1, Pallas kernels, shards(): pl.pallas_call(last_kernel, out_shape=jax.ShapeDtypeStruct((rows, 2 * sam...  0.79 us

profile of v28, /device:TPU:0, one launch (start us, length us, event | category | flops | bytes accessed | tf_op | source)
XLA Modules:
  0.0 18.4 jit_solution(14636346628814180344)
XLA Ops:
  0.0 3.2 %partial_tied.1 = bf16[32,2,768]{2,1,0:T(2,128)(2,1)S(1)} custom-call(bf16[768,2048]{1,0:T(8,128)(2,1)} %bitcast.7, bf16[24,2,2048]{2,1,0:T(2,128)(2,1)} %aw_hbm.1, bf16[24,2,128]{2,1,0:T(2,128)(2,1)} %sw_hbm.1, s32[1,128]{1,0:T(1,128)} %bitcast.10, s32[1,128]{1,0:T(1,128)} %bitcast.11, f32[2,128]{1,0:T(2,128)} %bitcast.8, f32[2,64]{1,0:T(2,128)} %bitcast.9, ...), custom_call_target="tpu_custom_call" | custom-call | tf_op jit(solution)/shard_map/partial_tied/pallas_call | solution.py:258
  3.2 14.4 %all_to_all.5.parts_ref = bf16[32,2,768]{2,1,0:T(2,128)(2,1)S(1)} all-to-all(bf16[32,2,768]{2,1,0:T(2,128)(2,1)S(1)} %partial_tied.1), channel_id=1, replica_groups={{31,30,29,28,27,26,25,24,23,22,21,20,19,18,17,16,15,14,13,12,11,10,9,8,..., dimensions={0} | all-to-all | bytes 196608 | tf_op jit(solution)/shard_map/all_to_all | solution.py:271
  17.6 0.8 %tied_beams.1 = bf16[2,32,48]{2,1,0:T(8,128)(2,1)} custom-call(bf16[32,2,768]{2,1,0:T(2,128)(2,1)S(1)} %all_to_all.5.parts_ref), custom_call_target="tpu_custom_call" | custom-call | tf_op jit(solution)/shard_map/tied_beams/pallas_call | solution.py:280

commit v29 on v28

--- a/solution.py
+++ b/solution.py
@@ -82,52 +82,90 @@
     dir_ref,
     order_ref,
     tied_ref,
+    station_ref,
+    tile_ref,
     sems,
 ):
     channels, _, tiles = sw_ref.shape
-    antennas = volt_hbm.shape[1]
-    samples = volt_hbm.shape[0] // (2 * channels)
+    groups, rows_g, antennas = volt_hbm.shape
     stations = tiles // TPS
-    groups = channels // CB
-    rows_c = 2 * samples
+    rows_c = rows_g // CB
+    samples = rows_c // 2
     beams = order_ref.shape[1]
     lanes = CB * 2 * stations
     scale = 1.0 / math.sqrt(group_ref.shape[1])
 
-    def start(source, target, k):
-        copy = pltpu.make_async_copy(source, target, sems.at[k])
-        copy.start()
-        return copy
-
-    def voltages(g):
-        part = pl.ds(g * CB * rows_c, CB * rows_c)
-        return volt_hbm.at[part], volts.at[part]
-
-    pairs = [
-        voltages(0),
-        (aw_hbm, aw_ref),
+    small = [
         (order_hbm, order_ref),
         (dir_hbm, dir_ref),
         (pos_hbm, pos_ref),
         (group_hbm, group_ref),
         (ts_hbm, ts_ref),
         (sw_hbm, sw_ref),
-    ] + [voltages(g) for g in range(1, groups)]
-    copies = [start(source, target, k) for k, (source, target) in enumerate(pairs)]
-    large = copies[:1] + copies[8:]
+        (aw_hbm, aw_ref),
+    ]
+    small = [pltpu.make_async_copy(*pair, sems.at[k]) for k, pair in enumerate(small)]
+
+    def voltages(g):
+        return pltpu.make_async_copy(volt_hbm.at[g], volts.at[g], sems.at[len(small) + g])
+
+    for copy in small[:4] + [voltages(0)] + small[4:] + [voltages(g) for g in range(1, groups)]:
+        copy.start()
     antenna_tile = iota((CHUNK // TILE_ANTENNAS, CHUNK), 1) // TILE_ANTENNAS
     sum_tile = (antenna_tile == iota(antenna_tile.shape, 0)).astype(jnp.bfloat16)
-    for copy in copies[:2]:
+    own_channel = iota((lanes, rows_g), 0) // (2 * stations) == iota((lanes, rows_g), 1) // rows_c
+    imag_column = iota((tiles, rows_g), 1) // samples % 2 == 1
+    tile_ref[...] = jnp.zeros_like(tile_ref)
+    for copy in small:
         copy.wait()
+
+    east_s, north_s, group_s = station_rows(pos_ref, group_ref, stations, lanes)
+    lane = iota((1, lanes), 1)
+    channel_lane = lane // (2 * stations)
+    quarter = 0.25 * ((lane // stations) % 2).astype(jnp.float32)
+    first_chan = lax.axis_index("chan") * channels
+    total_chans = channels * lax.axis_size("chan")
+    block = min(64, beams)
+
+    def tied_rows(i, carry):
+        first = pl.multiple_of(i * block, block)
+        east, north, group = beam_columns(order_ref, dir_ref, first, block)
+        delay = east * east_s + north * north_s
+        member = jnp.where(group == group_s, scale, 0.0)
+
+        def tied_group(g, carry):
+            freq = 1.0 + (first_chan + g * CB + channel_lane).astype(jnp.float32) / total_chans
+            wave = cos_turns(delay * freq - quarter)
+            tied_ref[g, pl.ds(first, block), :] = (wave * member).astype(jnp.bfloat16)
+            return carry
+
+        return lax.fori_loop(0, groups, tied_group, carry)
+
+    lax.fori_loop(0, beams // block, tied_rows, 0)
+    member_table = (iota((stations, tiles), 0) == ts_ref[...] % stations).astype(jnp.float32)
+
+    def station_group(g, carry):
+        swt = sw_ref[pl.ds(g * CB, CB)].astype(jnp.float32)
+        right = []
+        for c in range(CB):
+            re = swt[c, 0:1] * member_table
+            im = swt[c, 1:2] * member_table
+            right.append(jnp.concatenate([re, -im], axis=1))
+            right.append(jnp.concatenate([im, re], axis=1))
+        station_ref[g] = jnp.concatenate(right, axis=0).astype(jnp.bfloat16)
+        return carry
+
+    lax.fori_loop(0, groups, station_group, 0)
 
     def tile_beams(g):
         products = []
-        weights = aw_ref[g * CB : (g + 1) * CB].astype(jnp.float32)
+        weights = aw_ref[pl.ds(g * CB, CB)].astype(jnp.float32)
         for c in range(CB):
             w_re = jnp.broadcast_to(weights[c, 0:1], (samples, antennas)).astype(jnp.bfloat16)
             w_im = jnp.broadcast_to(weights[c, 1:2], (samples, antennas)).astype(jnp.bfloat16)
-            first = (g * CB + c) * rows_c
-            v_re, v_im = volts[first : first + samples], volts[first + samples : first + rows_c]
+            first = c * rows_c
+            v_re = volts[g, first : first + samples]
+            v_im = volts[g, first + samples : first + rows_c]
             products.append(w_re * v_re - w_im * v_im)
             products.append(w_re * v_im + w_im * v_re)
         products = jnp.concatenate(products, axis=0)
@@ -137,81 +175,29 @@
         ]
         return jnp.concatenate(sums, axis=0)
 
-    last = tile_beams(0)
-    for copy in copies[2:9]:
-        copy.wait()
-
-    east_s, north_s, group_s = station_rows(pos_ref, group_ref, stations, lanes)
-    lane = iota((1, lanes), 1)
-    channel_lane = lane // (2 * stations)
-    quarter = 0.25 * ((lane // stations) % 2).astype(jnp.float32)
-    first_chan = lax.axis_index("chan") * channels
-    total_chans = channels * lax.axis_size("chan")
-    block = min(64, beams)
-
-    def tied_rows(first):
-        east, north, group = beam_columns(order_ref, dir_ref, first, block)
-        delay = east * east_s + north * north_s
-        member = jnp.where(group == group_s, scale, 0.0)
-        for g in range(groups):
-            freq = 1.0 + (first_chan + g * CB + channel_lane).astype(jnp.float32) / total_chans
-            wave = cos_turns(delay * freq - quarter)
-            tied_ref[pl.ds(first, block), g * lanes : (g + 1) * lanes] = (wave * member).astype(
-                jnp.bfloat16
-            )
-
-    if beams == block:
-        tied_rows(0)
-    else:
-
-        def body(i, carry):
-            tied_rows(pl.multiple_of(i * block, block))
-            return carry
-
-        lax.fori_loop(0, beams // block, body, 0)
-
-    member_table = (iota((stations, tiles), 0) == ts_ref[...] % stations).astype(jnp.float32)
-    own_channel = iota((lanes, CB * rows_c), 0) // (2 * stations) == iota(
-        (lanes, CB * rows_c), 1
-    ) // rows_c
-
-    imag_column = iota((tiles, CB * rows_c), 1) // samples % 2 == 1
-    station_rows_of = []
-    for g in range(groups):
-        swt = sw_ref[g * CB : (g + 1) * CB].astype(jnp.float32)
-        right = []
-        for c in range(CB):
-            re = swt[c, 0:1] * member_table
-            im = swt[c, 1:2] * member_table
-            right.append(jnp.concatenate([re, -im], axis=1))
-            right.append(jnp.concatenate([im, re], axis=1))
-        station_rows_of.append(jnp.concatenate(right, axis=0).astype(jnp.bfloat16))
-
     def tied_beams(g, beams_tile):
-        width = CB * rows_c
         other = jnp.where(
             imag_column,
             -pltpu.roll(beams_tile, samples, 1),
-            pltpu.roll(beams_tile, width - samples, 1),
+            pltpu.roll(beams_tile, rows_g - samples, 1),
         )
         left = jnp.concatenate([beams_tile, other], axis=0).astype(jnp.bfloat16)
-        station = jnp.dot(station_rows_of[g], left, preferred_element_type=jnp.float32)
+        station = jnp.dot(station_ref[g], left, preferred_element_type=jnp.float32)
         station = jnp.where(own_channel, station, 0.0).astype(jnp.bfloat16)
-        tied = jnp.dot(
-            tied_ref[:, g * lanes : (g + 1) * lanes], station, preferred_element_type=jnp.float32
-        )
+        tied = jnp.dot(tied_ref[g], station, preferred_element_type=jnp.float32)
         devices, rows, _ = out_ref.shape
-        out_ref[:, :, g * CB * rows_c : (g + 1) * CB * rows_c] = tied.astype(jnp.bfloat16).reshape(
-            devices, rows, CB * rows_c
-        )
-
-    for g in range(1, groups):
-        if g > 1:
-            large[g].wait()
+        columns = pl.ds(pl.multiple_of(g * rows_g, rows_g), rows_g)
+        out_ref[:, :, columns] = tied.astype(jnp.bfloat16).reshape(devices, rows, rows_g)
+
+    def step(g, carry):
+        voltages(g).wait()
         now = tile_beams(g)
-        tied_beams(g - 1, last)
-        last = now
-    tied_beams(groups - 1, last)
+        tied_beams(jnp.maximum(g - 1, 0), tile_ref[...])
+        tile_ref[...] = now
+        return carry
+
+    lax.fori_loop(0, groups, step, 0)
+    tied_beams(groups - 1, tile_ref[...])
 
 
 def last_kernel(parts_ref, out_ref):
@@ -244,8 +230,10 @@
     n_stn, n_chan = lax.axis_size("stn"), lax.axis_size("chan")
     rows = beams // (n_stn * n_chan)
     width = channels * 2 * samples
+    tiles = station_weights.shape[2]
+    lanes = CB * 2 * (tiles // TPS)
     operands = (
-        volts.reshape(-1, volts.shape[3]),
+        volts.reshape(channels // CB, CB * 2 * samples, volts.shape[3]),
         antenna_tile_weights,
         station_weights,
         tile_station[None, :],
@@ -262,7 +250,9 @@
         out_specs=pl.BlockSpec(memory_space=pltpu.VMEM),
         scratch_shapes=[pltpu.VMEM(x.shape, x.dtype) for x in operands]
         + [
-            pltpu.VMEM((beams, channels * 2 * (station_weights.shape[2] // TPS)), jnp.bfloat16),
+            pltpu.VMEM((channels // CB, beams, lanes), jnp.bfloat16),
+            pltpu.VMEM((channels // CB, lanes, 2 * tiles), jnp.bfloat16),
+            pltpu.VMEM((tiles, CB * 2 * samples), jnp.float32),
             pltpu.SemaphoreType.DMA((len(operands) - 1 + channels // CB,)),
         ],
         compiler_params=pltpu.CompilerParams(vmem_limit_bytes=24 * 2**20),

time: 18.6 us -> 19.3 us (1.038)
  Pallas kernels: 3.99 us -> 4.73 us
    pallas_call x1, Pallas kernels: 3.2 us -> 3.94 us  [shards(): pl.pallas_call(kernel, out_shape=pltpu.VMEM((n_stn * n_chan, rows, width)...]
where the time goes in v29:
time: 19.3 us; the launch traced here: 19.2 us
  blocking collectives  14.4 us (75%)
  Pallas kernels  4.73 us (25%)
    all_to_all x1, blocking collectives, shards(): lax.all_to_all(partial, ('stn', 'chan'), split_axis=0, concat_axis=0, axi...  14.4 us
    pallas_call x1, Pallas kernels, shards(): pl.pallas_call(kernel, out_shape=pltpu.VMEM((n_stn * n_chan, rows, width)...  3.94 us
    pallas_call x1, Pallas kernels, shards(): pl.pallas_call(last_kernel, out_shape=jax.ShapeDtypeStruct((rows, 2 * sam...  0.79 us

profile of v29, /device:TPU:0, one launch (start us, length us, event | category | flops | bytes accessed | tf_op | source)
XLA Modules:
  0.0 19.2 jit_solution(10315847249692667465)
XLA Ops:
  0.0 3.9 %partial_tied.1 = bf16[32,2,768]{2,1,0:T(2,128)(2,1)S(1)} custom-call(bf16[3,256,2048]{2,1,0:T(8,128)(2,1)} %bitcast.7, bf16[24,2,2048]{2,1,0:T(2,128)(2,1)} %aw_hbm.1, bf16[24,2,128]{2,1,0:T(2,128)(2,1)} %sw_hbm.1, s32[1,128]{1,0:T(1,128)} %bitcast.10, s32[1,128]{1,0:T(1,128)} %bitcast.11, f32[2,128]{1,0:T(2,128)} %bitcast.8, f32[2,64]{1,0:T(2,128)} %bitcast.9, ...), custom_call_target="tpu_custom_call" | custom-call | tf_op jit(solution)/shard_map/partial_tied/pallas_call | solution.py:246
  3.9 14.4 %all_to_all.5.parts_ref = bf16[32,2,768]{2,1,0:T(2,128)(2,1)S(1)} all-to-all(bf16[32,2,768]{2,1,0:T(2,128)(2,1)S(1)} %partial_tied.1), channel_id=1, replica_groups={{31,30,29,28,27,26,25,24,23,22,21,20,19,18,17,16,15,14,13,12,11,10,9,8,..., dimensions={0} | all-to-all | bytes 196608 | tf_op jit(solution)/shard_map/all_to_all | solution.py:261
  18.4 0.8 %tied_beams.1 = bf16[2,32,48]{2,1,0:T(8,128)(2,1)} custom-call(bf16[32,2,768]{2,1,0:T(2,128)(2,1)S(1)} %all_to_all.5.parts_ref), custom_call_target="tpu_custom_call" | custom-call | tf_op jit(solution)/shard_map/tied_beams/pallas_call | solution.py:270

commit v30 on v28

--- a/solution.py
+++ b/solution.py
@@ -200,10 +200,7 @@
         tied = jnp.dot(
             tied_ref[:, g * lanes : (g + 1) * lanes], station, preferred_element_type=jnp.float32
         )
-        devices, rows, _ = out_ref.shape
-        out_ref[:, :, g * CB * rows_c : (g + 1) * CB * rows_c] = tied.astype(jnp.bfloat16).reshape(
-            devices, rows, CB * rows_c
-        )
+        out_ref[:, g * CB * rows_c : (g + 1) * CB * rows_c] = tied.astype(jnp.bfloat16)
 
     for g in range(1, groups):
         if g > 1:
@@ -257,7 +254,7 @@
     operands = [pltpu.with_memory_space_constraint(x, pltpu.HBM) for x in operands]
     partial = pl.pallas_call(
         kernel,
-        out_shape=pltpu.VMEM((n_stn * n_chan, rows, width), jnp.bfloat16),
+        out_shape=pltpu.VMEM((beams, width), jnp.bfloat16),
         in_specs=[pl.BlockSpec(memory_space=pltpu.HBM)] * len(operands),
         out_specs=pl.BlockSpec(memory_space=pltpu.VMEM),
         scratch_shapes=[pltpu.VMEM(x.shape, x.dtype) for x in operands]
@@ -269,7 +266,7 @@
         name="partial_tied",
     )(*operands)
     parts = lax.all_to_all(
-        partial,
+        partial.reshape(n_stn * n_chan, rows, width),
         ("stn", "chan"),
         split_axis=0,
         concat_axis=0,

time: 18.6 us -> 18.6 us (level)
  no operation moved by 1% of the time
where the time goes in v30:
time: 18.6 us; the launch traced here: 18.5 us
  blocking collectives  14.4 us (77%)
  Pallas kernels  3.99 us (21%)
    all_to_all x1, blocking collectives, shards(): lax.all_to_all(partial.reshape(n_stn * n_chan, rows, width), ('stn', 'cha...  14.4 us
    pallas_call x1, Pallas kernels, shards(): pl.pallas_call(kernel, out_shape=pltpu.VMEM((beams, width), jnp.bfloat16)...  3.19 us
    pallas_call x1, Pallas kernels, shards(): pl.pallas_call(last_kernel, out_shape=jax.ShapeDtypeStruct((rows, 2 * sam...  0.8 us

profile of v30, /device:TPU:0, one launch (start us, length us, event | category | flops | bytes accessed | tf_op | source)
XLA Modules:
  0.0 18.5 jit_solution(10677969745370607599)
XLA Ops:
  0.0 3.2 %partial_tied.1 = bf16[64,768]{1,0:T(8,128)(2,1)S(1)} custom-call(bf16[768,2048]{1,0:T(8,128)(2,1)} %bitcast.7, bf16[24,2,2048]{2,1,0:T(2,128)(2,1)} %aw_hbm.1, bf16[24,2,128]{2,1,0:T(2,128)(2,1)} %sw_hbm.1, s32[1,128]{1,0:T(1,128)} %bitcast.10, s32[1,128]{1,0:T(1,128)} %bitcast.11, f32[2,128]{1,0:T(2,128)} %bitcast.8, f32[2,64]{1,0:T(2,128)} %bitcast.9, ...), custom_call_target="tpu_custom_call" | custom-call | tf_op jit(solution)/shard_map/partial_tied/pallas_call | solution.py:255
  3.2 14.4 %all_to_all.5.parts_ref = bf16[32,2,768]{2,1,0:T(2,128)(2,1)S(1)} all-to-all(bf16[32,2,768]{2,1,0:T(2,128)(2,1)S(1)} %reshape.7), channel_id=1, replica_groups={{31,30,29,28,27,26,25,24,23,22,21,20,19,18,17,16,15,14,13,12,11,10,9,8,..., dimensions={0} | all-to-all | bytes 196608 | tf_op jit(solution)/shard_map/all_to_all | solution.py:268
  17.7 0.8 %tied_beams.1 = bf16[2,32,48]{2,1,0:T(8,128)(2,1)} custom-call(bf16[32,2,768]{2,1,0:T(2,128)(2,1)S(1)} %all_to_all.5.parts_ref), custom_call_target="tpu_custom_call" | custom-call | tf_op jit(solution)/shard_map/tied_beams/pallas_call | solution.py:277
  (1 shorter events, 0.0 us)

commit v31 on v28

--- a/solution.py
+++ b/solution.py
@@ -99,25 +99,20 @@
         copy.start()
         return copy
 
-    def voltages(g):
-        part = pl.ds(g * CB * rows_c, CB * rows_c)
-        return volt_hbm.at[part], volts.at[part]
-
     pairs = [
-        voltages(0),
         (aw_hbm, aw_ref),
+        (volt_hbm, volts),
         (order_hbm, order_ref),
         (dir_hbm, dir_ref),
         (pos_hbm, pos_ref),
         (group_hbm, group_ref),
         (ts_hbm, ts_ref),
         (sw_hbm, sw_ref),
-    ] + [voltages(g) for g in range(1, groups)]
+    ]
     copies = [start(source, target, k) for k, (source, target) in enumerate(pairs)]
-    large = copies[:1] + copies[8:]
     antenna_tile = iota((CHUNK // TILE_ANTENNAS, CHUNK), 1) // TILE_ANTENNAS
     sum_tile = (antenna_tile == iota(antenna_tile.shape, 0)).astype(jnp.bfloat16)
-    for copy in copies[:2]:
+    for copy in copies[2:]:
         copy.wait()
 
     def tile_beams(g):
@@ -136,10 +131,6 @@
             for first in range(0, antennas, CHUNK)
         ]
         return jnp.concatenate(sums, axis=0)
-
-    last = tile_beams(0)
-    for copy in copies[2:9]:
-        copy.wait()
 
     east_s, north_s, group_s = station_rows(pos_ref, group_ref, stations, lanes)
     lane = iota((1, lanes), 1)
@@ -205,9 +196,10 @@
             devices, rows, CB * rows_c
         )
 
+    for copy in copies[:2]:
+        copy.wait()
+    last = tile_beams(0)
     for g in range(1, groups):
-        if g > 1:
-            large[g].wait()
         now = tile_beams(g)
         tied_beams(g - 1, last)
         last = now
@@ -263,7 +255,7 @@
         scratch_shapes=[pltpu.VMEM(x.shape, x.dtype) for x in operands]
         + [
             pltpu.VMEM((beams, channels * 2 * (station_weights.shape[2] // TPS)), jnp.bfloat16),
-            pltpu.SemaphoreType.DMA((len(operands) - 1 + channels // CB,)),
+            pltpu.SemaphoreType.DMA((len(operands),)),
         ],
         compiler_params=pltpu.CompilerParams(vmem_limit_bytes=24 * 2**20),
         name="partial_tied",

time: 18.6 us -> 19.2 us (1.032)
  Pallas kernels: 3.99 us -> 4.5 us
    pallas_call x1, Pallas kernels: 3.2 us -> 3.7 us  [shards(): pl.pallas_call(kernel, out_shape=pltpu.VMEM((n_stn * n_chan, rows, width)...]
where the time goes in v31:
time: 19.2 us; the launch traced here: 18.9 us
  blocking collectives  14.4 us (75%)
  Pallas kernels  4.5 us (23%)
    all_to_all x1, blocking collectives, shards(): lax.all_to_all(partial, ('stn', 'chan'), split_axis=0, concat_axis=0, axi...  14.4 us
    pallas_call x1, Pallas kernels, shards(): pl.pallas_call(kernel, out_shape=pltpu.VMEM((n_stn * n_chan, rows, width)...  3.7 us
    pallas_call x1, Pallas kernels, shards(): pl.pallas_call(last_kernel, out_shape=jax.ShapeDtypeStruct((rows, 2 * sam...  0.8 us

profile of v31, /device:TPU:0, one launch (start us, length us, event | category | flops | bytes accessed | tf_op | source)
XLA Modules:
  0.0 18.9 jit_solution(7369915287712668846)
XLA Ops:
  0.0 3.7 %partial_tied.1 = bf16[32,2,768]{2,1,0:T(2,128)(2,1)S(1)} custom-call(bf16[768,2048]{1,0:T(8,128)(2,1)} %bitcast.7, bf16[24,2,2048]{2,1,0:T(2,128)(2,1)} %aw_hbm.1, bf16[24,2,128]{2,1,0:T(2,128)(2,1)} %sw_hbm.1, s32[1,128]{1,0:T(1,128)} %bitcast.10, s32[1,128]{1,0:T(1,128)} %bitcast.11, f32[2,128]{1,0:T(2,128)} %bitcast.8, f32[2,64]{1,0:T(2,128)} %bitcast.9, ...), custom_call_target="tpu_custom_call" | custom-call | tf_op jit(solution)/shard_map/partial_tied/pallas_call | solution.py:250
  3.7 14.4 %all_to_all.5.parts_ref = bf16[32,2,768]{2,1,0:T(2,128)(2,1)S(1)} all-to-all(bf16[32,2,768]{2,1,0:T(2,128)(2,1)S(1)} %partial_tied.1), channel_id=1, replica_groups={{31,30,29,28,27,26,25,24,23,22,21,20,19,18,17,16,15,14,13,12,11,10,9,8,..., dimensions={0} | all-to-all | bytes 196608 | tf_op jit(solution)/shard_map/all_to_all | solution.py:263
  18.1 0.8 %tied_beams.1 = bf16[2,32,48]{2,1,0:T(8,128)(2,1)} custom-call(bf16[32,2,768]{2,1,0:T(2,128)(2,1)S(1)} %all_to_all.5.parts_ref), custom_call_target="tpu_custom_call" | custom-call | tf_op jit(solution)/shard_map/tied_beams/pallas_call | solution.py:272

commit v32 on v28

--- a/solution.py
+++ b/solution.py
@@ -82,6 +82,7 @@
     dir_ref,
     order_ref,
     tied_ref,
+    rows_ref,
     sems,
 ):
     channels, _, tiles = sw_ref.shape
@@ -104,8 +105,8 @@
         return volt_hbm.at[part], volts.at[part]
 
     pairs = [
+        (aw_hbm, aw_ref),
         voltages(0),
-        (aw_hbm, aw_ref),
         (order_hbm, order_ref),
         (dir_hbm, dir_ref),
         (pos_hbm, pos_ref),
@@ -114,18 +115,21 @@
         (sw_hbm, sw_ref),
     ] + [voltages(g) for g in range(1, groups)]
     copies = [start(source, target, k) for k, (source, target) in enumerate(pairs)]
-    large = copies[:1] + copies[8:]
+    large = copies[1:2] + copies[8:]
     antenna_tile = iota((CHUNK // TILE_ANTENNAS, CHUNK), 1) // TILE_ANTENNAS
     sum_tile = (antenna_tile == iota(antenna_tile.shape, 0)).astype(jnp.bfloat16)
-    for copy in copies[:2]:
-        copy.wait()
+    copies[0].wait()
+    for c in range(channels):
+        weights = aw_ref[c].astype(jnp.float32)
+        for part in range(2):
+            row = jnp.broadcast_to(weights[part : part + 1], (samples, antennas))
+            rows_ref[c, part] = row.astype(jnp.bfloat16)
+    large[0].wait()
 
     def tile_beams(g):
         products = []
-        weights = aw_ref[g * CB : (g + 1) * CB].astype(jnp.float32)
         for c in range(CB):
-            w_re = jnp.broadcast_to(weights[c, 0:1], (samples, antennas)).astype(jnp.bfloat16)
-            w_im = jnp.broadcast_to(weights[c, 1:2], (samples, antennas)).astype(jnp.bfloat16)
+            w_re, w_im = rows_ref[g * CB + c, 0], rows_ref[g * CB + c, 1]
             first = (g * CB + c) * rows_c
             v_re, v_im = volts[first : first + samples], volts[first + samples : first + rows_c]
             products.append(w_re * v_re - w_im * v_im)
@@ -263,6 +267,7 @@
         scratch_shapes=[pltpu.VMEM(x.shape, x.dtype) for x in operands]
         + [
             pltpu.VMEM((beams, channels * 2 * (station_weights.shape[2] // TPS)), jnp.bfloat16),
+            pltpu.VMEM(volts.shape, jnp.bfloat16),
             pltpu.SemaphoreType.DMA((len(operands) - 1 + channels // CB,)),
         ],
         compiler_params=pltpu.CompilerParams(vmem_limit_bytes=24 * 2**20),

time: 18.6 us -> 18.6 us (level)
  no operation moved by 1% of the time
where the time goes in v32:
time: 18.6 us; the launch traced here: 18.5 us
  blocking collectives  14.4 us (77%)
  Pallas kernels  4.02 us (22%)
    all_to_all x1, blocking collectives, shards(): lax.all_to_all(partial, ('stn', 'chan'), split_axis=0, concat_axis=0, axi...  14.4 us
    pallas_call x1, Pallas kernels, shards(): pl.pallas_call(kernel, out_shape=pltpu.VMEM((n_stn * n_chan, rows, width)...  3.22 us
    pallas_call x1, Pallas kernels, shards(): pl.pallas_call(last_kernel, out_shape=jax.ShapeDtypeStruct((rows, 2 * sam...  0.8 us

profile of v32, /device:TPU:0, one launch (start us, length us, event | category | flops | bytes accessed | tf_op | source)
XLA Modules:
  0.0 18.5 jit_solution(7006936257765635163)
XLA Ops:
  0.0 3.2 %partial_tied.1 = bf16[32,2,768]{2,1,0:T(2,128)(2,1)S(1)} custom-call(bf16[768,2048]{1,0:T(8,128)(2,1)} %bitcast.7, bf16[24,2,2048]{2,1,0:T(2,128)(2,1)} %aw_hbm.1, bf16[24,2,128]{2,1,0:T(2,128)(2,1)} %sw_hbm.1, s32[1,128]{1,0:T(1,128)} %bitcast.10, s32[1,128]{1,0:T(1,128)} %bitcast.11, f32[2,128]{1,0:T(2,128)} %bitcast.8, f32[2,64]{1,0:T(2,128)} %bitcast.9, ...), custom_call_target="tpu_custom_call" | custom-call | tf_op jit(solution)/shard_map/partial_tied/pallas_call | solution.py:262
  3.2 14.4 %all_to_all.5.parts_ref = bf16[32,2,768]{2,1,0:T(2,128)(2,1)S(1)} all-to-all(bf16[32,2,768]{2,1,0:T(2,128)(2,1)S(1)} %partial_tied.1), channel_id=1, replica_groups={{31,30,29,28,27,26,25,24,23,22,21,20,19,18,17,16,15,14,13,12,11,10,9,8,..., dimensions={0} | all-to-all | bytes 196608 | tf_op jit(solution)/shard_map/all_to_all | solution.py:276
  17.7 0.8 %tied_beams.1 = bf16[2,32,48]{2,1,0:T(8,128)(2,1)} custom-call(bf16[32,2,768]{2,1,0:T(2,128)(2,1)S(1)} %all_to_all.5.parts_ref), custom_call_target="tpu_custom_call" | custom-call | tf_op jit(solution)/shard_map/tied_beams/pallas_call | solution.py:285

commit v33 on v31

--- a/solution.py
+++ b/solution.py
@@ -12,6 +12,7 @@
 TPS = 16
 GROUPS = 4
 CB = 8
+SPLIT = (4, 2, 1)
 CHUNK = 256
 NT = (((1,), (1,)), ((), ()))
 SIN = [(-1) ** i * (2 * math.pi) ** (2 * i + 1) / math.factorial(2 * i + 1) for i in range(7)]
@@ -89,6 +90,7 @@
     samples = volt_hbm.shape[0] // (2 * channels)
     stations = tiles // TPS
     groups = channels // CB
+    assert groups == len(SPLIT)
     rows_c = 2 * samples
     beams = order_ref.shape[1]
     lanes = CB * 2 * stations
@@ -99,9 +101,13 @@
         copy.start()
         return copy
 
-    pairs = [
+    def voltages(g):
+        rows = CB * rows_c // SPLIT[g]
+        parts = [pl.ds(g * CB * rows_c + k * rows, rows) for k in range(SPLIT[g])]
+        return [(volt_hbm.at[part], volts.at[part]) for part in parts]
+
+    pairs = voltages(0) + [
         (aw_hbm, aw_ref),
-        (volt_hbm, volts),
         (order_hbm, order_ref),
         (dir_hbm, dir_ref),
         (pos_hbm, pos_ref),
@@ -109,10 +115,14 @@
         (ts_hbm, ts_ref),
         (sw_hbm, sw_ref),
     ]
+    ends = [len(pairs)]
+    for g in range(1, groups):
+        pairs += voltages(g)
+        ends.append(len(pairs))
     copies = [start(source, target, k) for k, (source, target) in enumerate(pairs)]
     antenna_tile = iota((CHUNK // TILE_ANTENNAS, CHUNK), 1) // TILE_ANTENNAS
     sum_tile = (antenna_tile == iota(antenna_tile.shape, 0)).astype(jnp.bfloat16)
-    for copy in copies[2:]:
+    for copy in copies[: SPLIT[0] + 1]:
         copy.wait()
 
     def tile_beams(g):
@@ -131,6 +141,10 @@
             for first in range(0, antennas, CHUNK)
         ]
         return jnp.concatenate(sums, axis=0)
+
+    last = tile_beams(0)
+    for copy in copies[SPLIT[0] + 1 : ends[1]]:
+        copy.wait()
 
     east_s, north_s, group_s = station_rows(pos_ref, group_ref, stations, lanes)
     lane = iota((1, lanes), 1)
@@ -196,10 +210,10 @@
             devices, rows, CB * rows_c
         )
 
-    for copy in copies[:2]:
-        copy.wait()
-    last = tile_beams(0)
     for g in range(1, groups):
+        if g > 1:
+            for copy in copies[ends[g - 1] : ends[g]]:
+                copy.wait()
         now = tile_beams(g)
         tied_beams(g - 1, last)
         last = now
@@ -255,7 +269,7 @@
         scratch_shapes=[pltpu.VMEM(x.shape, x.dtype) for x in operands]
         + [
             pltpu.VMEM((beams, channels * 2 * (station_weights.shape[2] // TPS)), jnp.bfloat16),
-            pltpu.SemaphoreType.DMA((len(operands),)),
+            pltpu.SemaphoreType.DMA((len(operands) - 1 + sum(SPLIT),)),
         ],
         compiler_params=pltpu.CompilerParams(vmem_limit_bytes=24 * 2**20),
         name="partial_tied",

time: 19.2 us -> 18.6 us (0.969)
  Pallas kernels: 4.5 us -> 3.98 us
    pallas_call x1, Pallas kernels: 3.7 us -> 3.19 us  [shards(): pl.pallas_call(kernel, out_shape=pltpu.VMEM((n_stn * n_chan, rows, width)...]
where the time goes in v33:
time: 18.6 us; the launch traced here: 18.4 us
  blocking collectives  14.4 us (77%)
  Pallas kernels  3.98 us (21%)
    all_to_all x1, blocking collectives, shards(): lax.all_to_all(partial, ('stn', 'chan'), split_axis=0, concat_axis=0, axi...  14.4 us
    pallas_call x1, Pallas kernels, shards(): pl.pallas_call(kernel, out_shape=pltpu.VMEM((n_stn * n_chan, rows, width)...  3.19 us
    pallas_call x1, Pallas kernels, shards(): pl.pallas_call(last_kernel, out_shape=jax.ShapeDtypeStruct((rows, 2 * sam...  0.79 us

profile of v33, /device:TPU:0, one launch (start us, length us, event | category | flops | bytes accessed | tf_op | source)
XLA Modules:
  0.0 18.4 jit_solution(1666455241678339343)
XLA Ops:
  0.0 3.2 %partial_tied.1 = bf16[32,2,768]{2,1,0:T(2,128)(2,1)S(1)} custom-call(bf16[768,2048]{1,0:T(8,128)(2,1)} %bitcast.7, bf16[24,2,2048]{2,1,0:T(2,128)(2,1)} %aw_hbm.1, bf16[24,2,128]{2,1,0:T(2,128)(2,1)} %sw_hbm.1, s32[1,128]{1,0:T(1,128)} %bitcast.10, s32[1,128]{1,0:T(1,128)} %bitcast.11, f32[2,128]{1,0:T(2,128)} %bitcast.8, f32[2,64]{1,0:T(2,128)} %bitcast.9, ...), custom_call_target="tpu_custom_call" | custom-call | tf_op jit(solution)/shard_map/partial_tied/pallas_call | solution.py:264
  3.2 14.4 %all_to_all.5.parts_ref = bf16[32,2,768]{2,1,0:T(2,128)(2,1)S(1)} all-to-all(bf16[32,2,768]{2,1,0:T(2,128)(2,1)S(1)} %partial_tied.1), channel_id=1, replica_groups={{31,30,29,28,27,26,25,24,23,22,21,20,19,18,17,16,15,14,13,12,11,10,9,8,..., dimensions={0} | all-to-all | bytes 196608 | tf_op jit(solution)/shard_map/all_to_all | solution.py:277
  17.6 0.8 %tied_beams.1 = bf16[2,32,48]{2,1,0:T(8,128)(2,1)} custom-call(bf16[32,2,768]{2,1,0:T(2,128)(2,1)S(1)} %all_to_all.5.parts_ref), custom_call_target="tpu_custom_call" | custom-call | tf_op jit(solution)/shard_map/tied_beams/pallas_call | solution.py:286

commit v34 on v28

--- a/solution.py
+++ b/solution.py
@@ -27,11 +27,13 @@
 
 def beam_columns(order_ref, dir_ref, start, rows):
     beams = order_ref.shape[1]
-    each = beams // (lax.axis_size("stn") * lax.axis_size("chan"))
+    n_stn, n_chan = lax.axis_size("stn"), lax.axis_size("chan")
+    each = beams // (n_stn * n_chan)
     order = order_ref[...].astype(jnp.float32)
     lane = iota((rows, beams), 1)
-    slot = iota((rows, beams), 0) + start
-    own = lane == beams - each - slot // each * each + slot % each
+    slot = iota((rows, 1), 0) + start
+    place = n_stn * n_chan - 1 - slot // each
+    own = lane == (place % n_stn * n_chan + place // n_stn) * each + slot % each
     ids = jnp.sum(jnp.where(own, order, 0.0), axis=1, keepdims=True)
     pick = lane.astype(jnp.float32) == ids
     east = jnp.sum(jnp.where(pick, dir_ref[0:1, :], 0.0), axis=1, keepdims=True)
@@ -220,7 +222,7 @@
     channels = total_chans // n_chan
     width = channels * rows_c
     parts = parts_ref[...].astype(jnp.float32)
-    tied = [sum(parts[n_chan - 1 - chan + k * n_chan] for k in range(n_stn)) for chan in range(n_chan)]
+    tied = [sum(parts[(n_chan - 1 - chan) * n_stn + k] for k in range(n_stn)) for chan in range(n_chan)]
     diagonal = iota((channels, width), 0) == iota((channels, width), 1) // rows_c
     spread = (iota((rows_c, width), 0) == iota((rows_c, width), 1) % rows_c).astype(jnp.bfloat16)
     for b in range(own_beams):
@@ -268,12 +270,13 @@
         compiler_params=pltpu.CompilerParams(vmem_limit_bytes=24 * 2**20),
         name="partial_tied",
     )(*operands)
+    order = [stn * n_chan + chan for chan in range(n_chan) for stn in range(n_stn)][::-1]
     parts = lax.all_to_all(
         partial,
         ("stn", "chan"),
         split_axis=0,
         concat_axis=0,
-        axis_index_groups=[list(reversed(range(n_stn * n_chan)))],
+        axis_index_groups=[order],
         tiled=True,
     )
     vmem = pl.BlockSpec(memory_space=pltpu.VMEM)

time: 18.6 us -> 19 us (1.022)
  blocking collectives: 14.4 us -> 14.8 us
    all_to_all x1, blocking collectives: 14.4 us -> 14.8 us  [shards(): lax.all_to_all(partial, ('stn', 'chan'), split_axis=0, concat_axis=0, axi...]
where the time goes in v34:
time: 19 us; the launch traced here: 18.8 us
  blocking collectives  14.8 us (78%)
  Pallas kernels  4.01 us (21%)
    all_to_all x1, blocking collectives, shards(): lax.all_to_all(partial, ('stn', 'chan'), split_axis=0, concat_axis=0, axi...  14.8 us
    pallas_call x1, Pallas kernels, shards(): pl.pallas_call(kernel, out_shape=pltpu.VMEM((n_stn * n_chan, rows, width)...  3.21 us
    pallas_call x1, Pallas kernels, shards(): pl.pallas_call(last_kernel, out_shape=jax.ShapeDtypeStruct((rows, 2 * sam...  0.8 us

profile of v34, /device:TPU:0, one launch (start us, length us, event | category | flops | bytes accessed | tf_op | source)
XLA Modules:
  0.0 18.8 jit_solution(12690849548509705850)
XLA Ops:
  0.0 3.2 %partial_tied.1 = bf16[32,2,768]{2,1,0:T(2,128)(2,1)S(1)} custom-call(bf16[768,2048]{1,0:T(8,128)(2,1)} %bitcast.7, bf16[24,2,2048]{2,1,0:T(2,128)(2,1)} %aw_hbm.1, bf16[24,2,128]{2,1,0:T(2,128)(2,1)} %sw_hbm.1, s32[1,128]{1,0:T(1,128)} %bitcast.10, s32[1,128]{1,0:T(1,128)} %bitcast.11, f32[2,128]{1,0:T(2,128)} %bitcast.8, f32[2,64]{1,0:T(2,128)} %bitcast.9, ...), custom_call_target="tpu_custom_call" | custom-call | tf_op jit(solution)/shard_map/partial_tied/pallas_call | solution.py:260
  3.2 14.8 %all_to_all.5.parts_ref = bf16[32,2,768]{2,1,0:T(2,128)(2,1)S(1)} all-to-all(bf16[32,2,768]{2,1,0:T(2,128)(2,1)S(1)} %partial_tied.1), channel_id=1, replica_groups={{31,29,27,25,23,21,19,17,15,13,11,9,7,5,3,1,30,28,26,24,22,20,18,16,14,..., dimensions={0} | all-to-all | bytes 196608 | tf_op jit(solution)/shard_map/all_to_all | solution.py:274
  18.0 0.8 %tied_beams.1 = bf16[2,32,48]{2,1,0:T(8,128)(2,1)} custom-call(bf16[32,2,768]{2,1,0:T(2,128)(2,1)S(1)} %all_to_all.5.parts_ref), custom_call_target="tpu_custom_call" | custom-call | tf_op jit(solution)/shard_map/tied_beams/pallas_call | solution.py:283

commit v35 on v28

--- a/solution.py
+++ b/solution.py
@@ -114,7 +114,6 @@
         (sw_hbm, sw_ref),
     ] + [voltages(g) for g in range(1, groups)]
     copies = [start(source, target, k) for k, (source, target) in enumerate(pairs)]
-    large = copies[:1] + copies[8:]
     antenna_tile = iota((CHUNK // TILE_ANTENNAS, CHUNK), 1) // TILE_ANTENNAS
     sum_tile = (antenna_tile == iota(antenna_tile.shape, 0)).astype(jnp.bfloat16)
     for copy in copies[:2]:
@@ -138,7 +137,7 @@
         return jnp.concatenate(sums, axis=0)
 
     last = tile_beams(0)
-    for copy in copies[2:9]:
+    for copy in copies[2:]:
         copy.wait()
 
     east_s, north_s, group_s = station_rows(pos_ref, group_ref, stations, lanes)
@@ -205,13 +204,9 @@
             devices, rows, CB * rows_c
         )
 
-    for g in range(1, groups):
-        if g > 1:
-            large[g].wait()
-        now = tile_beams(g)
-        tied_beams(g - 1, last)
-        last = now
-    tied_beams(groups - 1, last)
+    found = [last] + [tile_beams(g) for g in range(1, groups)]
+    for g in range(groups):
+        tied_beams(g, found[g])
 
 
 def last_kernel(parts_ref, out_ref):

time: 18.6 us -> 18.7 us (level)
  no operation moved by 1% of the time
where the time goes in v35:
time: 18.7 us; the launch traced here: 18.5 us
  blocking collectives  14.4 us (77%)
  Pallas kernels  4.08 us (22%)
    all_to_all x1, blocking collectives, shards(): lax.all_to_all(partial, ('stn', 'chan'), split_axis=0, concat_axis=0, axi...  14.4 us
    pallas_call x1, Pallas kernels, shards(): pl.pallas_call(kernel, out_shape=pltpu.VMEM((n_stn * n_chan, rows, width)...  3.29 us
    pallas_call x1, Pallas kernels, shards(): pl.pallas_call(last_kernel, out_shape=jax.ShapeDtypeStruct((rows, 2 * sam...  0.8 us

profile of v35, /device:TPU:0, one launch (start us, length us, event | category | flops | bytes accessed | tf_op | source)
XLA Modules:
  0.0 18.5 jit_solution(10432557884090634203)
XLA Ops:
  0.0 3.3 %partial_tied.1 = bf16[32,2,768]{2,1,0:T(2,128)(2,1)S(1)} custom-call(bf16[768,2048]{1,0:T(8,128)(2,1)} %bitcast.7, bf16[24,2,2048]{2,1,0:T(2,128)(2,1)} %aw_hbm.1, bf16[24,2,128]{2,1,0:T(2,128)(2,1)} %sw_hbm.1, s32[1,128]{1,0:T(1,128)} %bitcast.10, s32[1,128]{1,0:T(1,128)} %bitcast.11, f32[2,128]{1,0:T(2,128)} %bitcast.8, f32[2,64]{1,0:T(2,128)} %bitcast.9, ...), custom_call_target="tpu_custom_call" | custom-call | tf_op jit(solution)/shard_map/partial_tied/pallas_call | solution.py:253
  3.3 14.4 %all_to_all.5.parts_ref = bf16[32,2,768]{2,1,0:T(2,128)(2,1)S(1)} all-to-all(bf16[32,2,768]{2,1,0:T(2,128)(2,1)S(1)} %partial_tied.1), channel_id=1, replica_groups={{31,30,29,28,27,26,25,24,23,22,21,20,19,18,17,16,15,14,13,12,11,10,9,8,..., dimensions={0} | all-to-all | bytes 196608 | tf_op jit(solution)/shard_map/all_to_all | solution.py:266
  17.7 0.8 %tied_beams.1 = bf16[2,32,48]{2,1,0:T(8,128)(2,1)} custom-call(bf16[32,2,768]{2,1,0:T(2,128)(2,1)S(1)} %all_to_all.5.parts_ref), custom_call_target="tpu_custom_call" | custom-call | tf_op jit(solution)/shard_map/tied_beams/pallas_call | solution.py:275

commit v36 on v28

--- a/solution.py
+++ b/solution.py
@@ -11,7 +11,7 @@
 TILE_ANTENNAS = 16
 TPS = 16
 GROUPS = 4
-CB = 8
+CB = 12
 CHUNK = 256
 NT = (((1,), (1,)), ((), ()))
 SIN = [(-1) ** i * (2 * math.pi) ** (2 * i + 1) / math.factorial(2 * i + 1) for i in range(7)]

time: 18.6 us -> 18.6 us (level)
  no operation moved by 1% of the time
where the time goes in v36:
time: 18.6 us; the launch traced here: 18.5 us
  blocking collectives  14.4 us (77%)
  Pallas kernels  4.03 us (22%)
    all_to_all x1, blocking collectives, shards(): lax.all_to_all(partial, ('stn', 'chan'), split_axis=0, concat_axis=0, axi...  14.4 us
    pallas_call x1, Pallas kernels, shards(): pl.pallas_call(kernel, out_shape=pltpu.VMEM((n_stn * n_chan, rows, width)...  3.23 us
    pallas_call x1, Pallas kernels, shards(): pl.pallas_call(last_kernel, out_shape=jax.ShapeDtypeStruct((rows, 2 * sam...  0.8 us

profile of v36, /device:TPU:0, one launch (start us, length us, event | category | flops | bytes accessed | tf_op | source)
XLA Modules:
  0.0 18.5 jit_solution(11937636088519032193)
XLA Ops:
  0.0 3.2 %partial_tied.1 = bf16[32,2,768]{2,1,0:T(2,128)(2,1)S(1)} custom-call(bf16[768,2048]{1,0:T(8,128)(2,1)} %bitcast.7, bf16[24,2,2048]{2,1,0:T(2,128)(2,1)} %aw_hbm.1, bf16[24,2,128]{2,1,0:T(2,128)(2,1)} %sw_hbm.1, s32[1,128]{1,0:T(1,128)} %bitcast.10, s32[1,128]{1,0:T(1,128)} %bitcast.11, f32[2,128]{1,0:T(2,128)} %bitcast.8, f32[2,64]{1,0:T(2,128)} %bitcast.9, ...), custom_call_target="tpu_custom_call" | custom-call | tf_op jit(solution)/shard_map/partial_tied/pallas_call | solution.py:258
  3.2 14.4 %all_to_all.5.parts_ref = bf16[32,2,768]{2,1,0:T(2,128)(2,1)S(1)} all-to-all(bf16[32,2,768]{2,1,0:T(2,128)(2,1)S(1)} %partial_tied.1), channel_id=1, replica_groups={{31,30,29,28,27,26,25,24,23,22,21,20,19,18,17,16,15,14,13,12,11,10,9,8,..., dimensions={0} | all-to-all | bytes 196608 | tf_op jit(solution)/shard_map/all_to_all | solution.py:271
  17.7 0.8 %tied_beams.1 = bf16[2,32,48]{2,1,0:T(8,128)(2,1)} custom-call(bf16[32,2,768]{2,1,0:T(2,128)(2,1)S(1)} %all_to_all.5.parts_ref), custom_call_target="tpu_custom_call" | custom-call | tf_op jit(solution)/shard_map/tied_beams/pallas_call | solution.py:280

commit v37 on v33

--- a/solution.py
+++ b/solution.py
@@ -32,7 +32,7 @@
     order = order_ref[...].astype(jnp.float32)
     lane = iota((rows, beams), 1)
     slot = iota((rows, beams), 0) + start
-    own = lane == beams - each - slot // each * each + slot % each
+    own = lane == (beams - slot // each * each) % beams + slot % each
     ids = jnp.sum(jnp.where(own, order, 0.0), axis=1, keepdims=True)
     pick = lane.astype(jnp.float32) == ids
     east = jnp.sum(jnp.where(pick, dir_ref[0:1, :], 0.0), axis=1, keepdims=True)
@@ -226,7 +226,8 @@
     channels = total_chans // n_chan
     width = channels * rows_c
     parts = parts_ref[...].astype(jnp.float32)
-    tied = [sum(parts[n_chan - 1 - chan + k * n_chan] for k in range(n_stn)) for chan in range(n_chan)]
+    devices = n_stn * n_chan
+    tied = [sum(parts[(devices - k * n_chan - chan) % devices] for k in range(n_stn)) for chan in range(n_chan)]
     diagonal = iota((channels, width), 0) == iota((channels, width), 1) // rows_c
     spread = (iota((rows_c, width), 0) == iota((rows_c, width), 1) % rows_c).astype(jnp.bfloat16)
     for b in range(own_beams):
@@ -279,7 +280,7 @@
         ("stn", "chan"),
         split_axis=0,
         concat_axis=0,
-        axis_index_groups=[list(reversed(range(n_stn * n_chan)))],
+        axis_index_groups=[[0, *reversed(range(1, n_stn * n_chan))]],
         tiled=True,
     )
     vmem = pl.BlockSpec(memory_space=pltpu.VMEM)

time: 18.6 us -> 18.6 us (level)
  no operation moved by 1% of the time
where the time goes in v37:
time: 18.6 us; the launch traced here: 18.4 us
  blocking collectives  14.4 us (77%)
  Pallas kernels  4 us (22%)
    all_to_all x1, blocking collectives, shards(): lax.all_to_all(partial, ('stn', 'chan'), split_axis=0, concat_axis=0, axi...  14.4 us
    pallas_call x1, Pallas kernels, shards(): pl.pallas_call(kernel, out_shape=pltpu.VMEM((n_stn * n_chan, rows, width)...  3.2 us
    pallas_call x1, Pallas kernels, shards(): pl.pallas_call(last_kernel, out_shape=jax.ShapeDtypeStruct((rows, 2 * sam...  0.79 us

profile of v37, /device:TPU:0, one launch (start us, length us, event | category | flops | bytes accessed | tf_op | source)
XLA Modules:
  0.0 18.4 jit_solution(13631662417879291168)
XLA Ops:
  0.0 3.2 %partial_tied.1 = bf16[32,2,768]{2,1,0:T(2,128)(2,1)S(1)} custom-call(bf16[768,2048]{1,0:T(8,128)(2,1)} %bitcast.7, bf16[24,2,2048]{2,1,0:T(2,128)(2,1)} %aw_hbm.1, bf16[24,2,128]{2,1,0:T(2,128)(2,1)} %sw_hbm.1, s32[1,128]{1,0:T(1,128)} %bitcast.10, s32[1,128]{1,0:T(1,128)} %bitcast.11, f32[2,128]{1,0:T(2,128)} %bitcast.8, f32[2,64]{1,0:T(2,128)} %bitcast.9, ...), custom_call_target="tpu_custom_call" | custom-call | tf_op jit(solution)/shard_map/partial_tied/pallas_call | solution.py:265
  3.2 14.4 %all_to_all.5.parts_ref = bf16[32,2,768]{2,1,0:T(2,128)(2,1)S(1)} all-to-all(bf16[32,2,768]{2,1,0:T(2,128)(2,1)S(1)} %partial_tied.1), channel_id=1, replica_groups={{0,31,30,29,28,27,26,25,24,23,22,21,20,19,18,17,16,15,14,13,12,11,10,9,..., dimensions={0} | all-to-all | bytes 196608 | tf_op jit(solution)/shard_map/all_to_all | solution.py:278
  17.7 0.8 %tied_beams.1 = bf16[2,32,48]{2,1,0:T(8,128)(2,1)} custom-call(bf16[32,2,768]{2,1,0:T(2,128)(2,1)S(1)} %all_to_all.5.parts_ref), custom_call_target="tpu_custom_call" | custom-call | tf_op jit(solution)/shard_map/tied_beams/pallas_call | solution.py:287

commit v38 on v33

--- a/solution.py
+++ b/solution.py
@@ -11,6 +11,7 @@
 TILE_ANTENNAS = 16
 TPS = 16
 GROUPS = 4
+LANES = 128
 CB = 8
 SPLIT = (4, 2, 1)
 CHUNK = 256
@@ -227,12 +228,21 @@
     width = channels * rows_c
     parts = parts_ref[...].astype(jnp.float32)
     tied = [sum(parts[n_chan - 1 - chan + k * n_chan] for k in range(n_stn)) for chan in range(n_chan)]
-    diagonal = iota((channels, width), 0) == iota((channels, width), 1) // rows_c
-    spread = (iota((rows_c, width), 0) == iota((rows_c, width), 1) % rows_c).astype(jnp.bfloat16)
+    per_tile = LANES // rows_c
+    row, lane = iota((2 * per_tile, LANES), 0), iota((2 * per_tile, LANES), 1)
+    own_lane = row % per_tile == lane // rows_c
+    spread = (iota((rows_c, LANES), 0) == iota((rows_c, LANES), 1) % rows_c).astype(jnp.bfloat16)
+    rows = []
     for b in range(own_beams):
-        rows = [jnp.where(diagonal, tied[chan][b : b + 1], 0.0) for chan in range(n_chan)]
-        rows = jnp.concatenate(rows, axis=0).astype(jnp.bfloat16)
-        out_ref[b] = dot_nt(spread, rows).astype(jnp.bfloat16)
+        for chan in range(n_chan):
+            for first in range(0, width, 2 * LANES):
+                low = tied[chan][b : b + 1, first : first + LANES]
+                high = tied[chan][b : b + 1, first + LANES : first + 2 * LANES]
+                rows.append(jnp.where(own_lane, jnp.where(row < per_tile, low, high), 0.0))
+    rows = jnp.concatenate(rows, axis=0).astype(jnp.bfloat16)
+    columns = dot_nt(spread, rows).astype(jnp.bfloat16)
+    for b in range(own_beams):
+        out_ref[b] = columns[:, b * total_chans : (b + 1) * total_chans]
 
 
 def shards(

time: 18.6 us -> 18.6 us (level)
  no operation moved by 1% of the time
where the time goes in v38:
time: 18.6 us; the launch traced here: 18.5 us
  blocking collectives  14.4 us (77%)
  Pallas kernels  4.03 us (22%)
    all_to_all x1, blocking collectives, shards(): lax.all_to_all(partial, ('stn', 'chan'), split_axis=0, concat_axis=0, axi...  14.4 us
    pallas_call x1, Pallas kernels, shards(): pl.pallas_call(kernel, out_shape=pltpu.VMEM((n_stn * n_chan, rows, width)...  3.19 us
    pallas_call x1, Pallas kernels, shards(): pl.pallas_call(last_kernel, out_shape=jax.ShapeDtypeStruct((rows, 2 * sam...  0.84 us

profile of v38, /device:TPU:0, one launch (start us, length us, event | category | flops | bytes accessed | tf_op | source)
XLA Modules:
  0.0 18.5 jit_solution(17287161901830305678)
XLA Ops:
  0.0 3.2 %partial_tied.1 = bf16[32,2,768]{2,1,0:T(2,128)(2,1)S(1)} custom-call(bf16[768,2048]{1,0:T(8,128)(2,1)} %bitcast.7, bf16[24,2,2048]{2,1,0:T(2,128)(2,1)} %aw_hbm.1, bf16[24,2,128]{2,1,0:T(2,128)(2,1)} %sw_hbm.1, s32[1,128]{1,0:T(1,128)} %bitcast.10, s32[1,128]{1,0:T(1,128)} %bitcast.11, f32[2,128]{1,0:T(2,128)} %bitcast.8, f32[2,64]{1,0:T(2,128)} %bitcast.9, ...), custom_call_target="tpu_custom_call" | custom-call | tf_op jit(solution)/shard_map/partial_tied/pallas_call | solution.py:274
  3.2 14.4 %all_to_all.5.parts_ref = bf16[32,2,768]{2,1,0:T(2,128)(2,1)S(1)} all-to-all(bf16[32,2,768]{2,1,0:T(2,128)(2,1)S(1)} %partial_tied.1), channel_id=1, replica_groups={{31,30,29,28,27,26,25,24,23,22,21,20,19,18,17,16,15,14,13,12,11,10,9,8,..., dimensions={0} | all-to-all | bytes 196608 | tf_op jit(solution)/shard_map/all_to_all | solution.py:287
  17.6 0.8 %tied_beams.1 = bf16[2,32,48]{2,1,0:T(8,128)(2,1)} custom-call(bf16[32,2,768]{2,1,0:T(2,128)(2,1)S(1)} %all_to_all.5.parts_ref), custom_call_target="tpu_custom_call" | custom-call | tf_op jit(solution)/shard_map/tied_beams/pallas_call | solution.py:296

commit v39 on v33

--- a/solution.py
+++ b/solution.py
@@ -26,13 +26,22 @@
     return lax.broadcasted_iota(jnp.int32, shape, dim)
 
 
+def device_at(place, n_chan):
+    stn = place // n_chan
+    stn = stn // 4 * 4 + stn % 2 * 2 + stn // 2 % 2
+    return stn * n_chan + place % n_chan
+
+
 def beam_columns(order_ref, dir_ref, start, rows):
     beams = order_ref.shape[1]
-    each = beams // (lax.axis_size("stn") * lax.axis_size("chan"))
+    n_chan = lax.axis_size("chan")
+    devices = lax.axis_size("stn") * n_chan
+    each = beams // devices
     order = order_ref[...].astype(jnp.float32)
     lane = iota((rows, beams), 1)
     slot = iota((rows, beams), 0) + start
-    own = lane == beams - each - slot // each * each + slot % each
+    place = devices - 1 - slot // each
+    own = lane == device_at(place, n_chan) * each + slot % each
     ids = jnp.sum(jnp.where(own, order, 0.0), axis=1, keepdims=True)
     pick = lane.astype(jnp.float32) == ids
     east = jnp.sum(jnp.where(pick, dir_ref[0:1, :], 0.0), axis=1, keepdims=True)
@@ -279,7 +288,7 @@
         ("stn", "chan"),
         split_axis=0,
         concat_axis=0,
-        axis_index_groups=[list(reversed(range(n_stn * n_chan)))],
+        axis_index_groups=[[device_at(k, n_chan) for k in reversed(range(n_stn * n_chan))]],
         tiled=True,
     )
     vmem = pl.BlockSpec(memory_space=pltpu.VMEM)

time: 18.6 us -> 18.7 us (level)
  no operation moved by 1% of the time
where the time goes in v39:
time: 18.7 us; the launch traced here: 18.6 us
  blocking collectives  14.5 us (78%)
  Pallas kernels  4.03 us (22%)
    all_to_all x1, blocking collectives, shards(): lax.all_to_all(partial, ('stn', 'chan'), split_axis=0, concat_axis=0, axi...  14.5 us
    pallas_call x1, Pallas kernels, shards(): pl.pallas_call(kernel, out_shape=pltpu.VMEM((n_stn * n_chan, rows, width)...  3.24 us
    pallas_call x1, Pallas kernels, shards(): pl.pallas_call(last_kernel, out_shape=jax.ShapeDtypeStruct((rows, 2 * sam...  0.79 us

profile of v39, /device:TPU:0, one launch (start us, length us, event | category | flops | bytes accessed | tf_op | source)
XLA Modules:
  0.0 18.6 jit_solution(13881023106941278846)
XLA Ops:
  0.0 3.2 %partial_tied.1 = bf16[32,2,768]{2,1,0:T(2,128)(2,1)S(1)} custom-call(bf16[768,2048]{1,0:T(8,128)(2,1)} %bitcast.7, bf16[24,2,2048]{2,1,0:T(2,128)(2,1)} %aw_hbm.1, bf16[24,2,128]{2,1,0:T(2,128)(2,1)} %sw_hbm.1, s32[1,128]{1,0:T(1,128)} %bitcast.10, s32[1,128]{1,0:T(1,128)} %bitcast.11, f32[2,128]{1,0:T(2,128)} %bitcast.8, f32[2,64]{1,0:T(2,128)} %bitcast.9, ...), custom_call_target="tpu_custom_call" | custom-call | tf_op jit(solution)/shard_map/partial_tied/pallas_call | solution.py:273
  3.2 14.5 %all_to_all.5.parts_ref = bf16[32,2,768]{2,1,0:T(2,128)(2,1)S(1)} all-to-all(bf16[32,2,768]{2,1,0:T(2,128)(2,1)S(1)} %partial_tied.1), channel_id=1, replica_groups={{31,30,27,26,29,28,25,24,23,22,19,18,21,20,17,16,15,14,11,10,13,12,9,8,..., dimensions={0} | all-to-all | bytes 196608 | tf_op jit(solution)/shard_map/all_to_all | solution.py:286
  17.8 0.8 %tied_beams.1 = bf16[2,32,48]{2,1,0:T(8,128)(2,1)} custom-call(bf16[32,2,768]{2,1,0:T(2,128)(2,1)S(1)} %all_to_all.5.parts_ref), custom_call_target="tpu_custom_call" | custom-call | tf_op jit(solution)/shard_map/tied_beams/pallas_call | solution.py:295

commit v40 on v39

--- a/solution.py
+++ b/solution.py
@@ -27,9 +27,8 @@
 
 
 def device_at(place, n_chan):
-    stn = place // n_chan
-    stn = stn // 4 * 4 + stn % 2 * 2 + stn // 2 % 2
-    return stn * n_chan + place % n_chan
+    pair, rest = place // (2 * n_chan), place % (2 * n_chan)
+    return (pair * 2 + rest % 2) * n_chan + rest // 2
 
 
 def beam_columns(order_ref, dir_ref, start, rows):
@@ -235,7 +234,9 @@
     channels = total_chans // n_chan
     width = channels * rows_c
     parts = parts_ref[...].astype(jnp.float32)
-    tied = [sum(parts[n_chan - 1 - chan + k * n_chan] for k in range(n_stn)) for chan in range(n_chan)]
+    devices = n_stn * n_chan
+    chan_of = [device_at(devices - 1 - k, n_chan) % n_chan for k in range(devices)]
+    tied = [sum(parts[k] for k in range(devices) if chan_of[k] == chan) for chan in range(n_chan)]
     diagonal = iota((channels, width), 0) == iota((channels, width), 1) // rows_c
     spread = (iota((rows_c, width), 0) == iota((rows_c, width), 1) % rows_c).astype(jnp.bfloat16)
     for b in range(own_beams):

time: 18.7 us -> 19 us (1.016)
  blocking collectives: 14.5 us -> 14.8 us
    all_to_all x1, blocking collectives: 14.5 us -> 14.8 us  [shards(): lax.all_to_all(partial, ('stn', 'chan'), split_axis=0, concat_axis=0, axi...]
where the time goes in v40:
time: 19 us; the launch traced here: 18.8 us
  blocking collectives  14.8 us (78%)
  Pallas kernels  4.01 us (21%)
    all_to_all x1, blocking collectives, shards(): lax.all_to_all(partial, ('stn', 'chan'), split_axis=0, concat_axis=0, axi...  14.8 us
    pallas_call x1, Pallas kernels, shards(): pl.pallas_call(kernel, out_shape=pltpu.VMEM((n_stn * n_chan, rows, width)...  3.22 us
    pallas_call x1, Pallas kernels, shards(): pl.pallas_call(last_kernel, out_shape=jax.ShapeDtypeStruct((rows, 2 * sam...  0.8 us

profile of v40, /device:TPU:0, one launch (start us, length us, event | category | flops | bytes accessed | tf_op | source)
XLA Modules:
  0.0 18.8 jit_solution(15289682387170276612)
XLA Ops:
  0.0 3.2 %partial_tied.1 = bf16[32,2,768]{2,1,0:T(2,128)(2,1)S(1)} custom-call(bf16[768,2048]{1,0:T(8,128)(2,1)} %bitcast.7, bf16[24,2,2048]{2,1,0:T(2,128)(2,1)} %aw_hbm.1, bf16[24,2,128]{2,1,0:T(2,128)(2,1)} %sw_hbm.1, s32[1,128]{1,0:T(1,128)} %bitcast.10, s32[1,128]{1,0:T(1,128)} %bitcast.11, f32[2,128]{1,0:T(2,128)} %bitcast.8, f32[2,64]{1,0:T(2,128)} %bitcast.9, ...), custom_call_target="tpu_custom_call" | custom-call | tf_op jit(solution)/shard_map/partial_tied/pallas_call | solution.py:274
  3.2 14.8 %all_to_all.5.parts_ref = bf16[32,2,768]{2,1,0:T(2,128)(2,1)S(1)} all-to-all(bf16[32,2,768]{2,1,0:T(2,128)(2,1)S(1)} %partial_tied.1), channel_id=1, replica_groups={{31,29,30,28,27,25,26,24,23,21,22,20,19,17,18,16,15,13,14,12,11,9,10,8,..., dimensions={0} | all-to-all | bytes 196608 | tf_op jit(solution)/shard_map/all_to_all | solution.py:287
  18.0 0.8 %tied_beams.1 = bf16[2,32,48]{2,1,0:T(8,128)(2,1)} custom-call(bf16[32,2,768]{2,1,0:T(2,128)(2,1)S(1)} %all_to_all.5.parts_ref), custom_call_target="tpu_custom_call" | custom-call | tf_op jit(solution)/shard_map/tied_beams/pallas_call | solution.py:296

commit v41 on v40

--- a/solution.py
+++ b/solution.py
@@ -28,7 +28,7 @@
 
 def device_at(place, n_chan):
     pair, rest = place // (2 * n_chan), place % (2 * n_chan)
-    return (pair * 2 + rest % 2) * n_chan + rest // 2
+    return (pair * 2 + 1 - rest % 2) * n_chan + rest // 2
 
 
 def beam_columns(order_ref, dir_ref, start, rows):

time: 19 us -> 19 us (level)
  no operation moved by 1% of the time
where the time goes in v41:
time: 19 us; the launch traced here: 18.8 us
  blocking collectives  14.8 us (78%)
  Pallas kernels  4.01 us (21%)
    all_to_all x1, blocking collectives, shards(): lax.all_to_all(partial, ('stn', 'chan'), split_axis=0, concat_axis=0, axi...  14.8 us
    pallas_call x1, Pallas kernels, shards(): pl.pallas_call(kernel, out_shape=pltpu.VMEM((n_stn * n_chan, rows, width)...  3.22 us
    pallas_call x1, Pallas kernels, shards(): pl.pallas_call(last_kernel, out_shape=jax.ShapeDtypeStruct((rows, 2 * sam...  0.8 us

profile of v41, /device:TPU:0, one launch (start us, length us, event | category | flops | bytes accessed | tf_op | source)
XLA Modules:
  0.0 18.8 jit_solution(18193003822467457047)
XLA Ops:
  0.0 3.2 %partial_tied.1 = bf16[32,2,768]{2,1,0:T(2,128)(2,1)S(1)} custom-call(bf16[768,2048]{1,0:T(8,128)(2,1)} %bitcast.7, bf16[24,2,2048]{2,1,0:T(2,128)(2,1)} %aw_hbm.1, bf16[24,2,128]{2,1,0:T(2,128)(2,1)} %sw_hbm.1, s32[1,128]{1,0:T(1,128)} %bitcast.10, s32[1,128]{1,0:T(1,128)} %bitcast.11, f32[2,128]{1,0:T(2,128)} %bitcast.8, f32[2,64]{1,0:T(2,128)} %bitcast.9, ...), custom_call_target="tpu_custom_call" | custom-call | tf_op jit(solution)/shard_map/partial_tied/pallas_call | solution.py:274
  3.2 14.8 %all_to_all.5.parts_ref = bf16[32,2,768]{2,1,0:T(2,128)(2,1)S(1)} all-to-all(bf16[32,2,768]{2,1,0:T(2,128)(2,1)S(1)} %partial_tied.1), channel_id=1, replica_groups={{29,31,28,30,25,27,24,26,21,23,20,22,17,19,16,18,13,15,12,14,9,11,8,10,..., dimensions={0} | all-to-all | bytes 196608 | tf_op jit(solution)/shard_map/all_to_all | solution.py:287
  18.0 0.8 %tied_beams.1 = bf16[2,32,48]{2,1,0:T(8,128)(2,1)} custom-call(bf16[32,2,768]{2,1,0:T(2,128)(2,1)S(1)} %all_to_all.5.parts_ref), custom_call_target="tpu_custom_call" | custom-call | tf_op jit(solution)/shard_map/tied_beams/pallas_call | solution.py:296
